TPU v7x, 256 devices: a whole 4x4x8 slice. The times are simulated.
256 devices in a mesh: tm: 8 (over y, core), sub: 32 (over x, z).
Axes of the slice: x: 4, y: 4, z: 8, core: 2. Of those that a mesh axis runs over, the one named last changes fastest.
Arguments:
- flex: bfloat16 [32, 2048, 2048], P('sub'), as said below
- mass: float32 [32, 2048], P('sub'), may hold values from 0.25 to 1
- coarse_rate: float32 [32, 2048], P('sub'), may hold values from 0.05 to 1
- face_perm: int32 [32, 1024], P('sub'), may hold values from 0 to 1023, each once within a row
- start_u: float32 [8, 32, 2048, 128], P('tm', 'sub'), may hold values from -6 to 6
- start_v: float32 [8, 32, 2048, 128], P('tm', 'sub'), may hold values from -6 to 6
- load: bfloat16 [8, 32, 2048, 128], P('tm', 'sub'), may hold values from -16 to 16
Outputs:
- end_u: float32 [8, 32, 2048, 128], P('tm', 'sub')
- end_v: float32 [8, 32, 2048, 128], P('tm', 'sub')
Inputs may be any that keep to these rules, and one draw needn't show every extreme that they name: Every row of face_perm holds each of 0 to 1023 once. flex[s] is symmetric positive definite, entries within -0.5 to 0.5.
All inputs are finite; a program needn't handle non-finite values.
Results may differ from a plain program's by a relative error of at most 0.0019.
Values sent between devices are 32-bit elements; how exact they have to be, the bound alone decides.
No kernel may reach another device: no remote copies, remote signals or barrier semaphores. Data moves between devices by JAX's collectives and lax.ppermute only.
A program may use at most 128 MiB of HBM per device.

v0:
```python
import jax
import jax.numpy as jnp
from jax import lax
from jax.sharding import PartitionSpec as P

FINE = 2
DUAL = 2


def shifted(value, axis, steps):
    count = lax.axis_size(axis)
    leading, last = (max(0, -steps), min(count, count - steps))
    return lax.ppermute(value, axis, [(source, source + steps) for source in range(leading, last)])


def on_device(flex, mass, coarse_rate, face_perm, start_u, start_v, load):
    matrix = flex[0]
    weight = 2.0 * mass[0][:, None]
    rate = coarse_rate[0][:, None]
    perm = face_perm[0]
    width = perm.shape[0]
    last_sub = lax.axis_index("sub") == lax.axis_size("sub") - 1
    first_slice = lax.axis_index("tm") == 0
    base_u = start_u[0, 0]
    base_v = start_v[0, 0]
    force = load[0, 0].astype(jnp.float32)

    def apply_flex(field):
        return jnp.dot(matrix, field.astype(jnp.bfloat16), preferred_element_type=jnp.float32)

    def gaps(field):
        scattered = jnp.zeros_like(field[:width]).at[perm].set(field[:width])
        after = shifted(scattered, "sub", -1)
        gap = field[width:] - after
        return jnp.where(last_sub, jnp.zeros_like(gap), gap)

    def local_inner(first, second):
        return jnp.sum(first * second, axis=0)

    u = base_u
    v = base_v
    for step in range(FINE):
        pred = u + v
        rhs = force + weight * pred
        y_field = apply_flex(rhs)
        res = gaps(y_field)
        accum = jnp.zeros_like(y_field)

        def reduce_one(term):
            return lax.psum(term, "sub")

        direction = res
        rr = reduce_one(local_inner(res, res))
        for k in range(DUAL):
            prior = shifted(direction, "sub", 1)
            left = -jnp.take(prior, perm, axis=0)
            q_field = apply_flex(jnp.concatenate([left, direction], axis=0))
            w_gap = gaps(q_field)
            alpha = rr / reduce_one(local_inner(direction, w_gap))
            accum = accum + alpha[None, :] * q_field
            if k + 1 < DUAL:
                res = res - alpha[None, :] * w_gap
                fresh = reduce_one(local_inner(res, res))
                direction = res + (fresh / rr)[None, :] * direction
                rr = fresh
        u_new = y_field - accum
        v = v + 2.0 * (u_new - pred)
        u = u_new
    span = float(FINE)
    denom = 1.0 + rate
    g_uu = (1.0 - rate) / denom
    g_uv = span / denom
    g_vu = -(4.0 * rate / span) / denom
    g_vv = (1.0 - rate) / denom

    def finish(carry_u, carry_v):
        du = carry_u - base_u
        dv = carry_v - base_v
        out_u = u + g_uu * du + g_uv * dv
        out_v = v + g_vu * du + g_vv * dv
        return (jnp.where(first_slice, u, out_u), jnp.where(first_slice, v, out_v))

    carry_u = jnp.zeros_like(u)
    carry_v = jnp.zeros_like(v)
    for turn in range(lax.axis_size("tm") - 1):
        out_u, out_v = finish(carry_u, carry_v)
        carry_u, carry_v = shifted((out_u, out_v), "tm", 1)
    end_u, end_v = finish(carry_u, carry_v)
    return (end_u[None, None], end_v[None, None])


def solution(mesh):
    return jax.shard_map(
        on_device,
        mesh=mesh,
        in_specs=(
            P("sub", None, None),
            P("sub", None),
            P("sub", None),
            P("sub", None),
            P("tm", "sub", None, None),
            P("tm", "sub", None, None),
            P("tm", "sub", None, None),
        ),
        out_specs=(P("tm", "sub", None, None), P("tm", "sub", None, None)),
        check_vma=False,
    )
```

profile of v0, /device:TPU:1, one launch (start us, length us, event | category | flops | bytes accessed | tf_op | source)
XLA Modules:
  0.0 896.9 jit_solution(13307581186947466509)
XLA Ops:
  2.0 2.1 copy.24
  7.2 6.5 fusion.12
  16.6 4.3 scatter_custom_fusion
  24.2 13.1 %collective-permute-done = f32[1024,128]{0,1:T(8,128)} collective-permute-done((f32[1024,128]{0,1:T(8,128)}, f32[1024,128]{0,1:T(8,128)}, u32[]{:S(2)}, u32[]{:S(2)}) %collective-permute-start) | collective-permute-done | bytes 524320 | tf_op jit(solution)/shard_map/ppermute | solution.py:13
  38.4 6.1 collective-permute-start.1
  44.6 9.0 %collective-permute-done.1 = f32[1024,128]{0,1:T(8,128)} collective-permute-done((f32[1024,128]{0,1:T(8,128)S(1)}, f32[1024,128]{0,1:T(8,128)}, u32[]{:S(2)}, u32[]{:S(2)}) %collective-permute-start.1) | collective-permute-done | bytes 524320 | tf_op jit(solution)/shard_map/ppermute | solution.py:13
  54.9 2.8 gather_fusion
  58.0 6.3 fusion.15
  67.2 4.3 scatter_custom_fusion.1
  74.8 13.1 %collective-permute-done.2 = f32[1024,128]{0,1:T(8,128)S(1)} collective-permute-done((f32[1024,128]{0,1:T(8,128)}, f32[1024,128]{0,1:T(8,128)S(1)}, u32[]{:S(2)}, u32[]{:S(2)}) %collective-permute-start.2) | collective-permute-done | bytes 524320 | tf_op jit(solution)/shard_map/ppermute | solution.py:13
  89.8 61.0 %all-reduce.1 = (f32[128]{0:T(128)S(1)}, f32[128]{0:T(128)S(1)}) all-reduce(f32[128]{0:T(128)S(1)} %get-tuple-element.10, f32[128]{0:T(128)S(1)} %get-tuple-element.9), channel_id=1, replica_groups=mesh['tm'=8,'sub'=32] {'sub'}, use_global_device_ids=true, to_apply=%region_2.3 | all-reduce | flops 256 | bytes 2048 | tf_op jit(solution)/shard_map/psum | solution.py:50
  152.2 56.0 %psum.58 = f32[128]{0:T(128)S(1)} all-reduce(f32[128]{0:T(128)S(1)} %multiply_reduce_fusion.3), channel_id=1, replica_groups=mesh['tm'=8,'sub'=32] {'sub'}, use_global_device_ids=true, to_apply=%region_7.9 | all-reduce | flops 128 | bytes 1024 | tf_op jit(solution)/shard_map/psum | solution.py:50
  209.6 4.7 collective-permute-start.3
  214.4 4.9 collective-permute-done.3
  220.5 4.0 gather_fusion.1
  224.6 2.1 copy.36
  227.8 6.3 fusion.18
  237.9 4.3 scatter_custom_fusion.2
  245.5 9.4 %collective-permute-done.4 = f32[1024,128]{0,1:T(8,128)S(1)} collective-permute-done((f32[1024,128]{0,1:T(8,128)}, f32[1024,128]{0,1:T(8,128)S(1)}, u32[]{:S(2)}, u32[]{:S(2)}) %collective-permute-start.4) | collective-permute-done | bytes 524320 | tf_op jit(solution)/shard_map/ppermute | solution.py:13
  256.3 57.4 %psum.59 = f32[128]{0:T(128)S(1)} all-reduce(f32[128]{0:T(128)S(1)} %fusion.46), channel_id=1, replica_groups=mesh['tm'=8,'sub'=32] {'sub'}, use_global_device_ids=true, to_apply=%region_10.12 | all-reduce | flops 128 | bytes 1024 | tf_op jit(solution)/shard_map/psum | solution.py:50
  316.4 6.5 fusion.21
  325.8 4.3 scatter_custom_fusion.3
  333.4 9.2 %collective-permute-done.5 = f32[1024,128]{0,1:T(8,128)S(1)} collective-permute-done((f32[1024,128]{0,1:T(8,128)}, f32[1024,128]{0,1:T(8,128)S(1)}, u32[]{:S(2)}, u32[]{:S(2)}) %collective-permute-start.5) | collective-permute-done | bytes 524320 | tf_op jit(solution)/shard_map/ppermute | solution.py:13
  342.7 2.4 collective-permute-start.6
  345.1 5.2 collective-permute-done.6
  351.5 2.8 gather_fusion.2
  354.6 6.3 fusion.24
  363.8 4.3 scatter_custom_fusion.4
  371.4 9.4 %collective-permute-done.7 = f32[1024,128]{0,1:T(8,128)S(1)} collective-permute-done((f32[1024,128]{0,1:T(8,128)}, f32[1024,128]{0,1:T(8,128)S(1)}, u32[]{:S(2)}, u32[]{:S(2)}) %collective-permute-start.7) | collective-permute-done | bytes 524320 | tf_op jit(solution)/shard_map/ppermute | solution.py:13
  382.8 57.1 %all-reduce = (f32[128]{0:T(128)S(1)}, f32[128]{0:T(128)S(1)}) all-reduce(f32[128]{0:T(128)S(1)} %get-tuple-element.8, f32[128]{0:T(128)S(1)} %get-tuple-element.7), channel_id=1, replica_groups=mesh['tm'=8,'sub'=32] {'sub'}, use_global_device_ids=true, to_apply=%region_13.15 | all-reduce | flops 256 | bytes 2048 | tf_op jit(solution)/shard_map/psum | solution.py:50
  441.3 56.3 %psum.62 = f32[128]{0:T(128)S(1)} all-reduce(f32[128]{0:T(128)S(1)} %multiply_reduce_fusion), channel_id=1, replica_groups=mesh['tm'=8,'sub'=32] {'sub'}, use_global_device_ids=true, to_apply=%region_18.20 | all-reduce | flops 128 | bytes 1024 | tf_op jit(solution)/shard_map/psum | solution.py:50
  499.0 3.6 collective-permute-start.8
  502.6 5.3 collective-permute-done.8
  509.2 2.8 gather_fusion.3
  512.3 6.3 fusion.27
  520.3 2.1 copy.53
  522.4 4.2 scatter_custom_fusion.5
  526.6 2.1 copy.54
  530.0 9.7 %collective-permute-done.9 = f32[1024,128]{0,1:T(8,128)} collective-permute-done((f32[1024,128]{0,1:T(8,128)}, f32[1024,128]{0,1:T(8,128)}, u32[]{:S(2)}, u32[]{:S(2)}) %collective-permute-start.9) | collective-permute-done | bytes 524320 | tf_op jit(solution)/shard_map/ppermute | solution.py:13
  541.3 57.2 %psum.63 = f32[128]{0:T(128)S(1)} all-reduce(f32[128]{0:T(128)S(1)} %fusion.41), channel_id=1, replica_groups=mesh['tm'=8,'sub'=32] {'sub'}, use_global_device_ids=true, to_apply=%region_21.23 | all-reduce | flops 128 | bytes 1024 | tf_op jit(solution)/shard_map/psum | solution.py:50
  598.5 2.5 add_select_fusion.13
  601.5 98.6 %collective-permute-start.11 = (f32[2048,128]{0,1:T(8,128)S(1)}, f32[2048,128]{0,1:T(8,128)S(1)}, u32[]{:S(2)}, u32[]{:S(2)}) collective-permute-start(f32[2048,128]{0,1:T(8,128)S(1)} %get-tuple-element.17), channel_id=1, source_target_pairs={{0,32},{32,64},{64,96},{96,128},{128,160},{160,192},{192,224},{1,3... | collective-permute-start | bytes 3145736 | tf_op jit(solution)/shard_map/ppermute | solution.py:13
  702.0 9.8 %collective-permute-done.11 = f32[2048,128]{0,1:T(8,128)S(1)} collective-permute-done((f32[2048,128]{0,1:T(8,128)S(1)}, f32[2048,128]{0,1:T(8,128)S(1)}, u32[]{:S(2)}, u32[]{:S(2)}) %collective-permute-start.11) | collective-permute-done | bytes 1048608 | tf_op jit(solution)/shard_map/ppermute | solution.py:13
  711.8 11.2 %collective-permute-done.10 = f32[2048,128]{0,1:T(8,128)S(1)} collective-permute-done((f32[2048,128]{0,1:T(8,128)S(1)}, f32[2048,128]{0,1:T(8,128)S(1)}, u32[]{:S(2)}, u32[]{:S(2)}) %collective-permute-start.10) | collective-permute-done | bytes 1048608 | tf_op jit(solution)/shard_map/ppermute | solution.py:13
  723.7 4.4 collective-permute-start.12
  728.1 2.1 collective-permute-start.13
  730.2 9.6 %collective-permute-done.12 = f32[2048,128]{0,1:T(8,128)S(1)} collective-permute-done((f32[2048,128]{0,1:T(8,128)S(1)}, f32[2048,128]{0,1:T(8,128)S(1)}, u32[]{:S(2)}, u32[]{:S(2)}) %collective-permute-start.12) | collective-permute-done | bytes 1048608 | tf_op jit(solution)/shard_map/ppermute | solution.py:13
  739.8 11.2 %collective-permute-done.13 = f32[2048,128]{0,1:T(8,128)S(1)} collective-permute-done((f32[2048,128]{0,1:T(8,128)S(1)}, f32[2048,128]{0,1:T(8,128)S(1)}, u32[]{:S(2)}, u32[]{:S(2)}) %collective-permute-start.13) | collective-permute-done | bytes 1048608 | tf_op jit(solution)/shard_map/ppermute | solution.py:13
  751.7 4.4 collective-permute-start.14
  758.0 9.8 %collective-permute-done.14 = f32[2048,128]{0,1:T(8,128)S(1)} collective-permute-done((f32[2048,128]{0,1:T(8,128)S(1)}, f32[2048,128]{0,1:T(8,128)S(1)}, u32[]{:S(2)}, u32[]{:S(2)}) %collective-permute-start.14) | collective-permute-done | bytes 1048608 | tf_op jit(solution)/shard_map/ppermute | solution.py:13
  767.8 11.2 %collective-permute-done.15 = f32[2048,128]{0,1:T(8,128)S(1)} collective-permute-done((f32[2048,128]{0,1:T(8,128)S(1)}, f32[2048,128]{0,1:T(8,128)S(1)}, u32[]{:S(2)}, u32[]{:S(2)}) %collective-permute-start.15) | collective-permute-done | bytes 1048608 | tf_op jit(solution)/shard_map/ppermute | solution.py:13
  779.7 4.4 collective-permute-start.16
  786.1 9.8 %collective-permute-done.16 = f32[2048,128]{0,1:T(8,128)S(1)} collective-permute-done((f32[2048,128]{0,1:T(8,128)S(1)}, f32[2048,128]{0,1:T(8,128)S(1)}, u32[]{:S(2)}, u32[]{:S(2)}) %collective-permute-start.16) | collective-permute-done | bytes 1048608 | tf_op jit(solution)/shard_map/ppermute | solution.py:13
  795.9 11.2 %collective-permute-done.17 = f32[2048,128]{0,1:T(8,128)S(1)} collective-permute-done((f32[2048,128]{0,1:T(8,128)S(1)}, f32[2048,128]{0,1:T(8,128)S(1)}, u32[]{:S(2)}, u32[]{:S(2)}) %collective-permute-start.17) | collective-permute-done | bytes 1048608 | tf_op jit(solution)/shard_map/ppermute | solution.py:13
  807.8 4.4 collective-permute-start.18
  814.1 9.8 %collective-permute-done.18 = f32[2048,128]{0,1:T(8,128)S(1)} collective-permute-done((f32[2048,128]{0,1:T(8,128)S(1)}, f32[2048,128]{0,1:T(8,128)S(1)}, u32[]{:S(2)}, u32[]{:S(2)}) %collective-permute-start.18) | collective-permute-done | bytes 1048608 | tf_op jit(solution)/shard_map/ppermute | solution.py:13
  823.9 11.2 %collective-permute-done.19 = f32[2048,128]{0,1:T(8,128)S(1)} collective-permute-done((f32[2048,128]{0,1:T(8,128)S(1)}, f32[2048,128]{0,1:T(8,128)S(1)}, u32[]{:S(2)}, u32[]{:S(2)}) %collective-permute-start.19) | collective-permute-done | bytes 1048608 | tf_op jit(solution)/shard_map/ppermute | solution.py:13
  835.8 4.4 collective-permute-start.20
  842.1 9.8 %collective-permute-done.20 = f32[2048,128]{0,1:T(8,128)S(1)} collective-permute-done((f32[2048,128]{0,1:T(8,128)S(1)}, f32[2048,128]{0,1:T(8,128)S(1)}, u32[]{:S(2)}, u32[]{:S(2)}) %collective-permute-start.20) | collective-permute-done | bytes 1048608 | tf_op jit(solution)/shard_map/ppermute | solution.py:13
  851.9 11.2 %collective-permute-done.21 = f32[2048,128]{0,1:T(8,128)S(1)} collective-permute-done((f32[2048,128]{0,1:T(8,128)S(1)}, f32[2048,128]{0,1:T(8,128)S(1)}, u32[]{:S(2)}, u32[]{:S(2)}) %collective-permute-start.21) | collective-permute-done | bytes 1048608 | tf_op jit(solution)/shard_map/ppermute | solution.py:13
  863.8 4.4 collective-permute-start.22
  870.1 9.8 %collective-permute-done.22 = f32[2048,128]{0,1:T(8,128)S(1)} collective-permute-done((f32[2048,128]{0,1:T(8,128)S(1)}, f32[2048,128]{0,1:T(8,128)S(1)}, u32[]{:S(2)}, u32[]{:S(2)}) %collective-permute-start.22) | collective-permute-done | bytes 1048608 | tf_op jit(solution)/shard_map/ppermute | solution.py:13
  879.9 11.2 %collective-permute-done.23 = f32[2048,128]{0,1:T(8,128)S(1)} collective-permute-done((f32[2048,128]{0,1:T(8,128)S(1)}, f32[2048,128]{0,1:T(8,128)S(1)}, u32[]{:S(2)}, u32[]{:S(2)}) %collective-permute-start.23) | collective-permute-done | bytes 1048608 | tf_op jit(solution)/shard_map/ppermute | solution.py:13
  892.8 2.5 copy.56
  (102 shorter events, 81.8 us)
Async XLA Ops:
  7.2 37.4 %copy-start.13 = (s32[1,1024]{1,0:T(1,128)S(1)}, s32[1,1024]{1,0:T(1,128)}, u32[]{:S(2)}) copy-start(s32[1,1024]{1,0:T(1,128)} %param.12) | copy-start | bytes 12292
  13.7 30.9 %copy-start = (f32[2048,128]{0,1:T(8,128)}, f32[2048,128]{0,1:T(8,128)S(1)}, u32[]{:S(2)}) copy-start(f32[2048,128]{0,1:T(8,128)S(1)} %fusion.12) | copy-start | bytes 3145732
  22.9 14.4 %collective-permute-start = (f32[1024,128]{0,1:T(8,128)}, f32[1024,128]{0,1:T(8,128)}, u32[]{:S(2)}, u32[]{:S(2)}) collective-permute-start(f32[1024,128]{0,1:T(8,128)} %copy.29), channel_id=1, source_target_pairs={{1,0},{2,1},{3,2},{4,3},{5,4},{6,5},{7,6},{8,7},{9,8},{10,9},{11,1... | collective-permute-start | bytes 1572872 | tf_op jit(solution)/shard_map/ppermute | solution.py:13
  38.4 6.2 copy-start.9
  38.4 15.2 %collective-permute-start.1 = (f32[1024,128]{0,1:T(8,128)S(1)}, f32[1024,128]{0,1:T(8,128)}, u32[]{:S(2)}, u32[]{:S(2)}) collective-permute-start(f32[1024,128]{0,1:T(8,128)S(1)} %get-tuple-element.28), channel_id=1, source_target_pairs={{0,1},{1,2},{2,3},{3,4},{4,5},{5,6},{6,7},{7,8},{8,9},{9,10},{10,1... | collective-permute-start | bytes 1572872 | tf_op jit(solution)/shard_map/ppermute | solution.py:13
  64.3 150.1 %copy-start.2 = (f32[2048,128]{0,1:T(8,128)}, f32[2048,128]{0,1:T(8,128)S(1)}, u32[]{:S(2)}) copy-start(f32[2048,128]{0,1:T(8,128)S(1)} %fusion.15) | copy-start | bytes 3145732
  73.5 14.4 %collective-permute-start.2 = (f32[1024,128]{0,1:T(8,128)}, f32[1024,128]{0,1:T(8,128)S(1)}, u32[]{:S(2)}, u32[]{:S(2)}) collective-permute-start(f32[1024,128]{0,1:T(8,128)} %copy.34), channel_id=1, source_target_pairs={{1,0},{2,1},{3,2},{4,3},{5,4},{6,5},{7,6},{8,7},{9,8},{10,9},{11,1... | collective-permute-start | bytes 1572872 | tf_op jit(solution)/shard_map/ppermute | solution.py:13
  209.6 4.8 copy-start.12
  209.6 9.7 %collective-permute-start.3 = (f32[1024,128]{0,1:T(8,128)S(1)}, f32[1024,128]{0,1:T(8,128)}, u32[]{:S(2)}, u32[]{:S(2)}) collective-permute-start(f32[1024,128]{0,1:T(8,128)S(1)} %get-tuple-element.25), channel_id=1, source_target_pairs={{0,1},{1,2},{2,3},{3,4},{4,5},{5,6},{6,7},{7,8},{8,9},{9,10},{10,1... | collective-permute-start | bytes 1572872 | tf_op jit(solution)/shard_map/ppermute | solution.py:13
  224.6 89.1 %copy-start.1 = (f32[2048,128]{0,1:T(8,128)S(1)}, f32[2048,128]{0,1:T(8,128)}, u32[]{:S(2)}) copy-start(f32[2048,128]{0,1:T(8,128)} %copy-done) | copy-start | bytes 3145732
  234.1 1.0 copy-start.3
  244.2 10.7 %collective-permute-start.4 = (f32[1024,128]{0,1:T(8,128)}, f32[1024,128]{0,1:T(8,128)S(1)}, u32[]{:S(2)}, u32[]{:S(2)}) collective-permute-start(f32[1024,128]{0,1:T(8,128)} %copy.39), channel_id=1, source_target_pairs={{1,0},{2,1},{3,2},{4,3},{5,4},{6,5},{7,6},{8,7},{9,8},{10,9},{11,1... | collective-permute-start | bytes 1572872 | tf_op jit(solution)/shard_map/ppermute | solution.py:13
  315.4 1.0 copy-start.4
  322.9 22.2 %copy-start.8 = (f32[2048,128]{0,1:T(8,128)}, f32[2048,128]{0,1:T(8,128)S(1)}, u32[]{:S(2)}) copy-start(f32[2048,128]{0,1:T(8,128)S(1)} %fusion.21) | copy-start | bytes 3145732
  332.1 10.5 %collective-permute-start.5 = (f32[1024,128]{0,1:T(8,128)}, f32[1024,128]{0,1:T(8,128)S(1)}, u32[]{:S(2)}, u32[]{:S(2)}) collective-permute-start(f32[1024,128]{0,1:T(8,128)} %copy.44), channel_id=1, source_target_pairs={{1,0},{2,1},{3,2},{4,3},{5,4},{6,5},{7,6},{8,7},{9,8},{10,9},{11,1... | collective-permute-start | bytes 1572872 | tf_op jit(solution)/shard_map/ppermute | solution.py:13
  342.6 2.5 copy-start.10
  342.7 7.6 collective-permute-start.6
  360.9 141.8 %copy-start.6 = (f32[2048,128]{0,1:T(8,128)}, f32[2048,128]{0,1:T(8,128)S(1)}, u32[]{:S(2)}) copy-start(f32[2048,128]{0,1:T(8,128)S(1)} %fusion.24) | copy-start | bytes 3145732
  370.1 10.7 %collective-permute-start.7 = (f32[1024,128]{0,1:T(8,128)}, f32[1024,128]{0,1:T(8,128)S(1)}, u32[]{:S(2)}, u32[]{:S(2)}) collective-permute-start(f32[1024,128]{0,1:T(8,128)} %copy.49), channel_id=1, source_target_pairs={{1,0},{2,1},{3,2},{4,3},{5,4},{6,5},{7,6},{8,7},{9,8},{10,9},{11,1... | collective-permute-start | bytes 1572872 | tf_op jit(solution)/shard_map/ppermute | solution.py:13
  499.0 3.7 copy-start.11
  499.0 8.9 collective-permute-start.8
  512.0 18.0 %copy-start.14 = (f32[1,2048]{1,0:T(1,128)S(1)}, f32[1,2048]{1,0:T(1,128)}, u32[]{:S(2)}) copy-start(f32[1,2048]{1,0:T(1,128)} %param.11) | copy-start | bytes 24580
  518.5 1.0 copy-start.7
  519.5 81.5 %copy-start.5 = (f32[2048,128]{0,1:T(8,128)S(1)}, f32[2048,128]{0,1:T(8,128)}, u32[]{:S(2)}) copy-start(f32[2048,128]{0,1:T(8,128)} %copy-done.4) | copy-start | bytes 3145732
  528.7 11.1 %collective-permute-start.9 = (f32[1024,128]{0,1:T(8,128)}, f32[1024,128]{0,1:T(8,128)}, u32[]{:S(2)}, u32[]{:S(2)}) collective-permute-start(f32[1024,128]{0,1:T(8,128)} %copy.54), channel_id=1, source_target_pairs={{1,0},{2,1},{3,2},{4,3},{5,4},{6,5},{7,6},{8,7},{9,8},{10,9},{11,1... | collective-permute-start | bytes 1572872 | tf_op jit(solution)/shard_map/ppermute | solution.py:13
  601.5 110.3 %collective-permute-start.11 = (f32[2048,128]{0,1:T(8,128)S(1)}, f32[2048,128]{0,1:T(8,128)S(1)}, u32[]{:S(2)}, u32[]{:S(2)}) collective-permute-start(f32[2048,128]{0,1:T(8,128)S(1)} %get-tuple-element.17), channel_id=1, source_target_pairs={{0,32},{32,64},{64,96},{96,128},{128,160},{160,192},{192,224},{1,3... | collective-permute-start | bytes 3145736 | tf_op jit(solution)/shard_map/ppermute | solution.py:13
  700.1 23.0 %collective-permute-start.10 = (f32[2048,128]{0,1:T(8,128)S(1)}, f32[2048,128]{0,1:T(8,128)S(1)}, u32[]{:S(2)}, u32[]{:S(2)}) collective-permute-start(f32[2048,128]{0,1:T(8,128)S(1)} %get-tuple-element.15), channel_id=1, source_target_pairs={{0,32},{32,64},{64,96},{96,128},{128,160},{160,192},{192,224},{1,3... | collective-permute-start | bytes 3145736 | tf_op jit(solution)/shard_map/ppermute | solution.py:13
  723.7 16.1 %collective-permute-start.12 = (f32[2048,128]{0,1:T(8,128)S(1)}, f32[2048,128]{0,1:T(8,128)S(1)}, u32[]{:S(2)}, u32[]{:S(2)}) collective-permute-start(f32[2048,128]{0,1:T(8,128)S(1)} %get-tuple-element.41), channel_id=1, source_target_pairs={{0,32},{32,64},{64,96},{96,128},{128,160},{160,192},{192,224},{1,3... | collective-permute-start | bytes 3145736 | tf_op jit(solution)/shard_map/ppermute | solution.py:13
  728.1 23.0 %collective-permute-start.13 = (f32[2048,128]{0,1:T(8,128)S(1)}, f32[2048,128]{0,1:T(8,128)S(1)}, u32[]{:S(2)}, u32[]{:S(2)}) collective-permute-start(f32[2048,128]{0,1:T(8,128)S(1)} %get-tuple-element.42), channel_id=1, source_target_pairs={{0,32},{32,64},{64,96},{96,128},{128,160},{160,192},{192,224},{1,3... | collective-permute-start | bytes 3145736 | tf_op jit(solution)/shard_map/ppermute | solution.py:13
  751.7 16.1 %collective-permute-start.14 = (f32[2048,128]{0,1:T(8,128)S(1)}, f32[2048,128]{0,1:T(8,128)S(1)}, u32[]{:S(2)}, u32[]{:S(2)}) collective-permute-start(f32[2048,128]{0,1:T(8,128)S(1)} %get-tuple-element.39), channel_id=1, source_target_pairs={{0,32},{32,64},{64,96},{96,128},{128,160},{160,192},{192,224},{1,3... | collective-permute-start | bytes 3145736 | tf_op jit(solution)/shard_map/ppermute | solution.py:13
  756.1 23.0 %collective-permute-start.15 = (f32[2048,128]{0,1:T(8,128)S(1)}, f32[2048,128]{0,1:T(8,128)S(1)}, u32[]{:S(2)}, u32[]{:S(2)}) collective-permute-start(f32[2048,128]{0,1:T(8,128)S(1)} %get-tuple-element.40), channel_id=1, source_target_pairs={{0,32},{32,64},{64,96},{96,128},{128,160},{160,192},{192,224},{1,3... | collective-permute-start | bytes 3145736 | tf_op jit(solution)/shard_map/ppermute | solution.py:13
  779.7 16.1 %collective-permute-start.16 = (f32[2048,128]{0,1:T(8,128)S(1)}, f32[2048,128]{0,1:T(8,128)S(1)}, u32[]{:S(2)}, u32[]{:S(2)}) collective-permute-start(f32[2048,128]{0,1:T(8,128)S(1)} %get-tuple-element.37), channel_id=1, source_target_pairs={{0,32},{32,64},{64,96},{96,128},{128,160},{160,192},{192,224},{1,3... | collective-permute-start | bytes 3145736 | tf_op jit(solution)/shard_map/ppermute | solution.py:13
  784.1 23.0 %collective-permute-start.17 = (f32[2048,128]{0,1:T(8,128)S(1)}, f32[2048,128]{0,1:T(8,128)S(1)}, u32[]{:S(2)}, u32[]{:S(2)}) collective-permute-start(f32[2048,128]{0,1:T(8,128)S(1)} %get-tuple-element.38), channel_id=1, source_target_pairs={{0,32},{32,64},{64,96},{96,128},{128,160},{160,192},{192,224},{1,3... | collective-permute-start | bytes 3145736 | tf_op jit(solution)/shard_map/ppermute | solution.py:13
  807.8 16.1 %collective-permute-start.18 = (f32[2048,128]{0,1:T(8,128)S(1)}, f32[2048,128]{0,1:T(8,128)S(1)}, u32[]{:S(2)}, u32[]{:S(2)}) collective-permute-start(f32[2048,128]{0,1:T(8,128)S(1)} %get-tuple-element.35), channel_id=1, source_target_pairs={{0,32},{32,64},{64,96},{96,128},{128,160},{160,192},{192,224},{1,3... | collective-permute-start | bytes 3145736 | tf_op jit(solution)/shard_map/ppermute | solution.py:13
  812.2 23.0 %collective-permute-start.19 = (f32[2048,128]{0,1:T(8,128)S(1)}, f32[2048,128]{0,1:T(8,128)S(1)}, u32[]{:S(2)}, u32[]{:S(2)}) collective-permute-start(f32[2048,128]{0,1:T(8,128)S(1)} %get-tuple-element.36), channel_id=1, source_target_pairs={{0,32},{32,64},{64,96},{96,128},{128,160},{160,192},{192,224},{1,3... | collective-permute-start | bytes 3145736 | tf_op jit(solution)/shard_map/ppermute | solution.py:13
  835.8 16.1 %collective-permute-start.20 = (f32[2048,128]{0,1:T(8,128)S(1)}, f32[2048,128]{0,1:T(8,128)S(1)}, u32[]{:S(2)}, u32[]{:S(2)}) collective-permute-start(f32[2048,128]{0,1:T(8,128)S(1)} %get-tuple-element.33), channel_id=1, source_target_pairs={{0,32},{32,64},{64,96},{96,128},{128,160},{160,192},{192,224},{1,3... | collective-permute-start | bytes 3145736 | tf_op jit(solution)/shard_map/ppermute | solution.py:13
  840.2 23.0 %collective-permute-start.21 = (f32[2048,128]{0,1:T(8,128)S(1)}, f32[2048,128]{0,1:T(8,128)S(1)}, u32[]{:S(2)}, u32[]{:S(2)}) collective-permute-start(f32[2048,128]{0,1:T(8,128)S(1)} %get-tuple-element.34), channel_id=1, source_target_pairs={{0,32},{32,64},{64,96},{96,128},{128,160},{160,192},{192,224},{1,3... | collective-permute-start | bytes 3145736 | tf_op jit(solution)/shard_map/ppermute | solution.py:13
  863.8 16.1 %collective-permute-start.22 = (f32[2048,128]{0,1:T(8,128)S(1)}, f32[2048,128]{0,1:T(8,128)S(1)}, u32[]{:S(2)}, u32[]{:S(2)}) collective-permute-start(f32[2048,128]{0,1:T(8,128)S(1)} %get-tuple-element.31), channel_id=1, source_target_pairs={{0,32},{32,64},{64,96},{96,128},{128,160},{160,192},{192,224},{1,3... | collective-permute-start | bytes 3145736 | tf_op jit(solution)/shard_map/ppermute | solution.py:13
  868.2 23.0 %collective-permute-start.23 = (f32[2048,128]{0,1:T(8,128)S(1)}, f32[2048,128]{0,1:T(8,128)S(1)}, u32[]{:S(2)}, u32[]{:S(2)}) collective-permute-start(f32[2048,128]{0,1:T(8,128)S(1)} %get-tuple-element.32), channel_id=1, source_target_pairs={{0,32},{32,64},{64,96},{96,128},{128,160},{160,192},{192,224},{1,3... | collective-permute-start | bytes 3145736 | tf_op jit(solution)/shard_map/ppermute | solution.py:13
where the time goes:
time: 906 us; the launch traced here: 897 us
  blocking collectives  345 us (38%)
  waiting for transfers between devices  235 us (26%)
  starting transfers between devices  163 us (18%)
  local copies, waits for them, and re-layouts  87.3 us (10%)
  matrix products  38 us (4%)
  other arithmetic  26.6 us (3%)
    psum x6, blocking collectives, reduce_one(): return lax.psum(term, 'sub')  345 us
    ppermute x24, waiting for transfers between devices, shifted(): lax.ppermute(value, axis, [(source, source + steps) for source in range(l...  235 us
    ppermute x24, starting transfers between devices, shifted(): lax.ppermute(value, axis, [(source, source + steps) for source in range(l...  163 us
    dot_general x6, matrix products, apply_flex(): jnp.dot(matrix, field.astype(jnp.bfloat16), preferred_element_type=jnp.fl...  38 us
    scatter x12, local copies, waits for them, and re-layouts, gaps(): scattered = jnp.zeros_like(field[:width]).at[perm].set(field[:width])  37.8 us
  transfers between devices with their start and end apart: 24, of which 24 were waited for; matrix products, arithmetic and copies ran while one was open for 0% of the time, Pallas kernels for 0%

commit v1 on v0

v1 whole, which is shorter than its diff:
```python
import functools

import jax
import jax.numpy as jnp
from jax import lax
from jax.experimental import pallas as pl
from jax.experimental.pallas import tpu as pltpu
from jax.sharding import PartitionSpec as P

F32 = jnp.float32
BF16 = jnp.bfloat16
VMEM = pl.BlockSpec(memory_space=pltpu.VMEM)


def call(kernel, name, outs, args, flops=0):
    moved = sum(a.size * a.dtype.itemsize for a in args)
    return pl.pallas_call(
        kernel,
        name=name,
        out_shape=[jax.ShapeDtypeStruct(shape, dtype) for shape, dtype in outs],
        in_specs=[VMEM] * len(args),
        out_specs=[VMEM] * len(outs),
        compiler_params=pltpu.CompilerParams(vmem_limit_bytes=44 * 2**20),
        cost_estimate=pl.CostEstimate(flops=flops, bytes_accessed=moved, transcendentals=0),
    )(*args)


def pair(value):
    high = value.astype(BF16)
    return high, (value - high.astype(F32)).astype(BF16)


def triple(value):
    high = value.astype(BF16)
    rest = value - high.astype(F32)
    middle = rest.astype(BF16)
    low = (rest - middle.astype(F32)).astype(BF16)
    return jnp.concatenate([high, middle, low], axis=1)


def fold(wide):
    return wide[:, :128] + wide[:, 128:256] + wide[:, 256:]


def to_multipliers(onehot, face):
    return fold(jnp.dot(onehot, triple(face), preferred_element_type=F32))


def to_left(onehot, block):
    return fold(lax.dot_general(onehot, triple(block), (((0,), (0,)), ((), ())), preferred_element_type=F32))


def column(row):
    width = row.shape[1]
    return jnp.concatenate([jnp.transpose(jnp.broadcast_to(row[:, k : k + 128], (128, 128))) for k in range(0, width, 128)], axis=0)


def split_faces(field, left_ref, right_ref):
    half = left_ref.shape[0]
    left_ref[...] = field[:half]
    right_ref[...] = field[half:]


def start_kernel(a, u, v, load, mass, perm, y_l, y_r, y_m, onehot):
    width = perm.shape[1]
    onehot[...] = (lax.broadcasted_iota(jnp.int32, (width, width), 0) == perm[...]).astype(F32).astype(BF16)
    rhs = load[...].astype(F32) + 2.0 * column(mass[...]) * (u[...] + v[...])
    y = jnp.dot(a[...], rhs.astype(BF16), preferred_element_type=F32)
    split_faces(y, y_l, y_r)
    y_m[...] = to_multipliers(onehot[...], y_l[...])


def jump(onehot, f_l, f_r, from_left, from_right):
    sub = lax.axis_index("sub")
    left = jnp.where(sub == 0, 0.0, f_l[...] - to_left(onehot[...], from_left[...]))
    right = jnp.where(sub == lax.axis_size("sub") - 1, 0.0, f_r[...] - from_right[...])
    return left, right


def apply_wide(a, left, right):
    high_l, low_l = pair(left)
    high_r, low_r = pair(right)
    z = jnp.concatenate([jnp.concatenate([high_l, low_l], axis=1), jnp.concatenate([high_r, low_r], axis=1)], axis=0)
    return jnp.dot(a[...], z, preferred_element_type=F32)


def add_up(value):
    return jnp.sum(value, axis=0, keepdims=True)


def first_kernel(a, onehot, y_l, y_r, from_left, from_right, q_l, q_r, q_m, t_l, t_r, sums):
    half = y_l.shape[0]
    left, right = jump(onehot, y_l, y_r, from_left, from_right)
    wide = apply_wide(a, left, right)
    q = wide[:, :128]
    split_faces(q, q_l, q_r)
    q_m[...] = to_multipliers(onehot[...], q_l[...])
    split_faces(q + wide[:, 128:], t_l, t_r)
    rr = add_up(right * right)
    pw = add_up(left * q[:half]) + add_up(right * q[half:])
    sums[...] = jnp.concatenate([rr, pw, jnp.zeros((6, 128), F32)], axis=0)


def second_kernel(a, onehot, q_l, q_r, from_left, from_right, sums, s_l, s_r, spread):
    half = q_l.shape[0]
    left, right = jump(onehot, q_l, q_r, from_left, from_right)
    wide = apply_wide(a, left, right)
    s = wide[:, :128] + wide[:, 128:]
    split_faces(s, s_l, s_r)
    ww = add_up(right * right)
    wfw = add_up(left * s[:half]) + add_up(right * s[half:])
    own = jnp.concatenate([sums[:2], ww, wfw, jnp.zeros((4, 128), F32)], axis=0)
    spread[...] = jnp.broadcast_to(own[None], spread.shape)


def corrected(gathered, y_l, y_r, q_l, q_r, t_l, t_r, s_l, s_r):
    total = jnp.sum(gathered[...], axis=0)
    rr, pw, ww, wfw = total[0:1], total[1:2], total[2:3], total[3:4]
    alpha = rr / pw
    ratio = ww / pw
    later = (alpha * alpha * ww - rr) / (alpha * alpha * (wfw - ww * ratio))
    gain = alpha * later

    def face(y, q, t, s):
        return y[...] - alpha * q[...] - gain * (ratio * t[...] - s[...])

    return jnp.concatenate([face(y_l, q_l, t_l, s_l), face(y_r, q_r, t_r, s_r)], axis=0)


def next_kernel(a, onehot, gathered, y_l, y_r, q_l, q_r, t_l, t_r, s_l, s_r, u, v, load, mass, z_l, z_r, z_m, held):
    u_new = corrected(gathered, y_l, y_r, q_l, q_r, t_l, t_r, s_l, s_r)
    v_new = v[...] + 2.0 * (u_new - (u[...] + v[...]))
    pred = u_new + v_new
    rhs = load[...].astype(F32) + 2.0 * column(mass[...]) * pred
    y = jnp.dot(a[...], rhs.astype(BF16), preferred_element_type=F32)
    split_faces(y, z_l, z_r)
    z_m[...] = to_multipliers(onehot[...], z_l[...])
    held[...] = v_new - 2.0 * pred


def coarse(rate):
    scale = 1.0 / (1.0 + rate)
    return (1.0 - rate) * scale, 2.0 * scale, -2.0 * rate * scale


def finish_kernel(gathered, y_l, y_r, q_l, q_r, t_l, t_r, s_l, s_r, u, v, held, rate, out):
    u_new = corrected(gathered, y_l, y_r, q_l, q_r, t_l, t_r, s_l, s_r)
    v_new = held[...] + 2.0 * u_new
    same, up, down = coarse(column(rate[...]))
    keep = lax.axis_index("tm") == 0
    own_u = u_new - jnp.where(keep, 0.0, same * u[...] + up * v[...])
    own_v = v_new - jnp.where(keep, 0.0, down * u[...] + same * v[...])
    parts, rows = out.shape[0], out.shape[1] // 2
    for k in range(parts):
        out[k, :rows] = own_u[k * rows : (k + 1) * rows]
        out[k, rows:] = own_v[k * rows : (k + 1) * rows]


def scan_kernel(parts, rate, out):
    count, rows = parts.shape[0], parts.shape[1] // 2
    same, up, down = coarse(column(rate[...]))
    end_u, end_v = parts[0, :rows], parts[0, rows:]
    out[0, :rows], out[0, rows:] = end_u, end_v
    for k in range(1, count):
        end_u, end_v = (
            parts[k, :rows] + (same * end_u + up * end_v),
            parts[k, rows:] + (down * end_u + same * end_v),
        )
        out[k, :rows], out[k, rows:] = end_u, end_v


def on_device(flex, mass, coarse_rate, face_perm, start_u, start_v, load):
    a = flex[0]
    size, cases = start_u.shape[2:]
    half = size // 2
    subs, slices = lax.axis_size("sub"), lax.axis_size("tm")
    u, v, force = start_u[0, 0], start_v[0, 0], load[0, 0]
    right = [(s, s + 1) for s in range(subs - 1)]
    left = [(s + 1, s) for s in range(subs - 1)]
    face = ((half, cases), F32)
    small = ((8, cases), F32)
    whole = ((size, cases), F32)
    once = 2 * size * size * cases

    def swap(face_r, face_m):
        return lax.ppermute(face_r, "sub", right), lax.ppermute(face_m, "sub", left)

    y_l, y_r, y_m, onehot = call(
        start_kernel, "start", [face, face, face, ((half, half), BF16)], (a, u, v, force, mass, face_perm), once
    )
    held = None
    for step in range(2):
        from_left, from_right = swap(y_r, y_m)
        q_l, q_r, q_m, t_l, t_r, sums = call(
            first_kernel, "first", [face] * 5 + [small], (a, onehot, y_l, y_r, from_left, from_right), 2 * once
        )
        from_left, from_right = swap(q_r, q_m)
        s_l, s_r, spread = call(
            second_kernel,
            "second",
            [face] * 2 + [((subs, 8, cases), F32)],
            (a, onehot, q_l, q_r, from_left, from_right, sums),
            2 * once,
        )
        gathered = lax.all_to_all(spread, "sub", 0, 0)
        fields = (gathered, y_l, y_r, q_l, q_r, t_l, t_r, s_l, s_r)
        if step == 0:
            y_l, y_r, y_m, held = call(
                next_kernel, "next", [face] * 3 + [whole], (a, onehot) + fields + (u, v, force, mass), once
            )
    rows = size // slices
    mine = lax.dynamic_slice(coarse_rate, (0, lax.axis_index("tm") * rows), (1, rows))
    (parts,) = call(
        finish_kernel, "finish", [((slices, 2 * rows, cases), F32)], fields + (u, v, held, coarse_rate), size * cases * 20
    )
    parts = lax.all_to_all(parts, "tm", 0, 0)
    (ends,) = call(scan_kernel, "scan", [(parts.shape, F32)], (parts, mine), size * cases * 10)
    ends = lax.all_to_all(ends, "tm", 0, 0)
    end_u = ends[:, :rows].reshape(1, 1, size, cases)
    end_v = ends[:, rows:].reshape(1, 1, size, cases)
    return end_u, end_v


def solution(mesh):
    return jax.shard_map(
        on_device,
        mesh=mesh,
        in_specs=(
            P("sub", None, None),
            P("sub", None),
            P("sub", None),
            P("sub", None),
            P("tm", "sub", None, None),
            P("tm", "sub", None, None),
            P("tm", "sub", None, None),
        ),
        out_specs=(P("tm", "sub", None, None), P("tm", "sub", None, None)),
        check_vma=False,
    )
```

time: 906 us -> 231 us (0.25)
  blocking collectives: 345 us -> 65.5 us
  waiting for transfers between devices: 235 us -> 71.8 us
  starting transfers between devices: 163 us -> 30.8 us
  local copies, waits for them, and re-layouts: 87.3 us -> 7.69 us
  Pallas kernels: 0 us -> 53.5 us
  matrix products: 38 us -> 0 us
  other arithmetic: 26.6 us -> 0 us
    psum x6 -> x0, blocking collectives: 345 us -> none  [reduce_one(): return lax.psum(term, 'sub')]
    ppermute x24 -> x8, waiting for transfers between devices: 235 us -> 45.5 us  [the longest x4 27.9 us: swap(): lax.ppermute(face_r, 'sub', right)]
    ppermute x24 -> x8, starting transfers between devices: 163 us -> 18.7 us  [the longest x4 13.2 us: swap(): lax.ppermute(face_r, 'sub', right)]
    all_to_all x0 -> x3, blocking collectives: none -> 65.5 us  [the longest x2 35.7 us: on_device(): gathered = lax.all_to_all(spread, 'sub', 0, 0)]
    pallas_call x0 -> x8, Pallas kernels: none -> 53.5 us  [call(): pl.pallas_call(kernel, name=name, out_shape=[jax.ShapeDtypeStruct(shape,...]
    dot_general x6 -> x0, matrix products: 38 us -> none  [apply_flex(): jnp.dot(matrix, field.astype(jnp.bfloat16), preferred_element_type=jnp.fl...]
    scatter x12 -> x0, local copies, waits for them, and re-layouts: 37.8 us -> none  [gaps(): scattered = jnp.zeros_like(field[:width]).at[perm].set(field[:width])]
    all_to_all x0 -> x1, waiting for transfers between devices: none -> 26.3 us  [on_device(): parts = lax.all_to_all(parts, 'tm', 0, 0)]
  transfers between devices with their start and end apart: 24 -> 9, of which waited for: 24 -> 9; matrix products, arithmetic and copies ran while one was open for 0% -> 0% of each run, Pallas kernels for 0% -> 0%
where the time goes in v1:
time: 231 us; the launch traced here: 230 us
  waiting for transfers between devices  71.8 us (31%)
  blocking collectives  65.5 us (28%)
  Pallas kernels  53.5 us (23%)
  starting transfers between devices  30.8 us (13%)
  local copies, waits for them, and re-layouts  7.69 us (3%)
    pallas_call x8, Pallas kernels, call(): pl.pallas_call(kernel, name=name, out_shape=[jax.ShapeDtypeStruct(shape,...  53.5 us
    all_to_all x2, blocking collectives, on_device(): gathered = lax.all_to_all(spread, 'sub', 0, 0)  35.7 us
    all_to_all x1, blocking collectives, on_device(): ends = lax.all_to_all(ends, 'tm', 0, 0)  29.8 us
    ppermute x4, waiting for transfers between devices, swap(): lax.ppermute(face_r, 'sub', right)  27.9 us
    all_to_all x1, waiting for transfers between devices, on_device(): parts = lax.all_to_all(parts, 'tm', 0, 0)  26.3 us
    ppermute x4, waiting for transfers between devices, swap(): lax.ppermute(face_m, 'sub', left)  17.6 us
    ppermute x4, starting transfers between devices, swap(): lax.ppermute(face_r, 'sub', right)  13.2 us
    all_to_all x1, starting transfers between devices, on_device(): parts = lax.all_to_all(parts, 'tm', 0, 0)  12 us
  transfers between devices with their start and end apart: 9, of which 9 were waited for; matrix products, arithmetic and copies ran while one was open for 0% of the time, Pallas kernels for 0%

profile of v1, /device:TPU:1, one launch (start us, length us, event | category | flops | bytes accessed | tf_op | source)
XLA Modules:
  0.0 230.1 jit_solution(6154067798866996834)
XLA Ops:
  0.6 0.0 copy-start.2
  0.6 1.2 copy-done.2
  1.9 0.0 copy-start.4
  1.9 1.2 copy-done.4
  3.1 0.0 copy-start.6
  3.1 1.0 copy-done.6
  4.1 0.0 copy-start.8
  4.1 0.7 copy-done.8
  4.8 0.0 copy-start.11
  4.8 0.7 copy-done.11
  5.5 8.8 %start.1 = (f32[1024,128]{1,0:T(8,128)S(1)}, f32[1024,128]{1,0:T(8,128)S(1)}, f32[1024,128]{1,0:T(8,128)S(1)}, bf16[1024,1024]{1,0:T(8,128)(2,1)S(1)}) custom-call(bf16[2048,2048]{1,0:T(8,128)(2,1)} %bitcast.14, f32[2048,128]{1,0:T(8,128)S(1)} %bitcast.6, f32[2048,128]{1,0:T(8,128)S(1)} %bitcast.9, bf16[2048,128]{1,0:T(8,128)(2,1)S(1)} %bitcast.12, ...), custom_call_target="tpu_custom_call" | custom-call | flops 1073741824 | bytes 11022336 | tf_op jit(solution)/shard_map/start/pallas_call | solution.py:17
  14.3 0.0 copy-start
  14.3 4.4 %collective-permute-start = (f32[1024,128]{1,0:T(8,128)S(1)}, f32[1024,128]{1,0:T(8,128)S(1)}, u32[]{:S(2)}, u32[]{:S(2)}) collective-permute-start(f32[1024,128]{1,0:T(8,128)S(1)} %get-tuple-element.30.y_r), channel_id=1, source_target_pairs={{0,1},{1,2},{2,3},{3,4},{4,5},{5,6},{6,7},{7,8},{8,9},{9,10},{10,1... | collective-permute-start | bytes 1572872 | tf_op jit(solution)/shard_map/ppermute | solution.py:186
  18.7 1.3 collective-permute-start.1
  20.0 9.2 %collective-permute-done.from_left = f32[1024,128]{1,0:T(8,128)S(1)} collective-permute-done((f32[1024,128]{1,0:T(8,128)S(1)}, f32[1024,128]{1,0:T(8,128)S(1)}, u32[]{:S(2)}, u32[]{:S(2)}) %collective-permute-start) | collective-permute-done | bytes 524320 | tf_op jit(solution)/shard_map/ppermute | solution.py:186
  29.3 4.2 %collective-permute-done.1.from_right = f32[1024,128]{1,0:T(8,128)S(1)} collective-permute-done((f32[1024,128]{1,0:T(8,128)S(1)}, f32[1024,128]{1,0:T(8,128)S(1)}, u32[]{:S(2)}, u32[]{:S(2)}) %collective-permute-start.1) | collective-permute-done | bytes 524320 | tf_op jit(solution)/shard_map/ppermute | solution.py:186
  33.4 9.9 %first.2 = (f32[1024,128]{1,0:T(8,128)S(1)}, f32[1024,128]{1,0:T(8,128)S(1)}, f32[1024,128]{1,0:T(8,128)S(1)}, f32[1024,128]{1,0:T(8,128)S(1)}, f32[1024,128]{1,0:T(8,128)S(1)}, /*index=5*/f32[8,128]{1,0:T(8,128)S(1)}) custom-call(bf16[2048,2048]{1,0:T(8,128)(2,1)} %bitcast.15, bf16[1024,1024]{1,0:T(8,128)(2,1)S(1)} %get-tuple-element.28.onehot, ...), custom_call_target="tpu_custom_call" | custom-call | flops 2147483648 | bytes 12582912 | tf_op jit(solution)/shard_map/first/pallas_call | solution.py:17
  43.3 3.6 %collective-permute-start.2 = (f32[1024,128]{1,0:T(8,128)S(1)}, f32[1024,128]{1,0:T(8,128)S(1)}, u32[]{:S(2)}, u32[]{:S(2)}) collective-permute-start(f32[1024,128]{1,0:T(8,128)S(1)} %get-tuple-element.33.q_r), channel_id=1, source_target_pairs={{0,1},{1,2},{2,3},{3,4},{4,5},{5,6},{6,7},{7,8},{8,9},{9,10},{10,1... | collective-permute-start | bytes 1572872 | tf_op jit(solution)/shard_map/ppermute | solution.py:186
  46.9 1.5 collective-permute-start.3
  48.4 8.0 %collective-permute-done.2.from_left = f32[1024,128]{1,0:T(8,128)S(1)} collective-permute-done((f32[1024,128]{1,0:T(8,128)S(1)}, f32[1024,128]{1,0:T(8,128)S(1)}, u32[]{:S(2)}, u32[]{:S(2)}) %collective-permute-start.2) | collective-permute-done | bytes 524320 | tf_op jit(solution)/shard_map/ppermute | solution.py:186
  56.4 5.7 %collective-permute-done.3.from_right = f32[1024,128]{1,0:T(8,128)S(1)} collective-permute-done((f32[1024,128]{1,0:T(8,128)S(1)}, f32[1024,128]{1,0:T(8,128)S(1)}, u32[]{:S(2)}, u32[]{:S(2)}) %collective-permute-start.3) | collective-permute-done | bytes 524320 | tf_op jit(solution)/shard_map/ppermute | solution.py:186
  62.2 0.0 copy-done
  62.2 0.0 copy-start.3
  62.2 0.0 copy-start.7
  62.2 0.0 copy-start.9
  62.2 7.0 %second.2 = (f32[1024,128]{1,0:T(8,128)S(1)}, f32[1024,128]{1,0:T(8,128)S(1)}, f32[32,8,128]{2,1,0:T(8,128)S(1)}) custom-call(bf16[2048,2048]{1,0:T(8,128)(2,1)} %bitcast.16, bf16[1024,1024]{1,0:T(8,128)(2,1)S(1)} %get-tuple-element.28.onehot, f32[1024,128]{1,0:T(8,128)S(1)} %get-tuple-element.32.q_l, f32[1024,128]{1,0:T(8,128)S(1)} %get-tuple-element.33.q_r, ...), custom_call_target="tpu_custom_call" | custom-call | flops 2147483648 | bytes 12587008 | tf_op jit(solution)/shard_map/second/pallas_call | solution.py:17
  69.2 18.0 %all_to_all.20.gathered = f32[32,8,128]{2,1,0:T(8,128)S(1)} all-to-all(f32[32,8,128]{2,1,0:T(8,128)S(1)} %get-tuple-element.36), channel_id=1, replica_groups=mesh['tm'=8,'sub'=32] {'sub'}, dimensions={0} | all-to-all | bytes 262144 | tf_op jit(solution)/shard_map/all_to_all | solution.py:205
  87.3 0.0 copy-done.3
  87.3 0.0 copy-done.7
  87.3 0.0 copy-done.9
  87.3 0.0 copy-start.1
  87.3 9.7 %next.1 = (f32[1024,128]{1,0:T(8,128)S(1)}, f32[1024,128]{1,0:T(8,128)S(1)}, f32[1024,128]{1,0:T(8,128)S(1)}, f32[2048,128]{1,0:T(8,128)S(1)}) custom-call(bf16[2048,2048]{1,0:T(8,128)(2,1)} %bitcast.17, bf16[1024,1024]{1,0:T(8,128)(2,1)} %copy-done, f32[32,8,128]{2,1,0:T(8,128)S(1)} %all_to_all.20.gathered, f32[1024,128]{1,0:T(8,128)S(1)} %get-tuple-element.29.y_l, ...), custom_call_target="tpu_custom_call" | custom-call | flops 1073741824 | bytes 17440768 | tf_op jit(solution)/shard_map/next/pallas_call | solution.py:17
  97.0 2.9 %collective-permute-start.4 = (f32[1024,128]{1,0:T(8,128)S(1)}, f32[1024,128]{1,0:T(8,128)S(1)}, u32[]{:S(2)}, u32[]{:S(2)}) collective-permute-start(f32[1024,128]{1,0:T(8,128)S(1)} %get-tuple-element.42.y_r), channel_id=1, source_target_pairs={{0,1},{1,2},{2,3},{3,4},{4,5},{5,6},{6,7},{7,8},{8,9},{9,10},{10,1... | collective-permute-start | bytes 1572872 | tf_op jit(solution)/shard_map/ppermute | solution.py:186
  100.0 1.5 collective-permute-start.5
  101.5 5.8 %collective-permute-done.4.from_left = f32[1024,128]{1,0:T(8,128)S(1)} collective-permute-done((f32[1024,128]{1,0:T(8,128)S(1)}, f32[1024,128]{1,0:T(8,128)S(1)}, u32[]{:S(2)}, u32[]{:S(2)}) %collective-permute-start.4) | collective-permute-done | bytes 524320 | tf_op jit(solution)/shard_map/ppermute | solution.py:186
  107.3 3.9 %collective-permute-done.5.from_right = f32[1024,128]{1,0:T(8,128)S(1)} collective-permute-done((f32[1024,128]{1,0:T(8,128)S(1)}, f32[1024,128]{1,0:T(8,128)S(1)}, u32[]{:S(2)}, u32[]{:S(2)}) %collective-permute-start.5) | collective-permute-done | bytes 524320 | tf_op jit(solution)/shard_map/ppermute | solution.py:186
  111.2 0.0 copy-done.1
  111.2 9.9 %first.3 = (f32[1024,128]{1,0:T(8,128)S(1)}, f32[1024,128]{1,0:T(8,128)S(1)}, f32[1024,128]{1,0:T(8,128)S(1)}, f32[1024,128]{1,0:T(8,128)S(1)}, f32[1024,128]{1,0:T(8,128)S(1)}, /*index=5*/f32[8,128]{1,0:T(8,128)S(1)}) custom-call(bf16[2048,2048]{1,0:T(8,128)(2,1)} %bitcast.18, bf16[1024,1024]{1,0:T(8,128)(2,1)S(1)} %copy-done.1, ...), custom_call_target="tpu_custom_call" | custom-call | flops 2147483648 | bytes 12582912 | tf_op jit(solution)/shard_map/first/pallas_call | solution.py:17
  121.1 2.3 collective-permute-start.6
  123.3 1.3 collective-permute-start.7
  124.6 4.8 %collective-permute-done.6.from_left = f32[1024,128]{1,0:T(8,128)S(1)} collective-permute-done((f32[1024,128]{1,0:T(8,128)S(1)}, f32[1024,128]{1,0:T(8,128)S(1)}, u32[]{:S(2)}, u32[]{:S(2)}) %collective-permute-start.6) | collective-permute-done | bytes 524320 | tf_op jit(solution)/shard_map/ppermute | solution.py:186
  129.4 3.8 %collective-permute-done.7.from_right = f32[1024,128]{1,0:T(8,128)S(1)} collective-permute-done((f32[1024,128]{1,0:T(8,128)S(1)}, f32[1024,128]{1,0:T(8,128)S(1)}, u32[]{:S(2)}, u32[]{:S(2)}) %collective-permute-start.7) | collective-permute-done | bytes 524320 | tf_op jit(solution)/shard_map/ppermute | solution.py:186
  133.3 0.0 copy-start.10
  133.3 6.9 %second.3 = (f32[1024,128]{1,0:T(8,128)S(1)}, f32[1024,128]{1,0:T(8,128)S(1)}, f32[32,8,128]{2,1,0:T(8,128)S(1)}) custom-call(bf16[2048,2048]{1,0:T(8,128)(2,1)} %bitcast.19, bf16[1024,1024]{1,0:T(8,128)(2,1)S(1)} %copy-done.1, f32[1024,128]{1,0:T(8,128)S(1)} %get-tuple-element.44.q_l, f32[1024,128]{1,0:T(8,128)S(1)} %get-tuple-element.45.q_r, ...), custom_call_target="tpu_custom_call" | custom-call | flops 2147483648 | bytes 12587008 | tf_op jit(solution)/shard_map/second/pallas_call | solution.py:17
  140.2 17.7 %all_to_all.21.gathered = f32[32,8,128]{2,1,0:T(8,128)S(1)} all-to-all(f32[32,8,128]{2,1,0:T(8,128)S(1)} %get-tuple-element.48), channel_id=1, replica_groups=mesh['tm'=8,'sub'=32] {'sub'}, dimensions={0} | all-to-all | bytes 262144 | tf_op jit(solution)/shard_map/all_to_all | solution.py:205
  157.9 0.0 copy-done.10
  157.9 0.9 finish.1
  158.8 0.0 copy-start.5
  158.8 1.3 copy-done.5
  160.1 12.0 %all-to-all-start.2 = ((f32[8,512,128]{2,1,0:T(8,128)}), f32[8,512,128]{2,1,0:T(8,128)S(1)}, u32[]{:S(2)}, u32[]{:S(2)}) async-start(f32[8,512,128]{2,1,0:T(8,128)} %copy-done.5), calls=%async_computation.2 | async-start | bytes 4194304 | tf_op jit(solution)/shard_map/all_to_all | solution.py:216
  172.1 26.3 %all-to-all-done.2.parts = f32[8,512,128]{2,1,0:T(8,128)S(1)} async-done(((f32[8,512,128]{2,1,0:T(8,128)}), f32[8,512,128]{2,1,0:T(8,128)S(1)}, u32[]{:S(2)}, u32[]{:S(2)}) %all-to-all-start.2) | async-done | bytes 2097184 | tf_op jit(solution)/shard_map/all_to_all | solution.py:216
  198.5 0.4 scan.1
  198.8 29.8 %all_to_all.22 = f32[8,512,128]{2,1,0:T(8,128)S(1)} all-to-all(f32[8,512,128]{2,1,0:T(8,128)S(1)} %scan.1), channel_id=1, replica_groups=mesh['tm'=8,'sub'=32] {'tm'}, dimensions={0} | all-to-all | bytes 4194304 | tf_op jit(solution)/shard_map/all_to_all | solution.py:218
  228.6 1.5 fusion
  (1 shorter events, 0.0 us)
Async XLA Ops:
  0.6 1.2 copy-start.2
  1.9 1.2 copy-start.4
  3.1 1.0 copy-start.6
  4.1 0.7 copy-start.8
  4.8 0.7 copy-start.11
  14.3 47.9 %copy-start = (bf16[1024,1024]{1,0:T(8,128)(2,1)}, bf16[1024,1024]{1,0:T(8,128)(2,1)S(1)}, u32[]{:S(2)}) copy-start(bf16[1024,1024]{1,0:T(8,128)(2,1)S(1)} %get-tuple-element.28.onehot) | copy-start | bytes 6291460
  14.3 15.0 %collective-permute-start = (f32[1024,128]{1,0:T(8,128)S(1)}, f32[1024,128]{1,0:T(8,128)S(1)}, u32[]{:S(2)}, u32[]{:S(2)}) collective-permute-start(f32[1024,128]{1,0:T(8,128)S(1)} %get-tuple-element.30.y_r), channel_id=1, source_target_pairs={{0,1},{1,2},{2,3},{3,4},{4,5},{5,6},{6,7},{7,8},{8,9},{9,10},{10,1... | collective-permute-start | bytes 1572872 | tf_op jit(solution)/shard_map/ppermute | solution.py:186
  18.7 14.7 %collective-permute-start.1 = (f32[1024,128]{1,0:T(8,128)S(1)}, f32[1024,128]{1,0:T(8,128)S(1)}, u32[]{:S(2)}, u32[]{:S(2)}) collective-permute-start(f32[1024,128]{1,0:T(8,128)S(1)} %get-tuple-element.31), channel_id=1, source_target_pairs={{1,0},{2,1},{3,2},{4,3},{5,4},{6,5},{7,6},{8,7},{9,8},{10,9},{11,1... | collective-permute-start | bytes 1572872 | tf_op jit(solution)/shard_map/ppermute | solution.py:186
  43.3 13.1 %collective-permute-start.2 = (f32[1024,128]{1,0:T(8,128)S(1)}, f32[1024,128]{1,0:T(8,128)S(1)}, u32[]{:S(2)}, u32[]{:S(2)}) collective-permute-start(f32[1024,128]{1,0:T(8,128)S(1)} %get-tuple-element.33.q_r), channel_id=1, source_target_pairs={{0,1},{1,2},{2,3},{3,4},{4,5},{5,6},{6,7},{7,8},{8,9},{9,10},{10,1... | collective-permute-start | bytes 1572872 | tf_op jit(solution)/shard_map/ppermute | solution.py:186
  46.9 15.2 %collective-permute-start.3 = (f32[1024,128]{1,0:T(8,128)S(1)}, f32[1024,128]{1,0:T(8,128)S(1)}, u32[]{:S(2)}, u32[]{:S(2)}) collective-permute-start(f32[1024,128]{1,0:T(8,128)S(1)} %get-tuple-element.34), channel_id=1, source_target_pairs={{1,0},{2,1},{3,2},{4,3},{5,4},{6,5},{7,6},{8,7},{9,8},{10,9},{11,1... | collective-permute-start | bytes 1572872 | tf_op jit(solution)/shard_map/ppermute | solution.py:186
  62.2 25.1 %copy-start.3 = (f32[1,1,2048,128]{3,2,1,0:T(8,128)S(1)}, f32[1,1,2048,128]{3,2,1,0:T(8,128)}, u32[]{:S(2)}) copy-start(f32[1,1,2048,128]{3,2,1,0:T(8,128)} %param.11) | copy-start | bytes 3145732
  62.2 25.1 %copy-start.7 = (bf16[1,1,2048,128]{3,2,1,0:T(8,128)(2,1)S(1)}, bf16[1,1,2048,128]{3,2,1,0:T(8,128)(2,1)}, u32[]{:S(2)}) copy-start(bf16[1,1,2048,128]{3,2,1,0:T(8,128)(2,1)} %param.13) | copy-start | bytes 1572868
  62.2 25.1 %copy-start.9 = (f32[1,2048]{1,0:T(1,128)S(1)}, f32[1,2048]{1,0:T(1,128)}, u32[]{:S(2)}) copy-start(f32[1,2048]{1,0:T(1,128)} %mass.3) | copy-start | bytes 24580
  87.3 23.9 %copy-start.1 = (bf16[1024,1024]{1,0:T(8,128)(2,1)S(1)}, bf16[1024,1024]{1,0:T(8,128)(2,1)}, u32[]{:S(2)}) copy-start(bf16[1024,1024]{1,0:T(8,128)(2,1)} %copy-done) | copy-start | bytes 6291460
  97.0 10.3 %collective-permute-start.4 = (f32[1024,128]{1,0:T(8,128)S(1)}, f32[1024,128]{1,0:T(8,128)S(1)}, u32[]{:S(2)}, u32[]{:S(2)}) collective-permute-start(f32[1024,128]{1,0:T(8,128)S(1)} %get-tuple-element.42.y_r), channel_id=1, source_target_pairs={{0,1},{1,2},{2,3},{3,4},{4,5},{5,6},{6,7},{7,8},{8,9},{9,10},{10,1... | collective-permute-start | bytes 1572872 | tf_op jit(solution)/shard_map/ppermute | solution.py:186
  100.0 11.2 %collective-permute-start.5 = (f32[1024,128]{1,0:T(8,128)S(1)}, f32[1024,128]{1,0:T(8,128)S(1)}, u32[]{:S(2)}, u32[]{:S(2)}) collective-permute-start(f32[1024,128]{1,0:T(8,128)S(1)} %get-tuple-element.43), channel_id=1, source_target_pairs={{1,0},{2,1},{3,2},{4,3},{5,4},{6,5},{7,6},{8,7},{9,8},{10,9},{11,1... | collective-permute-start | bytes 1572872 | tf_op jit(solution)/shard_map/ppermute | solution.py:186
  121.1 8.3 %collective-permute-start.6 = (f32[1024,128]{1,0:T(8,128)S(1)}, f32[1024,128]{1,0:T(8,128)S(1)}, u32[]{:S(2)}, u32[]{:S(2)}) collective-permute-start(f32[1024,128]{1,0:T(8,128)S(1)} %get-tuple-element.45.q_r), channel_id=1, source_target_pairs={{0,1},{1,2},{2,3},{3,4},{4,5},{5,6},{6,7},{7,8},{8,9},{9,10},{10,1... | collective-permute-start | bytes 1572872 | tf_op jit(solution)/shard_map/ppermute | solution.py:186
  123.3 9.9 %collective-permute-start.7 = (f32[1024,128]{1,0:T(8,128)S(1)}, f32[1024,128]{1,0:T(8,128)S(1)}, u32[]{:S(2)}, u32[]{:S(2)}) collective-permute-start(f32[1024,128]{1,0:T(8,128)S(1)} %get-tuple-element.46), channel_id=1, source_target_pairs={{1,0},{2,1},{3,2},{4,3},{5,4},{6,5},{7,6},{8,7},{9,8},{10,9},{11,1... | collective-permute-start | bytes 1572872 | tf_op jit(solution)/shard_map/ppermute | solution.py:186
  133.3 24.6 %copy-start.10 = (f32[1,2048]{1,0:T(1,128)S(1)}, f32[1,2048]{1,0:T(1,128)}, u32[]{:S(2)}) copy-start(f32[1,2048]{1,0:T(1,128)} %rate.1) | copy-start | bytes 24580
  158.8 1.3 copy-start.5
  160.1 38.4 %all-to-all-start.2 = ((f32[8,512,128]{2,1,0:T(8,128)}), f32[8,512,128]{2,1,0:T(8,128)S(1)}, u32[]{:S(2)}, u32[]{:S(2)}) async-start(f32[8,512,128]{2,1,0:T(8,128)} %copy-done.5), calls=%async_computation.2 | async-start | bytes 4194304 | tf_op jit(solution)/shard_map/all_to_all | solution.py:216

commit v2 on v1

v2 whole, which is shorter than its diff:
```python
import jax
import jax.numpy as jnp
from jax import lax
from jax.experimental import pallas as pl
from jax.experimental.pallas import tpu as pltpu
from jax.sharding import PartitionSpec as P

F32 = jnp.float32
BF16 = jnp.bfloat16
VMEM = pl.BlockSpec(memory_space=pltpu.VMEM)
ANY = pl.BlockSpec(memory_space=pl.ANY)
CHUNKS = 4


def call(kernel, name, outs, args, flops=0, in_specs=None, scratch=(), limit=24):
    moved = sum(a.size * a.dtype.itemsize for a in args)
    return pl.pallas_call(
        kernel,
        name=name,
        out_shape=[jax.ShapeDtypeStruct(shape, dtype) for shape, dtype in outs],
        in_specs=in_specs or [VMEM] * len(args),
        out_specs=[VMEM] * len(outs),
        scratch_shapes=scratch,
        compiler_params=pltpu.CompilerParams(vmem_limit_bytes=limit * 2**20),
        cost_estimate=pl.CostEstimate(flops=flops, bytes_accessed=moved, transcendentals=0),
    )(*args)


def pair(value):
    high = value.astype(BF16)
    return jnp.concatenate([high, (value - high.astype(F32)).astype(BF16)], axis=1)


def triple(value):
    high = value.astype(BF16)
    rest = value - high.astype(F32)
    middle = rest.astype(BF16)
    low = (rest - middle.astype(F32)).astype(BF16)
    return jnp.concatenate([high, middle, low], axis=1)


def fold(wide):
    return wide[:, :128] + wide[:, 128:256] + wide[:, 256:]


def to_multipliers(onehot, face):
    return fold(jnp.dot(onehot, triple(face), preferred_element_type=F32))


def to_left(onehot, block):
    return fold(lax.dot_general(onehot, triple(block), (((0,), (0,)), ((), ())), preferred_element_type=F32))


def column(row):
    width = row.shape[1]
    pieces = [jnp.transpose(jnp.broadcast_to(row[:, k : k + 128], (128, 128))) for k in range(0, width, 128)]
    return jnp.concatenate(pieces, axis=0)


def add_up(value):
    return jnp.sum(value, axis=0, keepdims=True)


def start_kernel(
    a_in, u_in, v_in, load_in, mass_in, perm_in, a, onehot, y_l, y_r, base, force, u, v, load, mass, perm, fields_sem, a_sem
):
    size = a.shape[0]
    half, rows = size // 2, size // CHUNKS
    small = [
        pltpu.make_async_copy(source, target, fields_sem.at[k])
        for k, (source, target) in enumerate(
            [(perm_in, perm), (mass_in, mass), (u_in, u), (v_in, v), (load_in, load)]
        )
    ]
    big = [
        pltpu.make_async_copy(a_in.at[pl.ds(k * rows, rows)], a.at[pl.ds(k * rows, rows)], a_sem.at[k])
        for k in range(CHUNKS)
    ]
    for copy in small + big:
        copy.start()
    small[0].wait()
    onehot[...] = (lax.broadcasted_iota(jnp.int32, (half, half), 0) == perm[...]).astype(F32).astype(BF16)
    for copy in small[1:]:
        copy.wait()
    weight = 2.0 * column(mass[...])
    outer = load[...].astype(F32)
    rhs = (outer + weight * (u[...] + v[...])).astype(BF16)
    before = 2.0 * u[...] + v[...]
    base[...] = before
    force[...] = outer - weight * before
    parts = []
    for k in range(CHUNKS):
        big[k].wait()
        parts.append(jnp.dot(a[k * rows : (k + 1) * rows], rhs, preferred_element_type=F32))
        if k == CHUNKS // 2 - 1:
            y_l[...] = to_multipliers(onehot[...], jnp.concatenate(parts, axis=0))
            parts = []
    y_r[...] = jnp.concatenate(parts, axis=0)


def prepare_kernel(a, onehot, force, mass, b, force_m, weight_m, turned):
    size = a.shape[0]
    half, rows = size // 2, size // CHUNKS
    hot = onehot[...]
    for k in range(CHUNKS):
        here = slice(k * rows, (k + 1) * rows)
        block = lax.dot_general(a[here, :half], hot, (((1,), (1,)), ((), ())), preferred_element_type=F32).astype(BF16)
        if k < CHUNKS // 2:
            turned[here] = block
        else:
            b[here, :half] = block
            b[here, half:] = a[here, half:]
    for k in range(CHUNKS):
        here = slice(k * rows, (k + 1) * rows)
        block = turned[:, here] if k < CHUNKS // 2 else a[:half, here]
        b[:half, here] = jnp.dot(hot, block, preferred_element_type=F32).astype(BF16)
    weight = 6.0 * column(mass[...])
    force_m[half:] = force[half:]
    force_m[:half] = to_multipliers(hot, force[:half])
    weight_m[half:] = weight[half:]
    weight_m[:half] = to_multipliers(hot, weight[:half])


def jump(f_l, f_r, from_left, from_right):
    sub = lax.axis_index("sub")
    left = jnp.where(sub == 0, 0.0, f_l[...] - from_left[...])
    right = jnp.where(sub == lax.axis_size("sub") - 1, 0.0, f_r[...] - from_right[...])
    return left, right


def first_kernel(b, y_l, y_r, from_left, from_right, q_l, q_r, t_l, t_r, sums):
    half = y_l.shape[0]
    left, right = jump(y_l, y_r, from_left, from_right)
    z = jnp.concatenate([pair(left), pair(right)], axis=0)
    wide = jnp.dot(b[...], z, preferred_element_type=F32)
    q = wide[:, :128]
    t = q + wide[:, 128:]
    q_l[...], q_r[...] = q[:half], q[half:]
    t_l[...], t_r[...] = t[:half], t[half:]
    rr = add_up(right * right)
    pw = add_up(left * q[:half]) + add_up(right * q[half:])
    sums[...] = jnp.concatenate([rr, pw, jnp.zeros((6, 128), F32)], axis=0)


def second_kernel(b, q_l, q_r, from_left, from_right, sums, s_l, s_r, spread):
    half = q_l.shape[0]
    left, right = jump(q_l, q_r, from_left, from_right)
    z = jnp.concatenate([pair(left), pair(right)], axis=0)
    wide = jnp.dot(b[...], z, preferred_element_type=F32)
    s = wide[:, :128] + wide[:, 128:]
    s_l[...], s_r[...] = s[:half], s[half:]
    ww = add_up(right * right)
    wfw = add_up(left * s[:half]) + add_up(right * s[half:])
    own = jnp.concatenate([sums[:2], ww, wfw, jnp.zeros((4, 128), F32)], axis=0)
    spread[...] = jnp.broadcast_to(own[None], spread.shape)


def corrected(gathered, y_l, y_r, q_l, q_r, t_l, t_r, s_l, s_r):
    total = jnp.sum(gathered[...], axis=0)
    rr, pw, ww, wfw = total[0:1], total[1:2], total[2:3], total[3:4]
    alpha = rr / pw
    ratio = ww / pw
    later = (alpha * alpha * ww - rr) / (alpha * alpha * (wfw - ww * ratio))
    gain = alpha * later

    def face(y, q, t, s):
        return y[...] - alpha * q[...] - gain * (ratio * t[...] - s[...])

    return face(y_l, q_l, t_l, s_l), face(y_r, q_r, t_r, s_r)


def next_kernel(b, gathered, y_l, y_r, q_l, q_r, t_l, t_r, s_l, s_r, force_m, weight_m, z_l, z_r, u_l, u_r):
    half = y_l.shape[0]
    left, right = corrected(gathered, y_l, y_r, q_l, q_r, t_l, t_r, s_l, s_r)
    u_l[...], u_r[...] = left, right
    rhs = (force_m[...] + weight_m[...] * jnp.concatenate([left, right], axis=0)).astype(BF16)
    y = jnp.dot(b[...], rhs, preferred_element_type=F32)
    z_l[...], z_r[...] = y[:half], y[half:]


def coarse(rate):
    scale = 1.0 / (1.0 + rate)
    return (1.0 - rate) * scale, 2.0 * scale, -2.0 * rate * scale


def early_kernel(onehot, u_l, u_r, base, u, v, rate, early_u, early_v, rate_own):
    tm = lax.axis_index("tm")
    half = u_l.shape[0]
    rates = column(rate[...])
    rate_own[...] = jnp.where(tm % 2 == 0, rates[:half], rates[half:])
    same, up, down = coarse(rates)
    later = jnp.concatenate([to_left(onehot[...], u_l[...]), u_r[...]], axis=0)
    early_u[...] = -jnp.where(tm == 0, 0.0, same * u[...] + up * v[...])
    early_v[...] = base[...] - 4.0 * later - jnp.where(tm == 0, 0.0, down * u[...] + same * v[...])


def finish_kernel(onehot, gathered, y_l, y_r, q_l, q_r, t_l, t_r, s_l, s_r, early_u, early_v, own, give):
    even = lax.axis_index("tm") % 2 == 0
    half = y_l.shape[0]
    left, right = corrected(gathered, y_l, y_r, q_l, q_r, t_l, t_r, s_l, s_r)
    left = to_left(onehot[...], left)
    for k, (early, factor) in enumerate([(early_u, 1.0), (early_v, 2.0)]):
        top = factor * left + early[:half]
        bottom = factor * right + early[half:]
        own[k] = jnp.where(even, top, bottom)
        give[k] = jnp.where(even, bottom, top)


def step_on(rate, state_u, state_v):
    same, up, down = coarse(rate)
    return same * state_u + up * state_v, down * state_u + same * state_v


def both_slices(own, got):
    even = lax.axis_index("tm") % 2 == 0
    return [jnp.where(even, own[k], got[k]) for k in range(2)], [jnp.where(even, got[k], own[k]) for k in range(2)]


def combine_kernel(own, got, rate_own, kept, ahead, across, behind, scratch):
    chip = lax.axis_index("tm") // 2
    chips = lax.axis_size("tm") // 2
    rows = kept.shape[1]
    first, second = both_slices(own, got)
    moved = step_on(rate_own[...], *first)
    for k in range(2):
        scratch[k] = second[k] + moved[k]
    for offset, out in enumerate([kept, ahead, across, behind]):
        start = pl.multiple_of(lax.rem(chip + offset, chips) * rows, rows)
        for k in range(2):
            out[k] = scratch[k, pl.ds(start, rows)]


def prefix_kernel(kept, from_1, from_2, from_3, rate_own, ahead, across, behind, mine, scratch):
    chip = lax.axis_index("tm") // 2
    chips = lax.axis_size("tm") // 2
    rows = kept.shape[1]
    for offset, arrived in enumerate([kept, from_1, from_2, from_3]):
        scratch[lax.rem(chip + chips - offset, chips)] = arrived[...]
    rate = rate_own[pl.ds(pl.multiple_of(chip * rows, rows), rows)]
    state = [scratch[0, k] for k in range(2)]
    for place in range(1, chips):
        after = [scratch[place, k] for k in range(2)]
        for k in range(2):
            scratch[place, k] = state[k]
        moved = step_on(rate, *step_on(rate, *state))
        state = [after[k] + moved[k] for k in range(2)]
    scratch[0] = jnp.zeros(scratch.shape[1:], F32)
    for offset, out in enumerate([mine, ahead, across, behind]):
        out[...] = scratch[lax.rem(chip + offset, chips)]


def end_kernel(mine, from_1, from_2, from_3, own, got, rate_own, stay, give, scratch):
    chip = lax.axis_index("tm") // 2
    chips = lax.axis_size("tm") // 2
    even = lax.axis_index("tm") % 2 == 0
    rows = mine.shape[1]
    for offset, arrived in enumerate([mine, from_1, from_2, from_3]):
        start = pl.multiple_of(lax.rem(chip + chips - offset, chips) * rows, rows)
        for k in range(2):
            scratch[k, pl.ds(start, rows)] = arrived[k]
    first, second = both_slices(own, got)
    rate = rate_own[...]
    moved = step_on(rate, scratch[0], scratch[1])
    first = [first[k] + moved[k] for k in range(2)]
    moved = step_on(rate, *first)
    second = [second[k] + moved[k] for k in range(2)]
    for k in range(2):
        stay[k] = jnp.where(even, first[k], second[k])
        give[k] = jnp.where(even, second[k], first[k])


def join_kernel(stay, got, end_u, end_v):
    even = lax.axis_index("tm") % 2 == 0
    half = stay.shape[1]
    for k, out in enumerate([end_u, end_v]):
        out[:half] = jnp.where(even, stay[k], got[k])
        out[half:] = jnp.where(even, got[k], stay[k])


def on_device(flex, mass, coarse_rate, face_perm, start_u, start_v, load):
    size, cases = start_u.shape[2:]
    half = size // 2
    subs, slices = lax.axis_size("sub"), lax.axis_size("tm")
    u, v, outer = start_u[0, 0], start_v[0, 0], load[0, 0]
    right = [(s, s + 1) for s in range(subs - 1)]
    left = [(s + 1, s) for s in range(subs - 1)]
    face = ((half, cases), F32)
    whole = ((size, cases), F32)
    square = ((size, size), BF16)
    once = 2 * size * size * cases

    def exchange(face_l, face_r):
        return lax.ppermute(face_r, "sub", right), lax.ppermute(face_l, "sub", left)

    a, onehot, y_l, y_r, base, force = call(
        start_kernel,
        "start",
        [square, ((half, half), BF16), face, face, whole, whole],
        (flex[0], u, v, outer, mass, face_perm),
        once,
        in_specs=[ANY] * 6,
        scratch=[
            pltpu.VMEM((size, cases), F32),
            pltpu.VMEM((size, cases), F32),
            pltpu.VMEM((size, cases), BF16),
            pltpu.VMEM((1, size), F32),
            pltpu.VMEM((1, half), jnp.int32),
            pltpu.SemaphoreType.DMA((5,)),
            pltpu.SemaphoreType.DMA((CHUNKS,)),
        ],
    )
    matrix = None
    for step in range(2):
        from_left, from_right = exchange(y_l, y_r)
        if step == 0:
            matrix, force_m, weight_m = call(
                prepare_kernel,
                "prepare",
                [square, whole, whole],
                (a, onehot, force, mass),
                8 * half**3 * 2,
                scratch=[pltpu.VMEM((half, half), BF16)],
            )
        else:
            early_u, early_v, rate_own = call(
                early_kernel, "early", [whole, whole, face], (onehot, u_l, u_r, base, u, v, coarse_rate), 3 * half * once // size
            )
        q_l, q_r, t_l, t_r, sums = call(
            first_kernel, "first", [face] * 4 + [((8, cases), F32)], (matrix, y_l, y_r, from_left, from_right), 2 * once
        )
        from_left, from_right = exchange(q_l, q_r)
        s_l, s_r, spread = call(
            second_kernel,
            "second",
            [face] * 2 + [((subs, 8, cases), F32)],
            (matrix, q_l, q_r, from_left, from_right, sums),
            2 * once,
        )
        gathered = lax.all_to_all(spread, "sub", 0, 0)
        fields = (gathered, y_l, y_r, q_l, q_r, t_l, t_r, s_l, s_r)
        if step == 0:
            y_l, y_r, u_l, u_r = call(next_kernel, "next", [face] * 4, (matrix,) + fields + (force_m, weight_m), once)

    chips = slices // 2
    rows = half // chips
    two = ((2, half, cases), F32)
    block = ((2, rows, cases), F32)
    light = size * cases * 10

    def swap(value):
        return lax.ppermute(value, "tm", [(t, t ^ 1) for t in range(slices)])

    own, give = call(finish_kernel, "finish", [two, two], (onehot,) + fields + (early_u, early_v), light)
    got = swap(give)
    kept, *out = call(
        combine_kernel, "combine", [block] * 4, (own, got, rate_own), light, scratch=[pltpu.VMEM((2, half, cases), F32)]
    )
    arrived = [
        lax.ppermute(out[k - 1], "tm", [(t, (t + 2 * k) % slices) for t in range(slices - 2)]) for k in range(1, chips)
    ]
    *out, mine = call(
        prefix_kernel,
        "prefix",
        [block] * 4,
        (kept, *arrived, rate_own),
        light,
        scratch=[pltpu.VMEM((chips, 2, rows, cases), F32)],
    )
    arrived = [
        lax.ppermute(out[k - 1], "tm", [(t, (t + 2 * k) % slices) for t in range(slices) if (t + 2 * k) % slices > 1])
        for k in range(1, chips)
    ]
    stay, give = call(
        end_kernel,
        "end",
        [two, two],
        (mine, *arrived, own, got, rate_own),
        light,
        scratch=[pltpu.VMEM((2, half, cases), F32)],
    )
    end_u, end_v = call(join_kernel, "join", [whole, whole], (stay, swap(give)), light)
    return end_u[None, None], end_v[None, None]


def solution(mesh):
    return jax.shard_map(
        on_device,
        mesh=mesh,
        in_specs=(
            P("sub", None, None),
            P("sub", None),
            P("sub", None),
            P("sub", None),
            P("tm", "sub", None, None),
            P("tm", "sub", None, None),
            P("tm", "sub", None, None),
        ),
        out_specs=(P("tm", "sub", None, None), P("tm", "sub", None, None)),
        check_vma=False,
    )
```

time: 231 us -> 207 us (0.90)
  blocking collectives: 65.5 us -> 20.9 us
  local copies, waits for them, and re-layouts: 7.69 us -> 35.6 us
  starting transfers between devices: 30.8 us -> 57.3 us
  waiting for transfers between devices: 71.8 us -> 50.2 us
  Pallas kernels: 53.5 us -> 39.2 us
    all_to_all x1 -> x0, blocking collectives: 29.8 us -> none  [on_device(): ends = lax.all_to_all(ends, 'tm', 0, 0)]
    ppermute x8 -> x16, starting transfers between devices: 18.7 us -> 48.3 us  [the longest x6 21 us: on_device(): lax.ppermute(out[k - 1], 'tm', [(t, (t + 2 * k) % slices) for t in range(...]
    unnamed x24 -> x72, local copies, waits for them, and re-layouts: 6.23 us -> 35.6 us
    all_to_all x1, waiting for transfers between devices: 26.3 us -> 0.01 us  [on_device(): gathered = lax.all_to_all(spread, 'sub', 0, 0)]
    all_to_all x2 -> x1, blocking collectives: 35.7 us -> 20.9 us  [on_device(): gathered = lax.all_to_all(spread, 'sub', 0, 0)]
    pallas_call x8 -> x13, Pallas kernels: 53.5 us -> 39.2 us  [call(): pl.pallas_call(kernel, name=name, out_shape=[jax.ShapeDtypeStruct(shape,...]
    ppermute x8 -> x16, waiting for transfers between devices: 45.5 us -> 50.2 us  [the longest x4 19.9 us: exchange(): lax.ppermute(face_r, 'sub', right)]
    all_to_all x1, starting transfers between devices: 12 us -> 8.97 us  [on_device(): gathered = lax.all_to_all(spread, 'sub', 0, 0)]
  transfers between devices with their start and end apart: 9 -> 17, of which waited for: 9 -> 12; matrix products, arithmetic and copies ran while one was open for 0% -> 0% of each run, Pallas kernels for 0% -> 6%
where the time goes in v2:
time: 207 us; the launch traced here: 204 us
  starting transfers between devices  57.3 us (28%)
  waiting for transfers between devices  50.2 us (24%)
  Pallas kernels  39.2 us (19%)
  local copies, waits for them, and re-layouts  35.6 us (17%)
  blocking collectives  20.9 us (10%)
    pallas_call x13, Pallas kernels, call(): pl.pallas_call(kernel, name=name, out_shape=[jax.ShapeDtypeStruct(shape,...  39.2 us
    unnamed x72, local copies, waits for them, and re-layouts  35.6 us
    ppermute x6, starting transfers between devices, on_device(): lax.ppermute(out[k - 1], 'tm', [(t, (t + 2 * k) % slices) for t in range(...  21 us
    all_to_all x1, blocking collectives, on_device(): gathered = lax.all_to_all(spread, 'sub', 0, 0)  20.9 us
    ppermute x4, waiting for transfers between devices, exchange(): lax.ppermute(face_r, 'sub', right)  19.9 us
    ppermute x4, starting transfers between devices, exchange(): lax.ppermute(face_r, 'sub', right)  13.8 us
    ppermute x6, waiting for transfers between devices, on_device(): lax.ppermute(out[k - 1], 'tm', [(t, (t + 2 * k) % slices) for t in range(...  13.8 us
    ppermute x4, waiting for transfers between devices, exchange(): lax.ppermute(face_l, 'sub', left)  11.9 us
  transfers between devices with their start and end apart: 17, of which 12 were waited for; matrix products, arithmetic and copies ran while one was open for 0% of the time, Pallas kernels for 6%

profile of v2, /device:TPU:1, one launch (start us, length us, event | category | flops | bytes accessed | tf_op | source)
XLA Modules:
  0.0 204.1 jit_solution(10313300129268346238)
XLA Ops:
  0.6 3.4 %copy-done = bf16[1,2048,2048]{2,1,0:T(8,128)(2,1)S(1)} copy-done((bf16[1,2048,2048]{2,1,0:T(8,128)(2,1)S(1)}, bf16[1,2048,2048]{2,1,0:T(8,128)(2,1)}, u32[]{:S(2)}) %copy-start) | copy-done | bytes 8388632
  4.0 1.2 copy-done.1
  5.2 1.2 copy-done.3
  6.5 1.0 copy-done.17
  8.9 7.6 %start.1 = (bf16[2048,2048]{1,0:T(8,128)(2,1)S(1)}, bf16[1024,1024]{1,0:T(8,128)(2,1)S(1)}, f32[1024,128]{1,0:T(8,128)S(1)}, f32[1024,128]{1,0:T(8,128)S(1)}, f3...) custom-call(bf16[2048,2048]{1,0:T(8,128)(2,1)S(1)} %bitcast.6, f32[2048,128]{1,0:T(8,128)S(1)} %bitcast.7, ...), custom_call_target="tpu_custom_call" | custom-call | flops 1073741824 | bytes 11022336 | tf_op jit(solution)/shard_map/start/pallas_call | solution.py:17
  16.5 3.3 %copy-done.34 = bf16[2048,2048]{1,0:T(8,128)(2,1)} copy-done((bf16[2048,2048]{1,0:T(8,128)(2,1)}, bf16[2048,2048]{1,0:T(8,128)(2,1)S(1)}, u32[]{:S(2)}) %copy-start.34) | copy-done | bytes 8388632
  19.8 4.4 %collective-permute-start = (f32[1024,128]{1,0:T(8,128)S(1)}, f32[1024,128]{1,0:T(8,128)S(1)}, u32[]{:S(2)}, u32[]{:S(2)}) collective-permute-start(f32[1024,128]{1,0:T(8,128)S(1)} %get-tuple-element.53.y_r), channel_id=1, source_target_pairs={{0,1},{1,2},{2,3},{3,4},{4,5},{5,6},{6,7},{7,8},{8,9},{9,10},{10,1... | collective-permute-start | bytes 1572872 | tf_op jit(solution)/shard_map/ppermute | solution.py:293
  24.2 1.5 collective-permute-start.1
  25.8 3.4 %copy-done.35 = bf16[2048,2048]{1,0:T(8,128)(2,1)S(1)} copy-done((bf16[2048,2048]{1,0:T(8,128)(2,1)S(1)}, bf16[2048,2048]{1,0:T(8,128)(2,1)}, u32[]{:S(2)}) %copy-start.35) | copy-done | bytes 8388632
  29.1 11.1 %prepare.1 = (bf16[2048,2048]{1,0:T(8,128)(2,1)S(1)}, f32[2048,128]{1,0:T(8,128)S(1)}, f32[2048,128]{1,0:T(8,128)S(1)}) custom-call(bf16[2048,2048]{1,0:T(8,128)(2,1)S(1)} %copy-done.35, bf16[1024,1024]{1,0:T(8,128)(2,1)S(1)} %get-tuple-element.48.onehot, f32[2048,128]{1,0:T(8,128)S(1)} %get-tuple-element.50.force, f32[1,2048]{1,0:T(1,128)S(1)} %copy-done.32), custom_call_target="tpu_custom_call" | custom-call | flops 17179869184 | bytes 11542528 | tf_op jit(solution)/shard_map/prepare/pallas_call | solution.py:17
  40.3 2.5 %first.2 = (f32[1024,128]{1,0:T(8,128)S(1)}, f32[1024,128]{1,0:T(8,128)S(1)}, f32[1024,128]{1,0:T(8,128)S(1)}, f32[1024,128]{1,0:T(8,128)S(1)}, f32[8,128]{1,0:T(8,128)S(1)}) custom-call(bf16[2048,2048]{1,0:T(8,128)(2,1)S(1)} %get-tuple-element.51.b, f32[1024,128]{1,0:T(8,128)S(1)} %get-tuple-element.52.y_l, f32[1024,128]{1,0:T(8,128)S(1)} %get-tuple-element.53.y_r, ...), custom_call_target="tpu_custom_call" | custom-call | flops 2147483648 | bytes 10485760 | tf_op jit(solution)/shard_map/first/pallas_call | solution.py:17
  42.7 4.2 %collective-permute-start.2 = (f32[1024,128]{1,0:T(8,128)S(1)}, f32[1024,128]{1,0:T(8,128)S(1)}, u32[]{:S(2)}, u32[]{:S(2)}) collective-permute-start(f32[1024,128]{1,0:T(8,128)S(1)} %get-tuple-element.55.q_r), channel_id=1, source_target_pairs={{0,1},{1,2},{2,3},{3,4},{4,5},{5,6},{6,7},{7,8},{8,9},{9,10},{10,1... | collective-permute-start | bytes 1572872 | tf_op jit(solution)/shard_map/ppermute | solution.py:293
  46.9 1.5 collective-permute-start.3
  48.5 8.6 %collective-permute-done.2.from_left = f32[1024,128]{1,0:T(8,128)S(1)} collective-permute-done((f32[1024,128]{1,0:T(8,128)S(1)}, f32[1024,128]{1,0:T(8,128)S(1)}, u32[]{:S(2)}, u32[]{:S(2)}) %collective-permute-start.2) | collective-permute-done | bytes 524320 | tf_op jit(solution)/shard_map/ppermute | solution.py:293
  57.0 4.2 %collective-permute-done.3.from_right = f32[1024,128]{1,0:T(8,128)S(1)} collective-permute-done((f32[1024,128]{1,0:T(8,128)S(1)}, f32[1024,128]{1,0:T(8,128)S(1)}, u32[]{:S(2)}, u32[]{:S(2)}) %collective-permute-start.3) | collective-permute-done | bytes 524320 | tf_op jit(solution)/shard_map/ppermute | solution.py:293
  61.2 2.5 %second.2 = (f32[1024,128]{1,0:T(8,128)S(1)}, f32[1024,128]{1,0:T(8,128)S(1)}, f32[32,8,128]{2,1,0:T(8,128)S(1)}) custom-call(bf16[2048,2048]{1,0:T(8,128)(2,1)S(1)} %get-tuple-element.51.b, f32[1024,128]{1,0:T(8,128)S(1)} %get-tuple-element.54.q_l, f32[1024,128]{1,0:T(8,128)S(1)} %get-tuple-element.55.q_r, ...), custom_call_target="tpu_custom_call" | custom-call | flops 2147483648 | bytes 10489856 | tf_op jit(solution)/shard_map/second/pallas_call | solution.py:17
  63.7 20.9 %all_to_all.10.gathered = f32[32,8,128]{2,1,0:T(8,128)S(1)} all-to-all(f32[32,8,128]{2,1,0:T(8,128)S(1)} %get-tuple-element.57), channel_id=1, replica_groups=mesh['tm'=8,'sub'=32] {'sub'}, dimensions={0} | all-to-all | bytes 262144 | tf_op jit(solution)/shard_map/all_to_all | solution.py:339
  84.5 2.5 %next.1 = (f32[1024,128]{1,0:T(8,128)S(1)}, f32[1024,128]{1,0:T(8,128)S(1)}, f32[1024,128]{1,0:T(8,128)S(1)}, f32[1024,128]{1,0:T(8,128)S(1)}) custom-call(bf16[2048,2048]{1,0:T(8,128)(2,1)S(1)} %get-tuple-element.51.b, f32[32,8,128]{2,1,0:T(8,128)S(1)} %all_to_all.10.gathered, f32[1024,128]{1,0:T(8,128)S(1)} %get-tuple-element.52.y_l, ...), custom_call_target="tpu_custom_call" | custom-call | flops 1073741824 | bytes 14811136 | tf_op jit(solution)/shard_map/next/pallas_call | solution.py:17
  87.1 2.8 %collective-permute-start.4 = (f32[1024,128]{1,0:T(8,128)S(1)}, f32[1024,128]{1,0:T(8,128)S(1)}, u32[]{:S(2)}, u32[]{:S(2)}) collective-permute-start(f32[1024,128]{1,0:T(8,128)S(1)} %get-tuple-element.65.y_r), channel_id=1, source_target_pairs={{0,1},{1,2},{2,3},{3,4},{4,5},{5,6},{6,7},{7,8},{8,9},{9,10},{10,1... | collective-permute-start | bytes 1572872 | tf_op jit(solution)/shard_map/ppermute | solution.py:293
  89.9 1.3 collective-permute-start.5
  91.2 6.2 %collective-permute-done.4.from_left = f32[1024,128]{1,0:T(8,128)S(1)} collective-permute-done((f32[1024,128]{1,0:T(8,128)S(1)}, f32[1024,128]{1,0:T(8,128)S(1)}, u32[]{:S(2)}, u32[]{:S(2)}) %collective-permute-start.4) | collective-permute-done | bytes 524320 | tf_op jit(solution)/shard_map/ppermute | solution.py:293
  97.5 3.9 %collective-permute-done.5.from_right = f32[1024,128]{1,0:T(8,128)S(1)} collective-permute-done((f32[1024,128]{1,0:T(8,128)S(1)}, f32[1024,128]{1,0:T(8,128)S(1)}, u32[]{:S(2)}, u32[]{:S(2)}) %collective-permute-start.5) | collective-permute-done | bytes 524320 | tf_op jit(solution)/shard_map/ppermute | solution.py:293
  101.4 2.5 %first.3 = (f32[1024,128]{1,0:T(8,128)S(1)}, f32[1024,128]{1,0:T(8,128)S(1)}, f32[1024,128]{1,0:T(8,128)S(1)}, f32[1024,128]{1,0:T(8,128)S(1)}, f32[8,128]{1,0:T(8,128)S(1)}) custom-call(bf16[2048,2048]{1,0:T(8,128)(2,1)S(1)} %get-tuple-element.51.b, f32[1024,128]{1,0:T(8,128)S(1)} %get-tuple-element.64.y_l, f32[1024,128]{1,0:T(8,128)S(1)} %get-tuple-element.65.y_r, ...), custom_call_target="tpu_custom_call" | custom-call | flops 2147483648 | bytes 10485760 | tf_op jit(solution)/shard_map/first/pallas_call | solution.py:17
  104.6 0.8 copy-done.24
  105.4 2.5 %collective-permute-start.6 = (f32[1024,128]{1,0:T(8,128)S(1)}, f32[1024,128]{1,0:T(8,128)S(1)}, u32[]{:S(2)}, u32[]{:S(2)}) collective-permute-start(f32[1024,128]{1,0:T(8,128)S(1)} %get-tuple-element.67.q_r), channel_id=1, source_target_pairs={{0,1},{1,2},{2,3},{3,4},{4,5},{5,6},{6,7},{7,8},{8,9},{9,10},{10,1... | collective-permute-start | bytes 1572872 | tf_op jit(solution)/shard_map/ppermute | solution.py:293
  107.9 1.3 collective-permute-start.7
  109.2 5.1 %collective-permute-done.6.from_left = f32[1024,128]{1,0:T(8,128)S(1)} collective-permute-done((f32[1024,128]{1,0:T(8,128)S(1)}, f32[1024,128]{1,0:T(8,128)S(1)}, u32[]{:S(2)}, u32[]{:S(2)}) %collective-permute-start.6) | collective-permute-done | bytes 524320 | tf_op jit(solution)/shard_map/ppermute | solution.py:293
  114.3 3.9 %collective-permute-done.7.from_right = f32[1024,128]{1,0:T(8,128)S(1)} collective-permute-done((f32[1024,128]{1,0:T(8,128)S(1)}, f32[1024,128]{1,0:T(8,128)S(1)}, u32[]{:S(2)}, u32[]{:S(2)}) %collective-permute-start.7) | collective-permute-done | bytes 524320 | tf_op jit(solution)/shard_map/ppermute | solution.py:293
  118.2 3.1 %second.3 = (f32[1024,128]{1,0:T(8,128)S(1)}, f32[1024,128]{1,0:T(8,128)S(1)}, f32[32,8,128]{2,1,0:T(8,128)}) custom-call(bf16[2048,2048]{1,0:T(8,128)(2,1)S(1)} %get-tuple-element.51.b, f32[1024,128]{1,0:T(8,128)S(1)} %get-tuple-element.66.q_l, f32[1024,128]{1,0:T(8,128)S(1)} %get-tuple-element.67.q_r, f32[1024,128]{1,0:T(8,128)S(1)} %collective-permute-done.6.from_left, ...), custom_call_target="tpu_custom_call" | custom-call | flops 2147483648 | bytes 10489856 | tf_op jit(solution)/shard_map/second/pallas_call | solution.py:17
  123.0 9.0 %all-to-all-start.1 = ((f32[32,8,128]{2,1,0:T(8,128)}), f32[32,8,128]{2,1,0:T(8,128)S(1)}, u32[]{:S(2)}, u32[]{:S(2)}) async-start(f32[32,8,128]{2,1,0:T(8,128)} %get-tuple-element.69), calls=%async_computation.1 | async-start | bytes 262144 | tf_op jit(solution)/shard_map/all_to_all | solution.py:339
  132.0 1.2 copy-done.2
  133.2 1.2 copy-done.4
  134.4 1.2 copy-done.12
  135.6 1.0 copy-done.19
  136.7 1.0 copy-done.21
  137.7 1.4 early.1
  139.2 1.0 copy-done.13
  140.1 1.0 copy-done.15
  141.1 1.0 copy-done.6
  142.2 1.0 copy-done.8
  143.2 1.0 copy-done.10
  144.2 1.2 copy-done.14
  145.5 1.2 copy-done.16
  146.7 1.0 copy-done.23
  147.7 1.0 copy-done.25
  148.8 1.0 copy-done.27
  149.8 1.0 copy-done.29
  150.9 1.4 finish.1
  152.3 7.0 %collective-permute-start.8 = (f32[2,1024,128]{2,1,0:T(8,128)S(1)}, f32[2,1024,128]{2,1,0:T(8,128)S(1)}, u32[]{:S(2)}, u32[]{:S(2)}) collective-permute-start(f32[2,1024,128]{2,1,0:T(8,128)S(1)} %get-tuple-element.80), channel_id=1, source_target_pairs={{0,32},{32,0},{64,96},{96,64},{128,160},{160,128},{192,224},{224,1... | collective-permute-start | bytes 3145736 | tf_op jit(solution)/shard_map/ppermute | solution.py:351
  159.3 2.3 %collective-permute-done.8.got = f32[2,1024,128]{2,1,0:T(8,128)S(1)} collective-permute-done((f32[2,1024,128]{2,1,0:T(8,128)S(1)}, f32[2,1024,128]{2,1,0:T(8,128)S(1)}, u32[]{:S(2)}, u32[]{:S(2)}) %collective-permute-start.8) | collective-permute-done | bytes 1048608 | tf_op jit(solution)/shard_map/ppermute | solution.py:351
  161.6 0.9 combine.1
  162.5 4.8 %collective-permute-start.10 = (f32[2,256,128]{2,1,0:T(8,128)S(1)}, f32[2,256,128]{2,1,0:T(8,128)S(1)}, u32[]{:S(2)}, u32[]{:S(2)}) collective-permute-start(f32[2,256,128]{2,1,0:T(8,128)S(1)} %get-tuple-element.84), channel_id=1, source_target_pairs={{0,128},{32,160},{64,192},{96,224},{128,0},{160,32},{1,129},{33,16... | collective-permute-start | bytes 786440 | tf_op jit(solution)/shard_map/ppermute | solution.py:359
  167.3 1.9 collective-permute-start.11
  169.3 3.4 %collective-permute-start.9 = (f32[2,256,128]{2,1,0:T(8,128)S(1)}, f32[2,256,128]{2,1,0:T(8,128)S(1)}, u32[]{:S(2)}, u32[]{:S(2)}) collective-permute-start(f32[2,256,128]{2,1,0:T(8,128)S(1)} %get-tuple-element.83), channel_id=1, source_target_pairs={{0,64},{32,96},{64,128},{96,160},{128,192},{160,224},{1,65},{33,97... | collective-permute-start | bytes 786440 | tf_op jit(solution)/shard_map/ppermute | solution.py:359
  173.4 6.0 %collective-permute-done.11.from_3 = f32[2,256,128]{2,1,0:T(8,128)S(1)} collective-permute-done((f32[2,256,128]{2,1,0:T(8,128)S(1)}, f32[2,256,128]{2,1,0:T(8,128)S(1)}, u32[]{:S(2)}, u32[]{:S(2)}) %collective-permute-start.11) | collective-permute-done | bytes 262176 | tf_op jit(solution)/shard_map/ppermute | solution.py:359
  180.0 2.6 %collective-permute-start.12 = (f32[2,256,128]{2,1,0:T(8,128)S(1)}, f32[2,256,128]{2,1,0:T(8,128)S(1)}, u32[]{:S(2)}, u32[]{:S(2)}) collective-permute-start(f32[2,256,128]{2,1,0:T(8,128)S(1)} %get-tuple-element.87), channel_id=1, source_target_pairs={{0,64},{32,96},{64,128},{96,160},{128,192},{160,224},{1,65},{33,97... | collective-permute-start | bytes 786440 | tf_op jit(solution)/shard_map/ppermute | solution.py:370
  182.6 5.5 %collective-permute-start.13 = (f32[2,256,128]{2,1,0:T(8,128)S(1)}, f32[2,256,128]{2,1,0:T(8,128)S(1)}, u32[]{:S(2)}, u32[]{:S(2)}) collective-permute-start(f32[2,256,128]{2,1,0:T(8,128)S(1)} %get-tuple-element.88), channel_id=1, source_target_pairs={{0,128},{32,160},{64,192},{96,224},{192,64},{224,96},{1,129},{33,1... | collective-permute-start | bytes 786440 | tf_op jit(solution)/shard_map/ppermute | solution.py:370
  188.1 2.7 %collective-permute-start.14 = (f32[2,256,128]{2,1,0:T(8,128)S(1)}, f32[2,256,128]{2,1,0:T(8,128)S(1)}, u32[]{:S(2)}, u32[]{:S(2)}) collective-permute-start(f32[2,256,128]{2,1,0:T(8,128)S(1)} %get-tuple-element.89), channel_id=1, source_target_pairs={{0,192},{32,224},{128,64},{160,96},{192,128},{224,160},{1,193},{33... | collective-permute-start | bytes 786440 | tf_op jit(solution)/shard_map/ppermute | solution.py:370
  190.9 2.5 %collective-permute-done.13.from_2 = f32[2,256,128]{2,1,0:T(8,128)S(1)} collective-permute-done((f32[2,256,128]{2,1,0:T(8,128)S(1)}, f32[2,256,128]{2,1,0:T(8,128)S(1)}, u32[]{:S(2)}, u32[]{:S(2)}) %collective-permute-start.13) | collective-permute-done | bytes 262176 | tf_op jit(solution)/shard_map/ppermute | solution.py:370
  193.3 4.6 %collective-permute-done.14.from_3 = f32[2,256,128]{2,1,0:T(8,128)S(1)} collective-permute-done((f32[2,256,128]{2,1,0:T(8,128)S(1)}, f32[2,256,128]{2,1,0:T(8,128)S(1)}, u32[]{:S(2)}, u32[]{:S(2)}) %collective-permute-start.14) | collective-permute-done | bytes 262176 | tf_op jit(solution)/shard_map/ppermute | solution.py:370
  197.9 1.5 end.1
  199.4 0.9 collective-permute-start.15
  200.3 2.3 %collective-permute-done.15.got = f32[2,1024,128]{2,1,0:T(8,128)S(1)} collective-permute-done((f32[2,1024,128]{2,1,0:T(8,128)S(1)}, f32[2,1024,128]{2,1,0:T(8,128)S(1)}, u32[]{:S(2)}, u32[]{:S(2)}) %collective-permute-start.15) | collective-permute-done | bytes 1048608 | tf_op jit(solution)/shard_map/ppermute | solution.py:351
  202.6 1.5 join.1
  (56 shorter events, 5.2 us)
Async XLA Ops:
  0.6 3.4 %copy-start = (bf16[1,2048,2048]{2,1,0:T(8,128)(2,1)S(1)}, bf16[1,2048,2048]{2,1,0:T(8,128)(2,1)}, u32[]{:S(2)}) copy-start(bf16[1,2048,2048]{2,1,0:T(8,128)(2,1)} %param.7) | copy-start | bytes 25165828
  4.0 1.2 copy-start.1
  5.2 1.2 copy-start.3
  6.5 1.0 copy-start.17
  7.5 0.7 copy-start.31
  8.2 0.7 copy-start.33
  8.9 16.8 %copy-start.32 = (f32[1,2048]{1,0:T(1,128)S(1)}, f32[1,2048]{1,0:T(1,128)}, u32[]{:S(2)}) copy-start(f32[1,2048]{1,0:T(1,128)} %mass.1) | copy-start | bytes 24580
  16.5 3.3 %copy-start.34 = (bf16[2048,2048]{1,0:T(8,128)(2,1)}, bf16[2048,2048]{1,0:T(8,128)(2,1)S(1)}, u32[]{:S(2)}) copy-start(bf16[2048,2048]{1,0:T(8,128)(2,1)S(1)} %get-tuple-element.49.a) | copy-start | bytes 25165828
  19.8 20.4 %copy-start.11 = (f32[2048,128]{1,0:T(8,128)}, f32[2048,128]{1,0:T(8,128)S(1)}, u32[]{:S(2)}) copy-start(f32[2048,128]{1,0:T(8,128)S(1)} %get-tuple-element.76.base) | copy-start | bytes 3145732
  19.8 20.4 %collective-permute-start = (f32[1024,128]{1,0:T(8,128)S(1)}, f32[1024,128]{1,0:T(8,128)S(1)}, u32[]{:S(2)}, u32[]{:S(2)}) collective-permute-start(f32[1024,128]{1,0:T(8,128)S(1)} %get-tuple-element.53.y_r), channel_id=1, source_target_pairs={{0,1},{1,2},{2,3},{3,4},{4,5},{5,6},{6,7},{7,8},{8,9},{9,10},{10,1... | collective-permute-start | bytes 1572872 | tf_op jit(solution)/shard_map/ppermute | solution.py:293
  24.2 16.0 %collective-permute-start.1 = (f32[1024,128]{1,0:T(8,128)S(1)}, f32[1024,128]{1,0:T(8,128)S(1)}, u32[]{:S(2)}, u32[]{:S(2)}) collective-permute-start(f32[1024,128]{1,0:T(8,128)S(1)} %get-tuple-element.52.y_l), channel_id=1, source_target_pairs={{1,0},{2,1},{3,2},{4,3},{5,4},{6,5},{7,6},{8,7},{9,8},{10,9},{11,1... | collective-permute-start | bytes 1572872 | tf_op jit(solution)/shard_map/ppermute | solution.py:293
  25.7 3.4 %copy-start.35 = (bf16[2048,2048]{1,0:T(8,128)(2,1)S(1)}, bf16[2048,2048]{1,0:T(8,128)(2,1)}, u32[]{:S(2)}) copy-start(bf16[2048,2048]{1,0:T(8,128)(2,1)} %copy-done.34) | copy-start | bytes 25165828
  42.7 14.3 %collective-permute-start.2 = (f32[1024,128]{1,0:T(8,128)S(1)}, f32[1024,128]{1,0:T(8,128)S(1)}, u32[]{:S(2)}, u32[]{:S(2)}) collective-permute-start(f32[1024,128]{1,0:T(8,128)S(1)} %get-tuple-element.55.q_r), channel_id=1, source_target_pairs={{0,1},{1,2},{2,3},{3,4},{4,5},{5,6},{6,7},{7,8},{8,9},{9,10},{10,1... | collective-permute-start | bytes 1572872 | tf_op jit(solution)/shard_map/ppermute | solution.py:293
  46.9 14.3 %collective-permute-start.3 = (f32[1024,128]{1,0:T(8,128)S(1)}, f32[1024,128]{1,0:T(8,128)S(1)}, u32[]{:S(2)}, u32[]{:S(2)}) collective-permute-start(f32[1024,128]{1,0:T(8,128)S(1)} %get-tuple-element.54.q_l), channel_id=1, source_target_pairs={{1,0},{2,1},{3,2},{4,3},{5,4},{6,5},{7,6},{8,7},{9,8},{10,9},{11,1... | collective-permute-start | bytes 1572872 | tf_op jit(solution)/shard_map/ppermute | solution.py:293
  87.1 34.2 %copy-start.5 = (f32[1024,128]{1,0:T(8,128)}, f32[1024,128]{1,0:T(8,128)S(1)}, u32[]{:S(2)}) copy-start(f32[1024,128]{1,0:T(8,128)S(1)} %get-tuple-element.65.y_r) | copy-start | bytes 1572868
  87.1 34.2 %copy-start.18 = (f32[1024,128]{1,0:T(8,128)}, f32[1024,128]{1,0:T(8,128)S(1)}, u32[]{:S(2)}) copy-start(f32[1024,128]{1,0:T(8,128)S(1)} %get-tuple-element.74.u_l) | copy-start | bytes 1572868
  87.1 34.2 %copy-start.20 = (f32[1024,128]{1,0:T(8,128)}, f32[1024,128]{1,0:T(8,128)S(1)}, u32[]{:S(2)}) copy-start(f32[1024,128]{1,0:T(8,128)S(1)} %get-tuple-element.75.u_r) | copy-start | bytes 1572868
  87.1 10.4 %collective-permute-start.4 = (f32[1024,128]{1,0:T(8,128)S(1)}, f32[1024,128]{1,0:T(8,128)S(1)}, u32[]{:S(2)}, u32[]{:S(2)}) collective-permute-start(f32[1024,128]{1,0:T(8,128)S(1)} %get-tuple-element.65.y_r), channel_id=1, source_target_pairs={{0,1},{1,2},{2,3},{3,4},{4,5},{5,6},{6,7},{7,8},{8,9},{9,10},{10,1... | collective-permute-start | bytes 1572872 | tf_op jit(solution)/shard_map/ppermute | solution.py:293
  89.9 42.0 %copy-start.30 = (f32[1,2048]{1,0:T(1,128)S(1)}, f32[1,2048]{1,0:T(1,128)}, u32[]{:S(2)}) copy-start(f32[1,2048]{1,0:T(1,128)} %rate.1) | copy-start | bytes 24580
  89.9 11.4 %collective-permute-start.5 = (f32[1024,128]{1,0:T(8,128)S(1)}, f32[1024,128]{1,0:T(8,128)S(1)}, u32[]{:S(2)}, u32[]{:S(2)}) collective-permute-start(f32[1024,128]{1,0:T(8,128)S(1)} %get-tuple-element.64.y_l), channel_id=1, source_target_pairs={{1,0},{2,1},{3,2},{4,3},{5,4},{6,5},{7,6},{8,7},{9,8},{10,9},{11,1... | collective-permute-start | bytes 1572872 | tf_op jit(solution)/shard_map/ppermute | solution.py:293
  103.8 0.8 copy-start.22
  104.6 0.8 copy-start.24
  105.4 15.9 %copy-start.7 = (f32[1024,128]{1,0:T(8,128)}, f32[1024,128]{1,0:T(8,128)S(1)}, u32[]{:S(2)}) copy-start(f32[1024,128]{1,0:T(8,128)S(1)} %get-tuple-element.66.q_l) | copy-start | bytes 1572868
  105.4 15.9 %copy-start.9 = (f32[1024,128]{1,0:T(8,128)}, f32[1024,128]{1,0:T(8,128)S(1)}, u32[]{:S(2)}) copy-start(f32[1024,128]{1,0:T(8,128)S(1)} %get-tuple-element.67.q_r) | copy-start | bytes 1572868
  105.4 8.9 %collective-permute-start.6 = (f32[1024,128]{1,0:T(8,128)S(1)}, f32[1024,128]{1,0:T(8,128)S(1)}, u32[]{:S(2)}, u32[]{:S(2)}) collective-permute-start(f32[1024,128]{1,0:T(8,128)S(1)} %get-tuple-element.67.q_r), channel_id=1, source_target_pairs={{0,1},{1,2},{2,3},{3,4},{4,5},{5,6},{6,7},{7,8},{8,9},{9,10},{10,1... | collective-permute-start | bytes 1572872 | tf_op jit(solution)/shard_map/ppermute | solution.py:293
  107.9 10.3 %collective-permute-start.7 = (f32[1024,128]{1,0:T(8,128)S(1)}, f32[1024,128]{1,0:T(8,128)S(1)}, u32[]{:S(2)}, u32[]{:S(2)}) collective-permute-start(f32[1024,128]{1,0:T(8,128)S(1)} %get-tuple-element.66.q_l), channel_id=1, source_target_pairs={{1,0},{2,1},{3,2},{4,3},{5,4},{6,5},{7,6},{8,7},{9,8},{10,9},{11,1... | collective-permute-start | bytes 1572872 | tf_op jit(solution)/shard_map/ppermute | solution.py:293
  121.4 0.8 copy-start.26
  122.2 0.8 copy-start.28
  123.0 18.2 %all-to-all-start.1 = ((f32[32,8,128]{2,1,0:T(8,128)}), f32[32,8,128]{2,1,0:T(8,128)S(1)}, u32[]{:S(2)}, u32[]{:S(2)}) async-start(f32[32,8,128]{2,1,0:T(8,128)} %get-tuple-element.69), calls=%async_computation.1 | async-start | bytes 262144 | tf_op jit(solution)/shard_map/all_to_all | solution.py:339
  131.9 1.2 copy-start.2
  133.2 1.2 copy-start.4
  134.4 1.2 copy-start.12
  135.6 1.0 copy-start.19
  136.7 1.0 copy-start.21
  139.2 1.0 copy-start.13
  140.1 1.0 copy-start.15
  141.1 1.0 copy-start.6
  142.2 1.0 copy-start.8
  143.2 1.0 copy-start.10
  144.2 1.2 copy-start.14
  145.5 1.2 copy-start.16
  146.7 1.0 copy-start.23
  147.7 1.0 copy-start.25
  148.8 1.0 copy-start.27
  149.8 1.0 copy-start.29
  152.3 9.3 %collective-permute-start.8 = (f32[2,1024,128]{2,1,0:T(8,128)S(1)}, f32[2,1024,128]{2,1,0:T(8,128)S(1)}, u32[]{:S(2)}, u32[]{:S(2)}) collective-permute-start(f32[2,1024,128]{2,1,0:T(8,128)S(1)} %get-tuple-element.80), channel_id=1, source_target_pairs={{0,32},{32,0},{64,96},{96,64},{128,160},{160,128},{192,224},{224,1... | collective-permute-start | bytes 3145736 | tf_op jit(solution)/shard_map/ppermute | solution.py:351
  162.5 10.9 %collective-permute-start.10 = (f32[2,256,128]{2,1,0:T(8,128)S(1)}, f32[2,256,128]{2,1,0:T(8,128)S(1)}, u32[]{:S(2)}, u32[]{:S(2)}) collective-permute-start(f32[2,256,128]{2,1,0:T(8,128)S(1)} %get-tuple-element.84), channel_id=1, source_target_pairs={{0,128},{32,160},{64,192},{96,224},{128,0},{160,32},{1,129},{33,16... | collective-permute-start | bytes 786440 | tf_op jit(solution)/shard_map/ppermute | solution.py:359
  167.3 12.1 %collective-permute-start.11 = (f32[2,256,128]{2,1,0:T(8,128)S(1)}, f32[2,256,128]{2,1,0:T(8,128)S(1)}, u32[]{:S(2)}, u32[]{:S(2)}) collective-permute-start(f32[2,256,128]{2,1,0:T(8,128)S(1)} %get-tuple-element.85), channel_id=1, source_target_pairs={{0,192},{32,224},{64,0},{96,32},{128,64},{160,96},{1,193},{33,225}... | collective-permute-start | bytes 786440 | tf_op jit(solution)/shard_map/ppermute | solution.py:359
  169.3 10.2 %collective-permute-start.9 = (f32[2,256,128]{2,1,0:T(8,128)S(1)}, f32[2,256,128]{2,1,0:T(8,128)S(1)}, u32[]{:S(2)}, u32[]{:S(2)}) collective-permute-start(f32[2,256,128]{2,1,0:T(8,128)S(1)} %get-tuple-element.83), channel_id=1, source_target_pairs={{0,64},{32,96},{64,128},{96,160},{128,192},{160,224},{1,65},{33,97... | collective-permute-start | bytes 786440 | tf_op jit(solution)/shard_map/ppermute | solution.py:359
  180.0 10.9 %collective-permute-start.12 = (f32[2,256,128]{2,1,0:T(8,128)S(1)}, f32[2,256,128]{2,1,0:T(8,128)S(1)}, u32[]{:S(2)}, u32[]{:S(2)}) collective-permute-start(f32[2,256,128]{2,1,0:T(8,128)S(1)} %get-tuple-element.87), channel_id=1, source_target_pairs={{0,64},{32,96},{64,128},{96,160},{128,192},{160,224},{1,65},{33,97... | collective-permute-start | bytes 786440 | tf_op jit(solution)/shard_map/ppermute | solution.py:370
  182.6 10.7 %collective-permute-start.13 = (f32[2,256,128]{2,1,0:T(8,128)S(1)}, f32[2,256,128]{2,1,0:T(8,128)S(1)}, u32[]{:S(2)}, u32[]{:S(2)}) collective-permute-start(f32[2,256,128]{2,1,0:T(8,128)S(1)} %get-tuple-element.88), channel_id=1, source_target_pairs={{0,128},{32,160},{64,192},{96,224},{192,64},{224,96},{1,129},{33,1... | collective-permute-start | bytes 786440 | tf_op jit(solution)/shard_map/ppermute | solution.py:370
  188.1 9.8 %collective-permute-start.14 = (f32[2,256,128]{2,1,0:T(8,128)S(1)}, f32[2,256,128]{2,1,0:T(8,128)S(1)}, u32[]{:S(2)}, u32[]{:S(2)}) collective-permute-start(f32[2,256,128]{2,1,0:T(8,128)S(1)} %get-tuple-element.89), channel_id=1, source_target_pairs={{0,192},{32,224},{128,64},{160,96},{192,128},{224,160},{1,193},{33... | collective-permute-start | bytes 786440 | tf_op jit(solution)/shard_map/ppermute | solution.py:370
  199.4 3.2 %collective-permute-start.15 = (f32[2,1024,128]{2,1,0:T(8,128)S(1)}, f32[2,1024,128]{2,1,0:T(8,128)S(1)}, u32[]{:S(2)}, u32[]{:S(2)}) collective-permute-start(f32[2,1024,128]{2,1,0:T(8,128)S(1)} %get-tuple-element.91), channel_id=1, source_target_pairs={{0,32},{32,0},{64,96},{96,64},{128,160},{160,128},{192,224},{224,1... | collective-permute-start | bytes 3145736 | tf_op jit(solution)/shard_map/ppermute | solution.py:351

commit v3 on v2

--- a/solution.py
+++ b/solution.py
@@ -8,16 +8,16 @@
 F32 = jnp.float32
 BF16 = jnp.bfloat16
 VMEM = pl.BlockSpec(memory_space=pltpu.VMEM)
-ANY = pl.BlockSpec(memory_space=pl.ANY)
+HBM = pl.BlockSpec(memory_space=pltpu.HBM)
 CHUNKS = 4
 
 
-def call(kernel, name, outs, args, flops=0, in_specs=None, scratch=(), limit=24):
+def call(kernel, name, outs, args, flops=0, in_specs=None, scratch=(), limit=12, space=pltpu.VMEM):
     moved = sum(a.size * a.dtype.itemsize for a in args)
     return pl.pallas_call(
         kernel,
         name=name,
-        out_shape=[jax.ShapeDtypeStruct(shape, dtype) for shape, dtype in outs],
+        out_shape=[space(shape, dtype) for shape, dtype in outs],
         in_specs=in_specs or [VMEM] * len(args),
         out_specs=[VMEM] * len(outs),
         scratch_shapes=scratch,
@@ -98,7 +98,8 @@
     y_r[...] = jnp.concatenate(parts, axis=0)
 
 
-def prepare_kernel(a, onehot, force, mass, b, force_m, weight_m, turned):
+def prepare_kernel(a, onehot, b, order, turned):
+    order[...] = jnp.zeros(order.shape, F32)
     size = a.shape[0]
     half, rows = size // 2, size // CHUNKS
     hot = onehot[...]
@@ -114,11 +115,31 @@
         here = slice(k * rows, (k + 1) * rows)
         block = turned[:, here] if k < CHUNKS // 2 else a[:half, here]
         b[:half, here] = jnp.dot(hot, block, preferred_element_type=F32).astype(BF16)
+
+
+def ready_kernel(onehot, force, mass_in, rate_in, u_in, v_in, base, sums_in, force_m, weight_m, early_u, early_v, rate_own, sums, mass, rate, u, v, sem):
+    copies = [
+        pltpu.make_async_copy(source, target, sem.at[k]) for k, (source, target) in enumerate([(mass_in, mass), (rate_in, rate), (u_in, u), (v_in, v)])
+    ]
+    for copy in copies:
+        copy.start()
+    sums[...] = sums_in[...]
+    hot = onehot[...]
+    half = hot.shape[0]
+    copies[0].wait()
     weight = 6.0 * column(mass[...])
     force_m[half:] = force[half:]
     force_m[:half] = to_multipliers(hot, force[:half])
     weight_m[half:] = weight[half:]
     weight_m[:half] = to_multipliers(hot, weight[:half])
+    for copy in copies[1:]:
+        copy.wait()
+    tm = lax.axis_index("tm")
+    rates = column(rate[...])
+    rate_own[...] = jnp.where(tm % 2 == 0, rates[:half], rates[half:])
+    same, up, down = coarse(rates)
+    early_u[...] = -jnp.where(tm == 0, 0.0, same * u[...] + up * v[...])
+    early_v[...] = base[...] - jnp.where(tm == 0, 0.0, down * u[...] + same * v[...])
 
 
 def jump(f_l, f_r, from_left, from_right):
@@ -128,7 +149,7 @@
     return left, right
 
 
-def first_kernel(b, y_l, y_r, from_left, from_right, q_l, q_r, t_l, t_r, sums):
+def first_kernel(b, y_l, y_r, from_left, from_right, order, q_l, q_r, t_l, t_r, sums):
     half = y_l.shape[0]
     left, right = jump(y_l, y_r, from_left, from_right)
     z = jnp.concatenate([pair(left), pair(right)], axis=0)
@@ -139,7 +160,7 @@
     t_l[...], t_r[...] = t[:half], t[half:]
     rr = add_up(right * right)
     pw = add_up(left * q[:half]) + add_up(right * q[half:])
-    sums[...] = jnp.concatenate([rr, pw, jnp.zeros((6, 128), F32)], axis=0)
+    sums[...] = jnp.concatenate([rr, pw, order[2:]], axis=0)
 
 
 def second_kernel(b, q_l, q_r, from_left, from_right, sums, s_l, s_r, spread):
@@ -183,15 +204,11 @@
     return (1.0 - rate) * scale, 2.0 * scale, -2.0 * rate * scale
 
 
-def early_kernel(onehot, u_l, u_r, base, u, v, rate, early_u, early_v, rate_own):
-    tm = lax.axis_index("tm")
+def early_kernel(onehot, u_l, u_r, early_in, early_v, order):
+    order[...] = jnp.zeros(order.shape, F32)
     half = u_l.shape[0]
-    rates = column(rate[...])
-    rate_own[...] = jnp.where(tm % 2 == 0, rates[:half], rates[half:])
-    same, up, down = coarse(rates)
-    later = jnp.concatenate([to_left(onehot[...], u_l[...]), u_r[...]], axis=0)
-    early_u[...] = -jnp.where(tm == 0, 0.0, same * u[...] + up * v[...])
-    early_v[...] = base[...] - 4.0 * later - jnp.where(tm == 0, 0.0, down * u[...] + same * v[...])
+    early_v[:half] = early_in[:half] - 4.0 * to_left(onehot[...], u_l[...])
+    early_v[half:] = early_in[half:] - 4.0 * u_r[...]
 
 
 def finish_kernel(onehot, gathered, y_l, y_r, q_l, q_r, t_l, t_r, s_l, s_r, early_u, early_v, own, give):
@@ -281,11 +298,15 @@
     size, cases = start_u.shape[2:]
     half = size // 2
     subs, slices = lax.axis_size("sub"), lax.axis_size("tm")
-    u, v, outer = start_u[0, 0], start_v[0, 0], load[0, 0]
+    flex, mass, coarse_rate, face_perm, u, v, outer = [
+        pltpu.with_memory_space_constraint(value, pltpu.HBM)
+        for value in (flex[0], mass, coarse_rate, face_perm, start_u[0, 0], start_v[0, 0], load[0, 0])
+    ]
     right = [(s, s + 1) for s in range(subs - 1)]
     left = [(s + 1, s) for s in range(subs - 1)]
     face = ((half, cases), F32)
     whole = ((size, cases), F32)
+    small = ((8, cases), F32)
     square = ((size, size), BF16)
     once = 2 * size * size * cases
 
@@ -296,9 +317,9 @@
         start_kernel,
         "start",
         [square, ((half, half), BF16), face, face, whole, whole],
-        (flex[0], u, v, outer, mass, face_perm),
+        (flex, u, v, outer, mass, face_perm),
         once,
-        in_specs=[ANY] * 6,
+        in_specs=[HBM] * 6,
         scratch=[
             pltpu.VMEM((size, cases), F32),
             pltpu.VMEM((size, cases), F32),
@@ -313,22 +334,31 @@
     for step in range(2):
         from_left, from_right = exchange(y_l, y_r)
         if step == 0:
-            matrix, force_m, weight_m = call(
-                prepare_kernel,
-                "prepare",
-                [square, whole, whole],
-                (a, onehot, force, mass),
-                8 * half**3 * 2,
-                scratch=[pltpu.VMEM((half, half), BF16)],
+            matrix, order = call(
+                prepare_kernel, "prepare", [square, small], (a, onehot), 8 * half**3, scratch=[pltpu.VMEM((half, half), BF16)]
             )
         else:
-            early_u, early_v, rate_own = call(
-                early_kernel, "early", [whole, whole, face], (onehot, u_l, u_r, base, u, v, coarse_rate), 3 * half * once // size
-            )
+            early_v, order = call(early_kernel, "early", [whole, small], (onehot, u_l, u_r, early_v), 2 * half * half * 3 * cases)
         q_l, q_r, t_l, t_r, sums = call(
-            first_kernel, "first", [face] * 4 + [((8, cases), F32)], (matrix, y_l, y_r, from_left, from_right), 2 * once
+            first_kernel, "first", [face] * 4 + [small], (matrix, y_l, y_r, from_left, from_right, order), 2 * once
         )
         from_left, from_right = exchange(q_l, q_r)
+        if step == 0:
+            force_m, weight_m, early_u, early_v, rate_own, sums = call(
+                ready_kernel,
+                "ready",
+                [whole] * 4 + [face, small],
+                (onehot, force, mass, coarse_rate, u, v, base, sums),
+                2 * half * half * 6 * cases,
+                in_specs=[VMEM] * 2 + [HBM] * 4 + [VMEM] * 2,
+                scratch=[
+                    pltpu.VMEM((1, size), F32),
+                    pltpu.VMEM((1, size), F32),
+                    pltpu.VMEM((size, cases), F32),
+                    pltpu.VMEM((size, cases), F32),
+                    pltpu.SemaphoreType.DMA((4,)),
+                ],
+            )
         s_l, s_r, spread = call(
             second_kernel,
             "second",
@@ -378,7 +408,7 @@
         light,
         scratch=[pltpu.VMEM((2, half, cases), F32)],
     )
-    end_u, end_v = call(join_kernel, "join", [whole, whole], (stay, swap(give)), light)
+    end_u, end_v = call(join_kernel, "join", [whole, whole], (stay, swap(give)), light, space=jax.ShapeDtypeStruct)
     return end_u[None, None], end_v[None, None]
 
 

time: 207 us -> 177 us (0.86); the launches traced: 204 us -> 177 us
  local copies, waits for them, and re-layouts: 35.6 us -> 0 us
  blocking collectives: 20.9 us -> 42.1 us
  waiting for transfers between devices: 50.2 us -> 38 us
  starting transfers between devices: 57.3 us -> 52.9 us
  Pallas kernels: 39.2 us -> 42.6 us
    unnamed x72 -> x0, local copies, waits for them, and re-layouts: 35.6 us -> none
    all_to_all x1 -> x2, blocking collectives: 20.9 us -> 42.1 us  [on_device(): gathered = lax.all_to_all(spread, 'sub', 0, 0)]
    ppermute x4, waiting for transfers between devices: 19.9 us -> 3.28 us  [exchange(): lax.ppermute(face_r, 'sub', right)]
    all_to_all x1 -> x0, starting transfers between devices: 8.97 us -> none  [on_device(): gathered = lax.all_to_all(spread, 'sub', 0, 0)]
    ppermute x4, starting transfers between devices: 13.8 us -> 19.7 us  [exchange(): lax.ppermute(face_r, 'sub', right)]
    ppermute x6, waiting for transfers between devices: 13.8 us -> 17.3 us  [on_device(): lax.ppermute(out[k - 1], 'tm', [(t, (t + 2 * k) % slices) for t in range(...]
    pallas_call x13 -> x14, Pallas kernels: 39.2 us -> 42.6 us  [call(): pl.pallas_call(kernel, name=name, out_shape=[space(shape, dtype) for shap...]
  transfers between devices with their start and end apart: 17 -> 16, of which waited for: 12 -> 12; matrix products, arithmetic and copies ran while one was open for 0% -> 0% of each run, Pallas kernels for 6% -> 8%
where the time goes in v3:
time: 177 us
  starting transfers between devices  52.9 us (30%)
  Pallas kernels  42.6 us (24%)
  blocking collectives  42.1 us (24%)
  waiting for transfers between devices  38 us (21%)
    pallas_call x14, Pallas kernels, call(): pl.pallas_call(kernel, name=name, out_shape=[space(shape, dtype) for shap...  42.6 us
    all_to_all x2, blocking collectives, on_device(): gathered = lax.all_to_all(spread, 'sub', 0, 0)  42.1 us
    ppermute x4, starting transfers between devices, exchange(): lax.ppermute(face_r, 'sub', right)  19.7 us
    ppermute x6, starting transfers between devices, on_device(): lax.ppermute(out[k - 1], 'tm', [(t, (t + 2 * k) % slices) for t in range(...  19.1 us
    ppermute x6, waiting for transfers between devices, on_device(): lax.ppermute(out[k - 1], 'tm', [(t, (t + 2 * k) % slices) for t in range(...  17.3 us
    ppermute x4, waiting for transfers between devices, exchange(): lax.ppermute(face_l, 'sub', left)  12.9 us
    ppermute x2, starting transfers between devices, swap(): return lax.ppermute(value, 'tm', [(t, t ^ 1) for t in range(slices)])  8.71 us
    ppermute x4, starting transfers between devices, exchange(): lax.ppermute(face_l, 'sub', left)  5.43 us
  transfers between devices with their start and end apart: 16, of which 12 were waited for; matrix products, arithmetic and copies ran while one was open for 0% of the time, Pallas kernels for 8%

profile of v3, /device:TPU:1, one launch (start us, length us, event | category | flops | bytes accessed | tf_op | source)
XLA Modules:
  0.0 176.6 jit_solution(3068673419176269881)
XLA Ops:
  0.6 10.1 %start.1 = (bf16[2048,2048]{1,0:T(8,128)(2,1)S(1)}, bf16[1024,1024]{1,0:T(8,128)(2,1)S(1)}, f32[1024,128]{1,0:T(8,128)S(1)}, f32[1024,128]{1,0:T(8,128)S(1)}, f3...) custom-call(bf16[2048,2048]{1,0:T(8,128)(2,1)} %bitcast.6, f32[2048,128]{1,0:T(8,128)} %bitcast.7, f32[2048,128]{1,0:T(8,128)} %bitcast.9, ...), custom_call_target="tpu_custom_call" | custom-call | flops 1073741824 | bytes 11022336 | tf_op jit(solution)/shard_map/start/pallas_call | solution.py:17
  10.7 1.3 collective-permute-start.1
  12.0 5.2 %collective-permute-start = (f32[1024,128]{1,0:T(8,128)S(1)}, f32[1024,128]{1,0:T(8,128)S(1)}, u32[]{:S(2)}, u32[]{:S(2)}) collective-permute-start(f32[1024,128]{1,0:T(8,128)S(1)} %get-tuple-element.56.y_r), channel_id=1, source_target_pairs={{0,1},{1,2},{2,3},{3,4},{4,5},{5,6},{6,7},{7,8},{8,9},{9,10},{10,1... | collective-permute-start | bytes 1572872 | tf_op jit(solution)/shard_map/ppermute | solution.py:314
  17.2 8.9 %prepare.1 = (bf16[2048,2048]{1,0:T(8,128)(2,1)S(1)}, f32[8,128]{1,0:T(8,128)S(1)}) custom-call(bf16[2048,2048]{1,0:T(8,128)(2,1)S(1)} %get-tuple-element.53.a, bf16[1024,1024]{1,0:T(8,128)(2,1)S(1)} %get-tuple-element.52.onehot), custom_call_target="tpu_custom_call" | custom-call | flops 8589934592 | bytes 10485760 | tf_op jit(solution)/shard_map/prepare/pallas_call | solution.py:17
  26.2 0.0 collective-permute-done.1.from_right
  26.2 0.0 collective-permute-done.from_left
  26.2 2.5 %first.2 = (f32[1024,128]{1,0:T(8,128)S(1)}, f32[1024,128]{1,0:T(8,128)S(1)}, f32[1024,128]{1,0:T(8,128)S(1)}, f32[1024,128]{1,0:T(8,128)S(1)}, f32[8,128]{1,0:T(8,128)S(1)}) custom-call(bf16[2048,2048]{1,0:T(8,128)(2,1)S(1)} %get-tuple-element.54.b, f32[1024,128]{1,0:T(8,128)S(1)} %get-tuple-element.55.y_l, f32[1024,128]{1,0:T(8,128)S(1)} %get-tuple-element.56.y_r, ...), custom_call_target="tpu_custom_call" | custom-call | flops 2147483648 | bytes 10489856 | tf_op jit(solution)/shard_map/first/pallas_call | solution.py:17
  28.7 1.3 collective-permute-start.3
  30.0 5.7 %collective-permute-start.2 = (f32[1024,128]{1,0:T(8,128)S(1)}, f32[1024,128]{1,0:T(8,128)S(1)}, u32[]{:S(2)}, u32[]{:S(2)}) collective-permute-start(f32[1024,128]{1,0:T(8,128)S(1)} %get-tuple-element.59.q_r), channel_id=1, source_target_pairs={{0,1},{1,2},{2,3},{3,4},{4,5},{5,6},{6,7},{7,8},{8,9},{9,10},{10,1... | collective-permute-start | bytes 1572872 | tf_op jit(solution)/shard_map/ppermute | solution.py:314
  35.7 3.9 %ready.1 = (f32[2048,128]{1,0:T(8,128)S(1)}, f32[2048,128]{1,0:T(8,128)S(1)}, f32[2048,128]{1,0:T(8,128)S(1)}, f32[2048,128]{1,0:T(8,128)S(1)}, f32[1024,128]{1,0:T(8,128)S(1)}, /*index=5*/f32[8,128]{1,0:T(8,128)S(1)}) custom-call(bf16[1024,1024]{1,0:T(8,128)(2,1)S(1)} %get-tuple-element.52.onehot, f32[2048,128]{1,0:T(8,128)S(1)} %get-tuple-element.60.force, ...), custom_call_target="tpu_custom_call" | custom-call | flops 1610612736 | bytes 6311936 | tf_op jit(solution)/shard_map/ready/pallas_call | solution.py:17
  39.6 3.9 %collective-permute-done.3.from_right = f32[1024,128]{1,0:T(8,128)S(1)} collective-permute-done((f32[1024,128]{1,0:T(8,128)S(1)}, f32[1024,128]{1,0:T(8,128)S(1)}, u32[]{:S(2)}, u32[]{:S(2)}) %collective-permute-start.3) | collective-permute-done | bytes 524320 | tf_op jit(solution)/shard_map/ppermute | solution.py:314
  43.5 0.9 collective-permute-done.2.from_left
  44.4 2.5 %second.2 = (f32[1024,128]{1,0:T(8,128)S(1)}, f32[1024,128]{1,0:T(8,128)S(1)}, f32[32,8,128]{2,1,0:T(8,128)S(1)}) custom-call(bf16[2048,2048]{1,0:T(8,128)(2,1)S(1)} %get-tuple-element.54.b, f32[1024,128]{1,0:T(8,128)S(1)} %get-tuple-element.58.q_l, f32[1024,128]{1,0:T(8,128)S(1)} %get-tuple-element.59.q_r, ...), custom_call_target="tpu_custom_call" | custom-call | flops 2147483648 | bytes 10489856 | tf_op jit(solution)/shard_map/second/pallas_call | solution.py:17
  46.9 24.4 %all_to_all.10.gathered = f32[32,8,128]{2,1,0:T(8,128)S(1)} all-to-all(f32[32,8,128]{2,1,0:T(8,128)S(1)} %get-tuple-element.64), channel_id=1, replica_groups=mesh['tm'=8,'sub'=32] {'sub'}, dimensions={0} | all-to-all | bytes 262144 | tf_op jit(solution)/shard_map/all_to_all | solution.py:369
  71.4 2.5 %next.1 = (f32[1024,128]{1,0:T(8,128)S(1)}, f32[1024,128]{1,0:T(8,128)S(1)}, f32[1024,128]{1,0:T(8,128)S(1)}, f32[1024,128]{1,0:T(8,128)S(1)}) custom-call(bf16[2048,2048]{1,0:T(8,128)(2,1)S(1)} %get-tuple-element.54.b, f32[32,8,128]{2,1,0:T(8,128)S(1)} %all_to_all.10.gathered, f32[1024,128]{1,0:T(8,128)S(1)} %get-tuple-element.55.y_l, ...), custom_call_target="tpu_custom_call" | custom-call | flops 1073741824 | bytes 14811136 | tf_op jit(solution)/shard_map/next/pallas_call | solution.py:17
  73.9 1.3 collective-permute-start.5
  75.2 4.0 %collective-permute-start.4 = (f32[1024,128]{1,0:T(8,128)S(1)}, f32[1024,128]{1,0:T(8,128)S(1)}, u32[]{:S(2)}, u32[]{:S(2)}) collective-permute-start(f32[1024,128]{1,0:T(8,128)S(1)} %get-tuple-element.72.y_r), channel_id=1, source_target_pairs={{0,1},{1,2},{2,3},{3,4},{4,5},{5,6},{6,7},{7,8},{8,9},{9,10},{10,1... | collective-permute-start | bytes 1572872 | tf_op jit(solution)/shard_map/ppermute | solution.py:314
  79.2 1.3 early.1
  80.6 4.4 %collective-permute-done.5.from_right = f32[1024,128]{1,0:T(8,128)S(1)} collective-permute-done((f32[1024,128]{1,0:T(8,128)S(1)}, f32[1024,128]{1,0:T(8,128)S(1)}, u32[]{:S(2)}, u32[]{:S(2)}) %collective-permute-start.5) | collective-permute-done | bytes 524320 | tf_op jit(solution)/shard_map/ppermute | solution.py:314
  84.9 0.9 collective-permute-done.4.from_left
  85.8 2.5 %first.3 = (f32[1024,128]{1,0:T(8,128)S(1)}, f32[1024,128]{1,0:T(8,128)S(1)}, f32[1024,128]{1,0:T(8,128)S(1)}, f32[1024,128]{1,0:T(8,128)S(1)}, f32[8,128]{1,0:T(8,128)S(1)}) custom-call(bf16[2048,2048]{1,0:T(8,128)(2,1)S(1)} %get-tuple-element.54.b, f32[1024,128]{1,0:T(8,128)S(1)} %get-tuple-element.71.y_l, f32[1024,128]{1,0:T(8,128)S(1)} %get-tuple-element.72.y_r, ...), custom_call_target="tpu_custom_call" | custom-call | flops 2147483648 | bytes 10489856 | tf_op jit(solution)/shard_map/first/pallas_call | solution.py:17
  88.3 1.6 collective-permute-start.7
  89.9 4.8 %collective-permute-start.6 = (f32[1024,128]{1,0:T(8,128)S(1)}, f32[1024,128]{1,0:T(8,128)S(1)}, u32[]{:S(2)}, u32[]{:S(2)}) collective-permute-start(f32[1024,128]{1,0:T(8,128)S(1)} %get-tuple-element.78.q_r), channel_id=1, source_target_pairs={{0,1},{1,2},{2,3},{3,4},{4,5},{5,6},{6,7},{7,8},{8,9},{9,10},{10,1... | collective-permute-start | bytes 1572872 | tf_op jit(solution)/shard_map/ppermute | solution.py:314
  94.7 4.6 %collective-permute-done.7.from_right = f32[1024,128]{1,0:T(8,128)S(1)} collective-permute-done((f32[1024,128]{1,0:T(8,128)S(1)}, f32[1024,128]{1,0:T(8,128)S(1)}, u32[]{:S(2)}, u32[]{:S(2)}) %collective-permute-start.7) | collective-permute-done | bytes 524320 | tf_op jit(solution)/shard_map/ppermute | solution.py:314
  99.3 1.5 collective-permute-done.6.from_left
  100.7 2.5 %second.3 = (f32[1024,128]{1,0:T(8,128)S(1)}, f32[1024,128]{1,0:T(8,128)S(1)}, f32[32,8,128]{2,1,0:T(8,128)S(1)}) custom-call(bf16[2048,2048]{1,0:T(8,128)(2,1)S(1)} %get-tuple-element.54.b, f32[1024,128]{1,0:T(8,128)S(1)} %get-tuple-element.77.q_l, f32[1024,128]{1,0:T(8,128)S(1)} %get-tuple-element.78.q_r, ...), custom_call_target="tpu_custom_call" | custom-call | flops 2147483648 | bytes 10489856 | tf_op jit(solution)/shard_map/second/pallas_call | solution.py:17
  103.2 17.7 %all_to_all.11.gathered = f32[32,8,128]{2,1,0:T(8,128)S(1)} all-to-all(f32[32,8,128]{2,1,0:T(8,128)S(1)} %get-tuple-element.80), channel_id=1, replica_groups=mesh['tm'=8,'sub'=32] {'sub'}, dimensions={0} | all-to-all | bytes 262144 | tf_op jit(solution)/shard_map/all_to_all | solution.py:369
  120.9 1.4 finish.1
  122.3 8.1 %collective-permute-start.8 = (f32[2,1024,128]{2,1,0:T(8,128)S(1)}, f32[2,1024,128]{2,1,0:T(8,128)S(1)}, u32[]{:S(2)}, u32[]{:S(2)}) collective-permute-start(f32[2,1024,128]{2,1,0:T(8,128)S(1)} %get-tuple-element.88), channel_id=1, source_target_pairs={{0,32},{32,0},{64,96},{96,64},{128,160},{160,128},{192,224},{224,1... | collective-permute-start | bytes 3145736 | tf_op jit(solution)/shard_map/ppermute | solution.py:381
  130.5 2.3 %collective-permute-done.8.got = f32[2,1024,128]{2,1,0:T(8,128)S(1)} collective-permute-done((f32[2,1024,128]{2,1,0:T(8,128)S(1)}, f32[2,1024,128]{2,1,0:T(8,128)S(1)}, u32[]{:S(2)}, u32[]{:S(2)}) %collective-permute-start.8) | collective-permute-done | bytes 1048608 | tf_op jit(solution)/shard_map/ppermute | solution.py:381
  132.8 0.9 combine.1
  133.7 3.2 %collective-permute-start.9 = (f32[2,256,128]{2,1,0:T(8,128)S(1)}, f32[2,256,128]{2,1,0:T(8,128)S(1)}, u32[]{:S(2)}, u32[]{:S(2)}) collective-permute-start(f32[2,256,128]{2,1,0:T(8,128)S(1)} %get-tuple-element.91), channel_id=1, source_target_pairs={{0,64},{32,96},{64,128},{96,160},{128,192},{160,224},{1,65},{33,97... | collective-permute-start | bytes 786440 | tf_op jit(solution)/shard_map/ppermute | solution.py:389
  136.9 4.5 %collective-permute-start.10 = (f32[2,256,128]{2,1,0:T(8,128)S(1)}, f32[2,256,128]{2,1,0:T(8,128)S(1)}, u32[]{:S(2)}, u32[]{:S(2)}) collective-permute-start(f32[2,256,128]{2,1,0:T(8,128)S(1)} %get-tuple-element.92), channel_id=1, source_target_pairs={{0,128},{32,160},{64,192},{96,224},{128,0},{160,32},{1,129},{33,16... | collective-permute-start | bytes 786440 | tf_op jit(solution)/shard_map/ppermute | solution.py:389
  141.4 1.9 %collective-permute-start.11 = (f32[2,256,128]{2,1,0:T(8,128)S(1)}, f32[2,256,128]{2,1,0:T(8,128)S(1)}, u32[]{:S(2)}, u32[]{:S(2)}) collective-permute-start(f32[2,256,128]{2,1,0:T(8,128)S(1)} %get-tuple-element.93), channel_id=1, source_target_pairs={{0,192},{32,224},{64,0},{96,32},{128,64},{160,96},{1,193},{33,225}... | collective-permute-start | bytes 786440 | tf_op jit(solution)/shard_map/ppermute | solution.py:389
  143.4 0.0 collective-permute-done.9.from_1
  143.4 7.8 %collective-permute-done.10.from_2 = f32[2,256,128]{2,1,0:T(8,128)S(1)} collective-permute-done((f32[2,256,128]{2,1,0:T(8,128)S(1)}, f32[2,256,128]{2,1,0:T(8,128)S(1)}, u32[]{:S(2)}, u32[]{:S(2)}) %collective-permute-start.10) | collective-permute-done | bytes 262176 | tf_op jit(solution)/shard_map/ppermute | solution.py:389
  151.2 0.7 collective-permute-done.11.from_3
  151.9 0.5 prefix.1
  152.4 1.3 collective-permute-start.12
  153.7 6.8 %collective-permute-start.13 = (f32[2,256,128]{2,1,0:T(8,128)S(1)}, f32[2,256,128]{2,1,0:T(8,128)S(1)}, u32[]{:S(2)}, u32[]{:S(2)}) collective-permute-start(f32[2,256,128]{2,1,0:T(8,128)S(1)} %get-tuple-element.96), channel_id=1, source_target_pairs={{0,128},{32,160},{64,192},{96,224},{192,64},{224,96},{1,129},{33,1... | collective-permute-start | bytes 786440 | tf_op jit(solution)/shard_map/ppermute | solution.py:400
  160.6 1.3 collective-permute-start.14
  161.9 0.0 collective-permute-done.12.from_1
  161.9 3.5 %collective-permute-done.13.from_2 = f32[2,256,128]{2,1,0:T(8,128)S(1)} collective-permute-done((f32[2,256,128]{2,1,0:T(8,128)S(1)}, f32[2,256,128]{2,1,0:T(8,128)S(1)}, u32[]{:S(2)}, u32[]{:S(2)}) %collective-permute-start.13) | collective-permute-done | bytes 262176 | tf_op jit(solution)/shard_map/ppermute | solution.py:400
  165.4 5.3 %collective-permute-done.14.from_3 = f32[2,256,128]{2,1,0:T(8,128)S(1)} collective-permute-done((f32[2,256,128]{2,1,0:T(8,128)S(1)}, f32[2,256,128]{2,1,0:T(8,128)S(1)}, u32[]{:S(2)}, u32[]{:S(2)}) %collective-permute-start.14) | collective-permute-done | bytes 262176 | tf_op jit(solution)/shard_map/ppermute | solution.py:400
  170.7 1.5 end.1
  172.2 0.6 collective-permute-start.15
  172.7 2.3 %collective-permute-done.15.got = f32[2,1024,128]{2,1,0:T(8,128)S(1)} collective-permute-done((f32[2,1024,128]{2,1,0:T(8,128)S(1)}, f32[2,1024,128]{2,1,0:T(8,128)S(1)}, u32[]{:S(2)}, u32[]{:S(2)}) %collective-permute-start.15) | collective-permute-done | bytes 1048608 | tf_op jit(solution)/shard_map/ppermute | solution.py:381
  175.0 1.5 join.1
Async XLA Ops:
  10.7 15.4 %collective-permute-start.1 = (f32[1024,128]{1,0:T(8,128)S(1)}, f32[1024,128]{1,0:T(8,128)S(1)}, u32[]{:S(2)}, u32[]{:S(2)}) collective-permute-start(f32[1024,128]{1,0:T(8,128)S(1)} %get-tuple-element.55.y_l), channel_id=1, source_target_pairs={{1,0},{2,1},{3,2},{4,3},{5,4},{6,5},{7,6},{8,7},{9,8},{10,9},{11,1... | collective-permute-start | bytes 1572872 | tf_op jit(solution)/shard_map/ppermute | solution.py:314
  12.0 14.2 %collective-permute-start = (f32[1024,128]{1,0:T(8,128)S(1)}, f32[1024,128]{1,0:T(8,128)S(1)}, u32[]{:S(2)}, u32[]{:S(2)}) collective-permute-start(f32[1024,128]{1,0:T(8,128)S(1)} %get-tuple-element.56.y_r), channel_id=1, source_target_pairs={{0,1},{1,2},{2,3},{3,4},{4,5},{5,6},{6,7},{7,8},{8,9},{9,10},{10,1... | collective-permute-start | bytes 1572872 | tf_op jit(solution)/shard_map/ppermute | solution.py:314
  28.7 14.9 %collective-permute-start.3 = (f32[1024,128]{1,0:T(8,128)S(1)}, f32[1024,128]{1,0:T(8,128)S(1)}, u32[]{:S(2)}, u32[]{:S(2)}) collective-permute-start(f32[1024,128]{1,0:T(8,128)S(1)} %get-tuple-element.58.q_l), channel_id=1, source_target_pairs={{1,0},{2,1},{3,2},{4,3},{5,4},{6,5},{7,6},{8,7},{9,8},{10,9},{11,1... | collective-permute-start | bytes 1572872 | tf_op jit(solution)/shard_map/ppermute | solution.py:314
  30.0 14.5 %collective-permute-start.2 = (f32[1024,128]{1,0:T(8,128)S(1)}, f32[1024,128]{1,0:T(8,128)S(1)}, u32[]{:S(2)}, u32[]{:S(2)}) collective-permute-start(f32[1024,128]{1,0:T(8,128)S(1)} %get-tuple-element.59.q_r), channel_id=1, source_target_pairs={{0,1},{1,2},{2,3},{3,4},{4,5},{5,6},{6,7},{7,8},{8,9},{9,10},{10,1... | collective-permute-start | bytes 1572872 | tf_op jit(solution)/shard_map/ppermute | solution.py:314
  73.9 11.0 %collective-permute-start.5 = (f32[1024,128]{1,0:T(8,128)S(1)}, f32[1024,128]{1,0:T(8,128)S(1)}, u32[]{:S(2)}, u32[]{:S(2)}) collective-permute-start(f32[1024,128]{1,0:T(8,128)S(1)} %get-tuple-element.71.y_l), channel_id=1, source_target_pairs={{1,0},{2,1},{3,2},{4,3},{5,4},{6,5},{7,6},{8,7},{9,8},{10,9},{11,1... | collective-permute-start | bytes 1572872 | tf_op jit(solution)/shard_map/ppermute | solution.py:314
  75.2 10.6 %collective-permute-start.4 = (f32[1024,128]{1,0:T(8,128)S(1)}, f32[1024,128]{1,0:T(8,128)S(1)}, u32[]{:S(2)}, u32[]{:S(2)}) collective-permute-start(f32[1024,128]{1,0:T(8,128)S(1)} %get-tuple-element.72.y_r), channel_id=1, source_target_pairs={{0,1},{1,2},{2,3},{3,4},{4,5},{5,6},{6,7},{7,8},{8,9},{9,10},{10,1... | collective-permute-start | bytes 1572872 | tf_op jit(solution)/shard_map/ppermute | solution.py:314
  88.3 10.9 %collective-permute-start.7 = (f32[1024,128]{1,0:T(8,128)S(1)}, f32[1024,128]{1,0:T(8,128)S(1)}, u32[]{:S(2)}, u32[]{:S(2)}) collective-permute-start(f32[1024,128]{1,0:T(8,128)S(1)} %get-tuple-element.77.q_l), channel_id=1, source_target_pairs={{1,0},{2,1},{3,2},{4,3},{5,4},{6,5},{7,6},{8,7},{9,8},{10,9},{11,1... | collective-permute-start | bytes 1572872 | tf_op jit(solution)/shard_map/ppermute | solution.py:314
  89.9 10.8 %collective-permute-start.6 = (f32[1024,128]{1,0:T(8,128)S(1)}, f32[1024,128]{1,0:T(8,128)S(1)}, u32[]{:S(2)}, u32[]{:S(2)}) collective-permute-start(f32[1024,128]{1,0:T(8,128)S(1)} %get-tuple-element.78.q_r), channel_id=1, source_target_pairs={{0,1},{1,2},{2,3},{3,4},{4,5},{5,6},{6,7},{7,8},{8,9},{9,10},{10,1... | collective-permute-start | bytes 1572872 | tf_op jit(solution)/shard_map/ppermute | solution.py:314
  122.3 10.4 %collective-permute-start.8 = (f32[2,1024,128]{2,1,0:T(8,128)S(1)}, f32[2,1024,128]{2,1,0:T(8,128)S(1)}, u32[]{:S(2)}, u32[]{:S(2)}) collective-permute-start(f32[2,1024,128]{2,1,0:T(8,128)S(1)} %get-tuple-element.88), channel_id=1, source_target_pairs={{0,32},{32,0},{64,96},{96,64},{128,160},{160,128},{192,224},{224,1... | collective-permute-start | bytes 3145736 | tf_op jit(solution)/shard_map/ppermute | solution.py:381
  133.7 9.7 %collective-permute-start.9 = (f32[2,256,128]{2,1,0:T(8,128)S(1)}, f32[2,256,128]{2,1,0:T(8,128)S(1)}, u32[]{:S(2)}, u32[]{:S(2)}) collective-permute-start(f32[2,256,128]{2,1,0:T(8,128)S(1)} %get-tuple-element.91), channel_id=1, source_target_pairs={{0,64},{32,96},{64,128},{96,160},{128,192},{160,224},{1,65},{33,97... | collective-permute-start | bytes 786440 | tf_op jit(solution)/shard_map/ppermute | solution.py:389
  136.9 14.3 %collective-permute-start.10 = (f32[2,256,128]{2,1,0:T(8,128)S(1)}, f32[2,256,128]{2,1,0:T(8,128)S(1)}, u32[]{:S(2)}, u32[]{:S(2)}) collective-permute-start(f32[2,256,128]{2,1,0:T(8,128)S(1)} %get-tuple-element.92), channel_id=1, source_target_pairs={{0,128},{32,160},{64,192},{96,224},{128,0},{160,32},{1,129},{33,16... | collective-permute-start | bytes 786440 | tf_op jit(solution)/shard_map/ppermute | solution.py:389
  141.4 10.4 %collective-permute-start.11 = (f32[2,256,128]{2,1,0:T(8,128)S(1)}, f32[2,256,128]{2,1,0:T(8,128)S(1)}, u32[]{:S(2)}, u32[]{:S(2)}) collective-permute-start(f32[2,256,128]{2,1,0:T(8,128)S(1)} %get-tuple-element.93), channel_id=1, source_target_pairs={{0,192},{32,224},{64,0},{96,32},{128,64},{160,96},{1,193},{33,225}... | collective-permute-start | bytes 786440 | tf_op jit(solution)/shard_map/ppermute | solution.py:389
  152.4 9.4 %collective-permute-start.12 = (f32[2,256,128]{2,1,0:T(8,128)S(1)}, f32[2,256,128]{2,1,0:T(8,128)S(1)}, u32[]{:S(2)}, u32[]{:S(2)}) collective-permute-start(f32[2,256,128]{2,1,0:T(8,128)S(1)} %get-tuple-element.95), channel_id=1, source_target_pairs={{0,64},{32,96},{64,128},{96,160},{128,192},{160,224},{1,65},{33,97... | collective-permute-start | bytes 786440 | tf_op jit(solution)/shard_map/ppermute | solution.py:400
  153.7 11.6 %collective-permute-start.13 = (f32[2,256,128]{2,1,0:T(8,128)S(1)}, f32[2,256,128]{2,1,0:T(8,128)S(1)}, u32[]{:S(2)}, u32[]{:S(2)}) collective-permute-start(f32[2,256,128]{2,1,0:T(8,128)S(1)} %get-tuple-element.96), channel_id=1, source_target_pairs={{0,128},{32,160},{64,192},{96,224},{192,64},{224,96},{1,129},{33,1... | collective-permute-start | bytes 786440 | tf_op jit(solution)/shard_map/ppermute | solution.py:400
  160.6 10.1 %collective-permute-start.14 = (f32[2,256,128]{2,1,0:T(8,128)S(1)}, f32[2,256,128]{2,1,0:T(8,128)S(1)}, u32[]{:S(2)}, u32[]{:S(2)}) collective-permute-start(f32[2,256,128]{2,1,0:T(8,128)S(1)} %get-tuple-element.97), channel_id=1, source_target_pairs={{0,192},{32,224},{128,64},{160,96},{192,128},{224,160},{1,193},{33... | collective-permute-start | bytes 786440 | tf_op jit(solution)/shard_map/ppermute | solution.py:400
  172.2 2.9 %collective-permute-start.15 = (f32[2,1024,128]{2,1,0:T(8,128)S(1)}, f32[2,1024,128]{2,1,0:T(8,128)S(1)}, u32[]{:S(2)}, u32[]{:S(2)}) collective-permute-start(f32[2,1024,128]{2,1,0:T(8,128)S(1)} %get-tuple-element.99), channel_id=1, source_target_pairs={{0,32},{32,0},{64,96},{96,64},{128,160},{160,128},{192,224},{224,1... | collective-permute-start | bytes 3145736 | tf_op jit(solution)/shard_map/ppermute | solution.py:381

commit v4 on v3

v4 whole, which is shorter than its diff:
```python
import jax
import jax.numpy as jnp
from jax import lax
from jax.experimental import pallas as pl
from jax.experimental.pallas import tpu as pltpu
from jax.sharding import PartitionSpec as P

F32 = jnp.float32
BF16 = jnp.bfloat16
VMEM = pl.BlockSpec(memory_space=pltpu.VMEM)
HBM = pl.BlockSpec(memory_space=pltpu.HBM)
CHUNKS = 4


def call(kernel, name, outs, args, flops=0, in_specs=None, scratch=(), limit=12, space=pltpu.VMEM):
    moved = sum(a.size * a.dtype.itemsize for a in args)
    return pl.pallas_call(
        kernel,
        name=name,
        out_shape=[space(shape, dtype) for shape, dtype in outs],
        in_specs=in_specs or [VMEM] * len(args),
        out_specs=[VMEM] * len(outs),
        scratch_shapes=scratch,
        compiler_params=pltpu.CompilerParams(vmem_limit_bytes=limit * 2**20),
        cost_estimate=pl.CostEstimate(flops=flops, bytes_accessed=moved, transcendentals=0),
    )(*args)


def pair(value):
    high = value.astype(BF16)
    return jnp.concatenate([high, (value - high.astype(F32)).astype(BF16)], axis=1)


def triple(value):
    high = value.astype(BF16)
    rest = value - high.astype(F32)
    middle = rest.astype(BF16)
    low = (rest - middle.astype(F32)).astype(BF16)
    return jnp.concatenate([high, middle, low], axis=1)


def fold(wide):
    return wide[:, :128] + wide[:, 128:256] + wide[:, 256:]


def to_multipliers(onehot, face):
    return fold(jnp.dot(onehot, triple(face), preferred_element_type=F32))


def to_left(onehot, block):
    return fold(lax.dot_general(onehot, triple(block), (((0,), (0,)), ((), ())), preferred_element_type=F32))


def column(row):
    width = row.shape[1]
    pieces = [jnp.transpose(jnp.broadcast_to(row[:, k : k + 128], (128, 128))) for k in range(0, width, 128)]
    return jnp.concatenate(pieces, axis=0)


def add_up(value):
    return jnp.sum(value, axis=0, keepdims=True)


def is_even():
    return lax.rem(lax.axis_index("sub"), 2) == 0


def by_pairs(left, right):
    even = is_even()
    return jnp.where(even, right, left), jnp.where(even, left, right)


def by_sides(face_a, face_b):
    even = is_even()
    return jnp.where(even, face_b, face_a), jnp.where(even, face_a, face_b)


def start_kernel(
    a_in, u_in, v_in, load_in, mass_in, perm_in, a, onehot, y_a, y_b, base, force, u, v, load, mass, perm, fields_sem, a_sem
):
    size = a.shape[0]
    half, rows = size // 2, size // CHUNKS
    small = [
        pltpu.make_async_copy(source, target, fields_sem.at[k])
        for k, (source, target) in enumerate(
            [(perm_in, perm), (mass_in, mass), (u_in, u), (v_in, v), (load_in, load)]
        )
    ]
    big = [
        pltpu.make_async_copy(a_in.at[pl.ds(k * rows, rows)], a.at[pl.ds(k * rows, rows)], a_sem.at[k])
        for k in range(CHUNKS)
    ]
    for copy in small:
        copy.start()
    small[0].wait()
    onehot[...] = (lax.broadcasted_iota(jnp.int32, (half, half), 0) == perm[...]).astype(F32).astype(BF16)
    for copy in small[1:]:
        copy.wait()
    for copy in big:
        copy.start()
    weight = 2.0 * column(mass[...])
    outer = load[...].astype(F32)
    rhs = (outer + weight * (u[...] + v[...])).astype(BF16)
    before = 2.0 * u[...] + v[...]
    base[...] = before
    force[...] = outer - weight * before
    faces = []
    for first in (0, CHUNKS // 2):
        parts = []
        for k in range(first, first + CHUNKS // 2):
            big[k].wait()
            parts.append(jnp.dot(a[k * rows : (k + 1) * rows], rhs, preferred_element_type=F32))
        faces.append(jnp.concatenate(parts, axis=0))
        if first == 0:
            faces[0] = to_multipliers(onehot[...], faces[0])
    y_a[...], y_b[...] = by_pairs(*faces)


def prepare_kernel(a, onehot, b, order, turned):
    order[...] = jnp.zeros(order.shape, F32)
    size = a.shape[0]
    half, rows = size // 2, size // CHUNKS
    hot = onehot[...]
    odd = lax.rem(lax.axis_index("sub"), 2)

    def left(offset, count):
        return pl.ds(pl.multiple_of((1 - odd) * half + offset, rows), count)

    def right(offset, count):
        return pl.ds(pl.multiple_of(odd * half + offset, rows), count)

    for k in range(CHUNKS):
        here = slice(k * rows, (k + 1) * rows)
        block = lax.dot_general(a[here, :half], hot, (((1,), (1,)), ((), ())), preferred_element_type=F32).astype(BF16)
        if k < CHUNKS // 2:
            turned[here] = block
        else:
            down = right(k * rows - half, rows)
            b[down, left(0, half)] = block
            b[down, right(0, half)] = a[here, half:]
    for k in range(CHUNKS):
        here = slice(k * rows, (k + 1) * rows)
        if k < CHUNKS // 2:
            block, across = turned[:, here], left(k * rows, rows)
        else:
            block, across = a[:half, here], right(k * rows - half, rows)
        b[left(0, half), across] = jnp.dot(hot, block, preferred_element_type=F32).astype(BF16)


def ready_kernel(onehot, force, mass_in, rate_in, u_in, v_in, base, sums_in, force_m, weight_m, early_u, early_v, rate_own, sums, mass, rate, u, v, sem):
    copies = [
        pltpu.make_async_copy(source, target, sem.at[k]) for k, (source, target) in enumerate([(mass_in, mass), (rate_in, rate), (u_in, u), (v_in, v)])
    ]
    for copy in copies:
        copy.start()
    sums[...] = sums_in[...]
    hot = onehot[...]
    half = hot.shape[0]
    copies[0].wait()
    weight = 6.0 * column(mass[...])
    force_m[:half], force_m[half:] = by_pairs(to_multipliers(hot, force[:half]), force[half:])
    weight_m[:half], weight_m[half:] = by_pairs(to_multipliers(hot, weight[:half]), weight[half:])
    for copy in copies[1:]:
        copy.wait()
    tm = lax.axis_index("tm")
    rates = column(rate[...])
    rate_own[...] = jnp.where(tm % 2 == 0, rates[:half], rates[half:])
    same, up, down = coarse(rates)
    early_u[...] = -jnp.where(tm == 0, 0.0, same * u[...] + up * v[...])
    early_v[...] = base[...] - jnp.where(tm == 0, 0.0, down * u[...] + same * v[...])


def jump(f_a, f_b, from_a, from_b):
    sub = lax.axis_index("sub")
    alone = jnp.logical_or(sub == 0, sub == lax.axis_size("sub") - 1)
    return f_a[...] - from_a[...], jnp.where(alone, 0.0, f_b[...] - from_b[...])


def first_kernel(b, y_a, y_b, from_a, from_b, order, q_a, q_b, t_a, t_b, sums):
    half = y_a.shape[0]
    r_a, r_b = jump(y_a, y_b, from_a, from_b)
    z = jnp.concatenate([pair(r_a), pair(r_b)], axis=0)
    wide = jnp.dot(b[...], z, preferred_element_type=F32)
    q = wide[:, :128]
    t = q + wide[:, 128:]
    q_a[...], q_b[...] = q[:half], q[half:]
    t_a[...], t_b[...] = t[:half], t[half:]
    rr = 0.5 * (add_up(r_a * r_a) + add_up(r_b * r_b))
    pw = add_up(r_a * q[:half]) + add_up(r_b * q[half:])
    sums[...] = jnp.concatenate([rr, pw, order[2:]], axis=0)


def second_kernel(b, q_a, q_b, from_a, from_b, sums, s_a, s_b, spread):
    half = q_a.shape[0]
    w_a, w_b = jump(q_a, q_b, from_a, from_b)
    z = jnp.concatenate([pair(w_a), pair(w_b)], axis=0)
    wide = jnp.dot(b[...], z, preferred_element_type=F32)
    s = wide[:, :128] + wide[:, 128:]
    s_a[...], s_b[...] = s[:half], s[half:]
    ww = 0.5 * (add_up(w_a * w_a) + add_up(w_b * w_b))
    wfw = add_up(w_a * s[:half]) + add_up(w_b * s[half:])
    own = jnp.concatenate([sums[:2], ww, wfw, jnp.zeros((4, 128), F32)], axis=0)
    spread[...] = jnp.broadcast_to(own[None], spread.shape)


def corrected(gathered, y_a, y_b, q_a, q_b, t_a, t_b, s_a, s_b):
    total = jnp.sum(gathered[...], axis=0)
    rr, pw, ww, wfw = total[0:1], total[1:2], total[2:3], total[3:4]
    alpha = rr / pw
    ratio = ww / pw
    later = (alpha * alpha * ww - rr) / (alpha * alpha * (wfw - ww * ratio))
    gain = alpha * later

    def face(y, q, t, s):
        return y[...] - alpha * q[...] - gain * (ratio * t[...] - s[...])

    return face(y_a, q_a, t_a, s_a), face(y_b, q_b, t_b, s_b)


def next_kernel(b, gathered, y_a, y_b, q_a, q_b, t_a, t_b, s_a, s_b, force_m, weight_m, z_a, z_b, u_a, u_b):
    half = y_a.shape[0]
    new_a, new_b = corrected(gathered, y_a, y_b, q_a, q_b, t_a, t_b, s_a, s_b)
    u_a[...], u_b[...] = new_a, new_b
    rhs = (force_m[...] + weight_m[...] * jnp.concatenate([new_a, new_b], axis=0)).astype(BF16)
    y = jnp.dot(b[...], rhs, preferred_element_type=F32)
    z_a[...], z_b[...] = y[:half], y[half:]


def coarse(rate):
    scale = 1.0 / (1.0 + rate)
    return (1.0 - rate) * scale, 2.0 * scale, -2.0 * rate * scale


def early_kernel(onehot, u_a, u_b, early_in, early_v, order):
    order[...] = jnp.zeros(order.shape, F32)
    half = u_a.shape[0]
    left, right = by_sides(u_a[...], u_b[...])
    early_v[:half] = early_in[:half] - 4.0 * to_left(onehot[...], left)
    early_v[half:] = early_in[half:] - 4.0 * right


def finish_kernel(onehot, gathered, y_a, y_b, q_a, q_b, t_a, t_b, s_a, s_b, early_u, early_v, own, give):
    even = lax.axis_index("tm") % 2 == 0
    half = y_a.shape[0]
    left, right = by_sides(*corrected(gathered, y_a, y_b, q_a, q_b, t_a, t_b, s_a, s_b))
    left = to_left(onehot[...], left)
    for k, (early, factor) in enumerate([(early_u, 1.0), (early_v, 2.0)]):
        top = factor * left + early[:half]
        bottom = factor * right + early[half:]
        own[k] = jnp.where(even, top, bottom)
        give[k] = jnp.where(even, bottom, top)


def step_on(rate, state_u, state_v):
    same, up, down = coarse(rate)
    return same * state_u + up * state_v, down * state_u + same * state_v


def both_slices(own, got):
    even = lax.axis_index("tm") % 2 == 0
    return [jnp.where(even, own[k], got[k]) for k in range(2)], [jnp.where(even, got[k], own[k]) for k in range(2)]


def combine_kernel(own, got, rate_own, blocks):
    rows = blocks.shape[2]
    first, second = both_slices(own, got)
    moved = step_on(rate_own[...], *first)
    for k in range(2):
        both = second[k] + moved[k]
        for place in range(blocks.shape[0]):
            blocks[place, k] = both[place * rows : (place + 1) * rows]


def prefix_kernel(blocks, rate_own, states):
    rows = blocks.shape[2]
    chip = lax.axis_index("tm") // 2
    rate = rate_own[pl.ds(pl.multiple_of(chip * rows, rows), rows)]
    states[0] = jnp.zeros(states.shape[1:], F32)
    state = [blocks[0, k] for k in range(2)]
    for place in range(1, blocks.shape[0]):
        for k in range(2):
            states[place, k] = state[k]
        if place + 1 < blocks.shape[0]:
            moved = step_on(rate, *step_on(rate, *state))
            state = [blocks[place, k] + moved[k] for k in range(2)]


def end_kernel(states, own, got, rate_own, stay, give):
    even = lax.axis_index("tm") % 2 == 0
    first, second = both_slices(own, got)
    rate = rate_own[...]
    entering = [jnp.concatenate([states[place, k] for place in range(states.shape[0])], axis=0) for k in range(2)]
    moved = step_on(rate, *entering)
    first = [first[k] + moved[k] for k in range(2)]
    moved = step_on(rate, *first)
    second = [second[k] + moved[k] for k in range(2)]
    for k in range(2):
        stay[k] = jnp.where(even, first[k], second[k])
        give[k] = jnp.where(even, second[k], first[k])


def join_kernel(stay, got, end_u, end_v):
    even = lax.axis_index("tm") % 2 == 0
    half = stay.shape[1]
    for k, out in enumerate([end_u, end_v]):
        out[:half] = jnp.where(even, stay[k], got[k])
        out[half:] = jnp.where(even, got[k], stay[k])


def on_device(flex, mass, coarse_rate, face_perm, start_u, start_v, load):
    size, cases = start_u.shape[2:]
    half = size // 2
    subs, slices = lax.axis_size("sub"), lax.axis_size("tm")
    flex, mass, coarse_rate, face_perm, u, v, outer = [
        pltpu.with_memory_space_constraint(value, pltpu.HBM)
        for value in (flex[0], mass, coarse_rate, face_perm, start_u[0, 0], start_v[0, 0], load[0, 0])
    ]
    pairs = [[p for s in range(k, subs - 1, 2) for p in ((s, s + 1), (s + 1, s))] for k in range(2)]
    face = ((half, cases), F32)
    whole = ((size, cases), F32)
    small = ((8, cases), F32)
    square = ((size, size), BF16)
    once = 2 * size * size * cases

    def exchange(face_a, face_b):
        from_b = lax.ppermute(face_b, "sub", pairs[1])
        return lax.ppermute(face_a, "sub", pairs[0]), from_b

    a, onehot, y_a, y_b, base, force = call(
        start_kernel,
        "start",
        [square, ((half, half), BF16), face, face, whole, whole],
        (flex, u, v, outer, mass, face_perm),
        once,
        in_specs=[HBM] * 6,
        scratch=[
            pltpu.VMEM((size, cases), F32),
            pltpu.VMEM((size, cases), F32),
            pltpu.VMEM((size, cases), BF16),
            pltpu.VMEM((1, size), F32),
            pltpu.VMEM((1, half), jnp.int32),
            pltpu.SemaphoreType.DMA((5,)),
            pltpu.SemaphoreType.DMA((CHUNKS,)),
        ],
    )
    matrix = None
    for step in range(2):
        from_a, from_b = exchange(y_a, y_b)
        if step == 0:
            matrix, order = call(
                prepare_kernel, "prepare", [square, small], (a, onehot), 8 * half**3, scratch=[pltpu.VMEM((half, half), BF16)]
            )
        else:
            early_v, order = call(early_kernel, "early", [whole, small], (onehot, u_a, u_b, early_v), 2 * half * half * 3 * cases)
        q_a, q_b, t_a, t_b, sums = call(
            first_kernel, "first", [face] * 4 + [small], (matrix, y_a, y_b, from_a, from_b, order), 2 * once
        )
        from_a, from_b = exchange(q_a, q_b)
        if step == 0:
            force_m, weight_m, early_u, early_v, rate_own, sums = call(
                ready_kernel,
                "ready",
                [whole] * 4 + [face, small],
                (onehot, force, mass, coarse_rate, u, v, base, sums),
                2 * half * half * 6 * cases,
                in_specs=[VMEM] * 2 + [HBM] * 4 + [VMEM] * 2,
                scratch=[
                    pltpu.VMEM((1, size), F32),
                    pltpu.VMEM((1, size), F32),
                    pltpu.VMEM((size, cases), F32),
                    pltpu.VMEM((size, cases), F32),
                    pltpu.SemaphoreType.DMA((4,)),
                ],
            )
        s_a, s_b, spread = call(
            second_kernel,
            "second",
            [face] * 2 + [((subs, 8, cases), F32)],
            (matrix, q_a, q_b, from_a, from_b, sums),
            2 * once,
        )
        gathered = lax.all_to_all(spread, "sub", 0, 0)
        fields = (gathered, y_a, y_b, q_a, q_b, t_a, t_b, s_a, s_b)
        if step == 0:
            y_a, y_b, u_a, u_b = call(next_kernel, "next", [face] * 4, (matrix,) + fields + (force_m, weight_m), once)

    chips = slices // 2
    rows = half // chips
    two = ((2, half, cases), F32)
    blocks = ((chips, 2, rows, cases), F32)
    groups = [list(range(core, slices, 2)) for core in range(2)]
    light = size * cases * 10

    def swap(value):
        return lax.ppermute(value, "tm", [(t, t ^ 1) for t in range(slices)])

    own, give = call(finish_kernel, "finish", [two, two], (onehot,) + fields + (early_u, early_v), light)
    got = swap(give)
    (parts,) = call(combine_kernel, "combine", [blocks], (own, got, rate_own), light)
    parts = lax.all_to_all(parts, "tm", 0, 0, axis_index_groups=groups)
    (states,) = call(prefix_kernel, "prefix", [blocks], (parts, rate_own), light)
    states = lax.all_to_all(states, "tm", 0, 0, axis_index_groups=groups)
    stay, give = call(end_kernel, "end", [two, two], (states, own, got, rate_own), light)
    end_u, end_v = call(join_kernel, "join", [whole, whole], (stay, swap(give)), light, space=jax.ShapeDtypeStruct)
    return end_u[None, None], end_v[None, None]


def solution(mesh):
    return jax.shard_map(
        on_device,
        mesh=mesh,
        in_specs=(
            P("sub", None, None),
            P("sub", None),
            P("sub", None),
            P("sub", None),
            P("tm", "sub", None, None),
            P("tm", "sub", None, None),
            P("tm", "sub", None, None),
        ),
        out_specs=(P("tm", "sub", None, None), P("tm", "sub", None, None)),
        check_vma=False,
    )
```

time: 177 us -> 167 us (0.944)
  blocking collectives: 42.1 us -> 75.9 us
  starting transfers between devices: 52.9 us -> 26.7 us
  waiting for transfers between devices: 38 us -> 23 us
  Pallas kernels: 42.6 us -> 40.4 us
    all_to_all x0 -> x2, blocking collectives: none -> 34 us  [the longest x1 18.2 us: on_device(): parts = lax.all_to_all(parts, 'tm', 0, 0, axis_index_groups=groups)]
    ppermute x14 -> x8, starting transfers between devices: 44.2 us -> 16 us  [the longest x4 12.6 us: exchange(): return (lax.ppermute(face_a, 'sub', pairs[0]), from_b)]
    ppermute x14 -> x8, waiting for transfers between devices: 33.5 us -> 18.5 us  [the longest x4 18.5 us: exchange(): return (lax.ppermute(face_a, 'sub', pairs[0]), from_b)]
    pallas_call x14, Pallas kernels: 42.6 us -> 40.4 us  [call(): pl.pallas_call(kernel, name=name, out_shape=[space(shape, dtype) for shap...]
    ppermute x2, starting transfers between devices: 8.71 us -> 10.7 us  [swap(): return lax.ppermute(value, 'tm', [(t, t ^ 1) for t in range(slices)])]
  transfers between devices with their start and end apart: 16 -> 10, of which waited for: 12 -> 6; matrix products, arithmetic and copies ran while one was open for 0% -> 0% of each run, Pallas kernels for 8% -> 9%
where the time goes in v4:
time: 167 us
  blocking collectives  75.9 us (45%)
  Pallas kernels  40.4 us (24%)
  starting transfers between devices  26.7 us (16%)
  waiting for transfers between devices  23 us (14%)
    all_to_all x2, blocking collectives, on_device(): gathered = lax.all_to_all(spread, 'sub', 0, 0)  42 us
    pallas_call x14, Pallas kernels, call(): pl.pallas_call(kernel, name=name, out_shape=[space(shape, dtype) for shap...  40.4 us
    ppermute x4, waiting for transfers between devices, exchange(): return (lax.ppermute(face_a, 'sub', pairs[0]), from_b)  18.5 us
    all_to_all x1, blocking collectives, on_device(): parts = lax.all_to_all(parts, 'tm', 0, 0, axis_index_groups=groups)  18.2 us
    all_to_all x1, blocking collectives, on_device(): states = lax.all_to_all(states, 'tm', 0, 0, axis_index_groups=groups)  15.7 us
    ppermute x4, starting transfers between devices, exchange(): return (lax.ppermute(face_a, 'sub', pairs[0]), from_b)  12.6 us
    ppermute x2, starting transfers between devices, swap(): return lax.ppermute(value, 'tm', [(t, t ^ 1) for t in range(slices)])  10.7 us
    ppermute x2, waiting for transfers between devices, swap(): return lax.ppermute(value, 'tm', [(t, t ^ 1) for t in range(slices)])  4.57 us
  transfers between devices with their start and end apart: 10, of which 6 were waited for; matrix products, arithmetic and copies ran while one was open for 0% of the time, Pallas kernels for 9%

profile of v4, /device:TPU:1, one launch (start us, length us, event | category | flops | bytes accessed | tf_op | source)
XLA Modules:
  0.0 166.8 jit_solution(16577881659052198441)
XLA Ops:
  0.6 9.4 %start.1 = (bf16[2048,2048]{1,0:T(8,128)(2,1)S(1)}, bf16[1024,1024]{1,0:T(8,128)(2,1)S(1)}, f32[1024,128]{1,0:T(8,128)S(1)}, f32[1024,128]{1,0:T(8,128)S(1)}, f3...) custom-call(bf16[2048,2048]{1,0:T(8,128)(2,1)} %bitcast.6, f32[2048,128]{1,0:T(8,128)} %bitcast.7, f32[2048,128]{1,0:T(8,128)} %bitcast.9, ...), custom_call_target="tpu_custom_call" | custom-call | flops 1073741824 | bytes 11022336 | tf_op jit(solution)/shard_map/start/pallas_call | solution.py:17
  10.1 2.6 %collective-permute-start = (f32[1024,128]{1,0:T(8,128)S(1)}, f32[1024,128]{1,0:T(8,128)S(1)}, u32[]{:S(2)}, u32[]{:S(2)}) collective-permute-start(f32[1024,128]{1,0:T(8,128)S(1)} %get-tuple-element.47.y_a), channel_id=1, source_target_pairs={{0,1},{1,0},{2,3},{3,2},{4,5},{5,4},{6,7},{7,6},{8,9},{9,8},{10,11... | collective-permute-start | bytes 1572872 | tf_op jit(solution)/shard_map/ppermute | solution.py:327
  12.6 0.9 collective-permute-start.1
  13.5 9.0 %prepare.1 = (bf16[2048,2048]{1,0:T(8,128)(2,1)S(1)}, f32[8,128]{1,0:T(8,128)S(1)}) custom-call(bf16[2048,2048]{1,0:T(8,128)(2,1)S(1)} %get-tuple-element.45.a, bf16[1024,1024]{1,0:T(8,128)(2,1)S(1)} %get-tuple-element.44.onehot), custom_call_target="tpu_custom_call" | custom-call | flops 8589934592 | bytes 10485760 | tf_op jit(solution)/shard_map/prepare/pallas_call | solution.py:17
  22.5 0.7 collective-permute-done.from_a
  23.2 0.0 collective-permute-done.1.from_b
  23.2 2.5 %first.2 = (f32[1024,128]{1,0:T(8,128)S(1)}, f32[1024,128]{1,0:T(8,128)S(1)}, f32[1024,128]{1,0:T(8,128)S(1)}, f32[1024,128]{1,0:T(8,128)S(1)}, f32[8,128]{1,0:T(8,128)S(1)}) custom-call(bf16[2048,2048]{1,0:T(8,128)(2,1)S(1)} %get-tuple-element.46.b, f32[1024,128]{1,0:T(8,128)S(1)} %get-tuple-element.47.y_a, f32[1024,128]{1,0:T(8,128)S(1)} %get-tuple-element.48.y_b, ...), custom_call_target="tpu_custom_call" | custom-call | flops 2147483648 | bytes 10489856 | tf_op jit(solution)/shard_map/first/pallas_call | solution.py:17
  25.7 6.0 %collective-permute-start.2 = (f32[1024,128]{1,0:T(8,128)S(1)}, f32[1024,128]{1,0:T(8,128)S(1)}, u32[]{:S(2)}, u32[]{:S(2)}) collective-permute-start(f32[1024,128]{1,0:T(8,128)S(1)} %get-tuple-element.50.q_a), channel_id=1, source_target_pairs={{0,1},{1,0},{2,3},{3,2},{4,5},{5,4},{6,7},{7,6},{8,9},{9,8},{10,11... | collective-permute-start | bytes 1572872 | tf_op jit(solution)/shard_map/ppermute | solution.py:327
  31.7 0.9 collective-permute-start.3
  32.6 3.8 %ready.1 = (f32[2048,128]{1,0:T(8,128)S(1)}, f32[2048,128]{1,0:T(8,128)S(1)}, f32[2048,128]{1,0:T(8,128)S(1)}, f32[2048,128]{1,0:T(8,128)S(1)}, f32[1024,128]{1,0:T(8,128)S(1)}, /*index=5*/f32[8,128]{1,0:T(8,128)S(1)}) custom-call(bf16[1024,1024]{1,0:T(8,128)(2,1)S(1)} %get-tuple-element.44.onehot, f32[2048,128]{1,0:T(8,128)S(1)} %get-tuple-element.52.force, ...), custom_call_target="tpu_custom_call" | custom-call | flops 1610612736 | bytes 6311936 | tf_op jit(solution)/shard_map/ready/pallas_call | solution.py:17
  36.4 5.9 %collective-permute-done.2.from_a = f32[1024,128]{1,0:T(8,128)S(1)} collective-permute-done((f32[1024,128]{1,0:T(8,128)S(1)}, f32[1024,128]{1,0:T(8,128)S(1)}, u32[]{:S(2)}, u32[]{:S(2)}) %collective-permute-start.2) | collective-permute-done | bytes 524320 | tf_op jit(solution)/shard_map/ppermute | solution.py:327
  42.3 0.0 collective-permute-done.3.from_b
  42.3 2.5 %second.2 = (f32[1024,128]{1,0:T(8,128)S(1)}, f32[1024,128]{1,0:T(8,128)S(1)}, f32[32,8,128]{2,1,0:T(8,128)S(1)}) custom-call(bf16[2048,2048]{1,0:T(8,128)(2,1)S(1)} %get-tuple-element.46.b, f32[1024,128]{1,0:T(8,128)S(1)} %get-tuple-element.50.q_a, f32[1024,128]{1,0:T(8,128)S(1)} %get-tuple-element.51.q_b, f32[1024,128]{1,0:T(8,128)S(1)} %collective-permute-done.2.from_a, ...), custom_call_target="tpu_custom_call" | custom-call | flops 2147483648 | bytes 10489856 | tf_op jit(solution)/shard_map/second/pallas_call | solution.py:17
  44.9 22.6 %all_to_all.20.gathered = f32[32,8,128]{2,1,0:T(8,128)S(1)} all-to-all(f32[32,8,128]{2,1,0:T(8,128)S(1)} %get-tuple-element.56), channel_id=1, replica_groups=mesh['tm'=8,'sub'=32] {'sub'}, dimensions={0} | all-to-all | bytes 262144 | tf_op jit(solution)/shard_map/all_to_all | solution.py:382
  67.5 2.5 %next.1 = (f32[1024,128]{1,0:T(8,128)S(1)}, f32[1024,128]{1,0:T(8,128)S(1)}, f32[1024,128]{1,0:T(8,128)S(1)}, f32[1024,128]{1,0:T(8,128)S(1)}) custom-call(bf16[2048,2048]{1,0:T(8,128)(2,1)S(1)} %get-tuple-element.46.b, f32[32,8,128]{2,1,0:T(8,128)S(1)} %all_to_all.20.gathered, f32[1024,128]{1,0:T(8,128)S(1)} %get-tuple-element.47.y_a, ...), custom_call_target="tpu_custom_call" | custom-call | flops 1073741824 | bytes 14811136 | tf_op jit(solution)/shard_map/next/pallas_call | solution.py:17
  70.0 1.0 collective-permute-start.4
  71.0 0.9 collective-permute-start.5
  72.0 1.3 early.1
  73.3 6.0 %collective-permute-done.4.from_a = f32[1024,128]{1,0:T(8,128)S(1)} collective-permute-done((f32[1024,128]{1,0:T(8,128)S(1)}, f32[1024,128]{1,0:T(8,128)S(1)}, u32[]{:S(2)}, u32[]{:S(2)}) %collective-permute-start.4) | collective-permute-done | bytes 524320 | tf_op jit(solution)/shard_map/ppermute | solution.py:327
  79.3 0.0 collective-permute-done.5.from_b
  79.3 2.5 %first.3 = (f32[1024,128]{1,0:T(8,128)S(1)}, f32[1024,128]{1,0:T(8,128)S(1)}, f32[1024,128]{1,0:T(8,128)S(1)}, f32[1024,128]{1,0:T(8,128)S(1)}, f32[8,128]{1,0:T(8,128)S(1)}) custom-call(bf16[2048,2048]{1,0:T(8,128)(2,1)S(1)} %get-tuple-element.46.b, f32[1024,128]{1,0:T(8,128)S(1)} %get-tuple-element.63.y_a, f32[1024,128]{1,0:T(8,128)S(1)} %get-tuple-element.64.y_b, ...), custom_call_target="tpu_custom_call" | custom-call | flops 2147483648 | bytes 10489856 | tf_op jit(solution)/shard_map/first/pallas_call | solution.py:17
  81.8 3.2 %collective-permute-start.6 = (f32[1024,128]{1,0:T(8,128)S(1)}, f32[1024,128]{1,0:T(8,128)S(1)}, u32[]{:S(2)}, u32[]{:S(2)}) collective-permute-start(f32[1024,128]{1,0:T(8,128)S(1)} %get-tuple-element.69.q_a), channel_id=1, source_target_pairs={{0,1},{1,0},{2,3},{3,2},{4,5},{5,4},{6,7},{7,6},{8,9},{9,8},{10,11... | collective-permute-start | bytes 1572872 | tf_op jit(solution)/shard_map/ppermute | solution.py:327
  85.0 0.7 collective-permute-start.7
  85.6 5.9 %collective-permute-done.6.from_a = f32[1024,128]{1,0:T(8,128)S(1)} collective-permute-done((f32[1024,128]{1,0:T(8,128)S(1)}, f32[1024,128]{1,0:T(8,128)S(1)}, u32[]{:S(2)}, u32[]{:S(2)}) %collective-permute-start.6) | collective-permute-done | bytes 524320 | tf_op jit(solution)/shard_map/ppermute | solution.py:327
  91.5 0.0 collective-permute-done.7.from_b
  91.5 2.5 %second.3 = (f32[1024,128]{1,0:T(8,128)S(1)}, f32[1024,128]{1,0:T(8,128)S(1)}, f32[32,8,128]{2,1,0:T(8,128)S(1)}) custom-call(bf16[2048,2048]{1,0:T(8,128)(2,1)S(1)} %get-tuple-element.46.b, f32[1024,128]{1,0:T(8,128)S(1)} %get-tuple-element.69.q_a, f32[1024,128]{1,0:T(8,128)S(1)} %get-tuple-element.70.q_b, f32[1024,128]{1,0:T(8,128)S(1)} %collective-permute-done.6.from_a, ...), custom_call_target="tpu_custom_call" | custom-call | flops 2147483648 | bytes 10489856 | tf_op jit(solution)/shard_map/second/pallas_call | solution.py:17
  94.1 19.3 %all_to_all.21.gathered = f32[32,8,128]{2,1,0:T(8,128)S(1)} all-to-all(f32[32,8,128]{2,1,0:T(8,128)S(1)} %get-tuple-element.72), channel_id=1, replica_groups=mesh['tm'=8,'sub'=32] {'sub'}, dimensions={0} | all-to-all | bytes 262144 | tf_op jit(solution)/shard_map/all_to_all | solution.py:382
  113.4 1.4 finish.1
  114.8 7.8 %collective-permute-start.8 = (f32[2,1024,128]{2,1,0:T(8,128)S(1)}, f32[2,1024,128]{2,1,0:T(8,128)S(1)}, u32[]{:S(2)}, u32[]{:S(2)}) collective-permute-start(f32[2,1024,128]{2,1,0:T(8,128)S(1)} %get-tuple-element.80), channel_id=1, source_target_pairs={{0,32},{32,0},{64,96},{96,64},{128,160},{160,128},{192,224},{224,1... | collective-permute-start | bytes 3145736 | tf_op jit(solution)/shard_map/ppermute | solution.py:395
  122.6 2.3 %collective-permute-done.8.got = f32[2,1024,128]{2,1,0:T(8,128)S(1)} collective-permute-done((f32[2,1024,128]{2,1,0:T(8,128)S(1)}, f32[2,1024,128]{2,1,0:T(8,128)S(1)}, u32[]{:S(2)}, u32[]{:S(2)}) %collective-permute-start.8) | collective-permute-done | bytes 1048608 | tf_op jit(solution)/shard_map/ppermute | solution.py:395
  124.9 0.4 combine.1
  125.3 18.2 %all_to_all.22.blocks = f32[4,2,256,128]{3,2,1,0:T(8,128)S(1)} all-to-all(f32[4,2,256,128]{3,2,1,0:T(8,128)S(1)} %combine.1), channel_id=1, replica_groups={{0,64,128,192},{32,96,160,224},{1,65,129,193},{33,97,161,225},{2,66,130..., dimensions={0} | all-to-all | bytes 2097152 | tf_op jit(solution)/shard_map/all_to_all | solution.py:400
  143.5 0.3 prefix.1
  143.8 15.7 %all_to_all.23.states = f32[4,2,256,128]{3,2,1,0:T(8,128)S(1)} all-to-all(f32[4,2,256,128]{3,2,1,0:T(8,128)S(1)} %prefix.1), channel_id=1, replica_groups={{0,64,128,192},{32,96,160,224},{1,65,129,193},{33,97,161,225},{2,66,130..., dimensions={0} | all-to-all | bytes 2097152 | tf_op jit(solution)/shard_map/all_to_all | solution.py:402
  159.5 0.7 end.1
  160.2 2.8 %collective-permute-start.9 = (f32[2,1024,128]{2,1,0:T(8,128)S(1)}, f32[2,1024,128]{2,1,0:T(8,128)S(1)}, u32[]{:S(2)}, u32[]{:S(2)}) collective-permute-start(f32[2,1024,128]{2,1,0:T(8,128)S(1)} %get-tuple-element.83), channel_id=1, source_target_pairs={{0,32},{32,0},{64,96},{96,64},{128,160},{160,128},{192,224},{224,1... | collective-permute-start | bytes 3145736 | tf_op jit(solution)/shard_map/ppermute | solution.py:395
  163.0 2.3 %collective-permute-done.9.got = f32[2,1024,128]{2,1,0:T(8,128)S(1)} collective-permute-done((f32[2,1024,128]{2,1,0:T(8,128)S(1)}, f32[2,1024,128]{2,1,0:T(8,128)S(1)}, u32[]{:S(2)}, u32[]{:S(2)}) %collective-permute-start.9) | collective-permute-done | bytes 1048608 | tf_op jit(solution)/shard_map/ppermute | solution.py:395
  165.3 1.5 join.1
Async XLA Ops:
  10.1 13.1 %collective-permute-start = (f32[1024,128]{1,0:T(8,128)S(1)}, f32[1024,128]{1,0:T(8,128)S(1)}, u32[]{:S(2)}, u32[]{:S(2)}) collective-permute-start(f32[1024,128]{1,0:T(8,128)S(1)} %get-tuple-element.47.y_a), channel_id=1, source_target_pairs={{0,1},{1,0},{2,3},{3,2},{4,5},{5,4},{6,7},{7,6},{8,9},{9,8},{10,11... | collective-permute-start | bytes 1572872 | tf_op jit(solution)/shard_map/ppermute | solution.py:327
  12.6 10.6 %collective-permute-start.1 = (f32[1024,128]{1,0:T(8,128)S(1)}, f32[1024,128]{1,0:T(8,128)S(1)}, u32[]{:S(2)}, u32[]{:S(2)}) collective-permute-start(f32[1024,128]{1,0:T(8,128)S(1)} %get-tuple-element.48.y_b), channel_id=1, source_target_pairs={{1,2},{2,1},{3,4},{4,3},{5,6},{6,5},{7,8},{8,7},{9,10},{10,9},{11,... | collective-permute-start | bytes 1572872 | tf_op jit(solution)/shard_map/ppermute | solution.py:326
  25.7 16.6 %collective-permute-start.2 = (f32[1024,128]{1,0:T(8,128)S(1)}, f32[1024,128]{1,0:T(8,128)S(1)}, u32[]{:S(2)}, u32[]{:S(2)}) collective-permute-start(f32[1024,128]{1,0:T(8,128)S(1)} %get-tuple-element.50.q_a), channel_id=1, source_target_pairs={{0,1},{1,0},{2,3},{3,2},{4,5},{5,4},{6,7},{7,6},{8,9},{9,8},{10,11... | collective-permute-start | bytes 1572872 | tf_op jit(solution)/shard_map/ppermute | solution.py:327
  31.7 10.7 %collective-permute-start.3 = (f32[1024,128]{1,0:T(8,128)S(1)}, f32[1024,128]{1,0:T(8,128)S(1)}, u32[]{:S(2)}, u32[]{:S(2)}) collective-permute-start(f32[1024,128]{1,0:T(8,128)S(1)} %get-tuple-element.51.q_b), channel_id=1, source_target_pairs={{1,2},{2,1},{3,4},{4,3},{5,6},{6,5},{7,8},{8,7},{9,10},{10,9},{11,... | collective-permute-start | bytes 1572872 | tf_op jit(solution)/shard_map/ppermute | solution.py:326
  70.0 9.2 %collective-permute-start.4 = (f32[1024,128]{1,0:T(8,128)S(1)}, f32[1024,128]{1,0:T(8,128)S(1)}, u32[]{:S(2)}, u32[]{:S(2)}) collective-permute-start(f32[1024,128]{1,0:T(8,128)S(1)} %get-tuple-element.63.y_a), channel_id=1, source_target_pairs={{0,1},{1,0},{2,3},{3,2},{4,5},{5,4},{6,7},{7,6},{8,9},{9,8},{10,11... | collective-permute-start | bytes 1572872 | tf_op jit(solution)/shard_map/ppermute | solution.py:327
  71.0 8.3 %collective-permute-start.5 = (f32[1024,128]{1,0:T(8,128)S(1)}, f32[1024,128]{1,0:T(8,128)S(1)}, u32[]{:S(2)}, u32[]{:S(2)}) collective-permute-start(f32[1024,128]{1,0:T(8,128)S(1)} %get-tuple-element.64.y_b), channel_id=1, source_target_pairs={{1,2},{2,1},{3,4},{4,3},{5,6},{6,5},{7,8},{8,7},{9,10},{10,9},{11,... | collective-permute-start | bytes 1572872 | tf_op jit(solution)/shard_map/ppermute | solution.py:326
  81.8 9.7 %collective-permute-start.6 = (f32[1024,128]{1,0:T(8,128)S(1)}, f32[1024,128]{1,0:T(8,128)S(1)}, u32[]{:S(2)}, u32[]{:S(2)}) collective-permute-start(f32[1024,128]{1,0:T(8,128)S(1)} %get-tuple-element.69.q_a), channel_id=1, source_target_pairs={{0,1},{1,0},{2,3},{3,2},{4,5},{5,4},{6,7},{7,6},{8,9},{9,8},{10,11... | collective-permute-start | bytes 1572872 | tf_op jit(solution)/shard_map/ppermute | solution.py:327
  85.0 6.6 %collective-permute-start.7 = (f32[1024,128]{1,0:T(8,128)S(1)}, f32[1024,128]{1,0:T(8,128)S(1)}, u32[]{:S(2)}, u32[]{:S(2)}) collective-permute-start(f32[1024,128]{1,0:T(8,128)S(1)} %get-tuple-element.70.q_b), channel_id=1, source_target_pairs={{1,2},{2,1},{3,4},{4,3},{5,6},{6,5},{7,8},{8,7},{9,10},{10,9},{11,... | collective-permute-start | bytes 1572872 | tf_op jit(solution)/shard_map/ppermute | solution.py:326
  114.8 10.1 %collective-permute-start.8 = (f32[2,1024,128]{2,1,0:T(8,128)S(1)}, f32[2,1024,128]{2,1,0:T(8,128)S(1)}, u32[]{:S(2)}, u32[]{:S(2)}) collective-permute-start(f32[2,1024,128]{2,1,0:T(8,128)S(1)} %get-tuple-element.80), channel_id=1, source_target_pairs={{0,32},{32,0},{64,96},{96,64},{128,160},{160,128},{192,224},{224,1... | collective-permute-start | bytes 3145736 | tf_op jit(solution)/shard_map/ppermute | solution.py:395
  160.2 5.1 %collective-permute-start.9 = (f32[2,1024,128]{2,1,0:T(8,128)S(1)}, f32[2,1024,128]{2,1,0:T(8,128)S(1)}, u32[]{:S(2)}, u32[]{:S(2)}) collective-permute-start(f32[2,1024,128]{2,1,0:T(8,128)S(1)} %get-tuple-element.83), channel_id=1, source_target_pairs={{0,32},{32,0},{64,96},{96,64},{128,160},{160,128},{192,224},{224,1... | collective-permute-start | bytes 3145736 | tf_op jit(solution)/shard_map/ppermute | solution.py:395

commit v5 on v4

--- a/solution.py
+++ b/solution.py
@@ -9,7 +9,7 @@
 BF16 = jnp.bfloat16
 VMEM = pl.BlockSpec(memory_space=pltpu.VMEM)
 HBM = pl.BlockSpec(memory_space=pltpu.HBM)
-CHUNKS = 4
+CHUNKS = 8
 
 
 def call(kernel, name, outs, args, flops=0, in_specs=None, scratch=(), limit=12, space=pltpu.VMEM):
@@ -67,12 +67,24 @@
 
 def by_pairs(left, right):
     even = is_even()
-    return jnp.where(even, right, left), jnp.where(even, left, right)
+    return jnp.where(even, left, right), jnp.where(even, right, left)
 
 
 def by_sides(face_a, face_b):
     even = is_even()
-    return jnp.where(even, face_b, face_a), jnp.where(even, face_a, face_b)
+    return jnp.where(even, face_a, face_b), jnp.where(even, face_b, face_a)
+
+
+def sides(half, step):
+    odd = lax.rem(lax.axis_index("sub"), 2)
+
+    def left(offset, count):
+        return pl.ds(pl.multiple_of(odd * half + offset, step), count)
+
+    def right(offset, count):
+        return pl.ds(pl.multiple_of((1 - odd) * half + offset, step), count)
+
+    return left, right
 
 
 def start_kernel(
@@ -119,68 +131,56 @@
 def prepare_kernel(a, onehot, b, order, turned):
     order[...] = jnp.zeros(order.shape, F32)
     size = a.shape[0]
-    half, rows = size // 2, size // CHUNKS
+    half, rows = size // 2, size // 4
+    left, right = sides(half, rows)
     hot = onehot[...]
-    odd = lax.rem(lax.axis_index("sub"), 2)
-
-    def left(offset, count):
-        return pl.ds(pl.multiple_of((1 - odd) * half + offset, rows), count)
-
-    def right(offset, count):
-        return pl.ds(pl.multiple_of(odd * half + offset, rows), count)
-
-    for k in range(CHUNKS):
+    for k in range(4):
         here = slice(k * rows, (k + 1) * rows)
         block = lax.dot_general(a[here, :half], hot, (((1,), (1,)), ((), ())), preferred_element_type=F32).astype(BF16)
-        if k < CHUNKS // 2:
+        if k < 2:
             turned[here] = block
         else:
             down = right(k * rows - half, rows)
             b[down, left(0, half)] = block
             b[down, right(0, half)] = a[here, half:]
-    for k in range(CHUNKS):
+    for k in range(4):
         here = slice(k * rows, (k + 1) * rows)
-        if k < CHUNKS // 2:
+        if k < 2:
             block, across = turned[:, here], left(k * rows, rows)
         else:
             block, across = a[:half, here], right(k * rows - half, rows)
         b[left(0, half), across] = jnp.dot(hot, block, preferred_element_type=F32).astype(BF16)
 
 
-def ready_kernel(onehot, force, mass_in, rate_in, u_in, v_in, base, sums_in, force_m, weight_m, early_u, early_v, rate_own, sums, mass, rate, u, v, sem):
-    copies = [
-        pltpu.make_async_copy(source, target, sem.at[k]) for k, (source, target) in enumerate([(mass_in, mass), (rate_in, rate), (u_in, u), (v_in, v)])
-    ]
-    for copy in copies:
-        copy.start()
+def ready_kernel(onehot, force, mass_in, sums_in, force_m, weight_m, sums, mass, sem):
+    copy = pltpu.make_async_copy(mass_in, mass, sem)
+    copy.start()
     sums[...] = sums_in[...]
-    hot = onehot[...]
-    half = hot.shape[0]
-    copies[0].wait()
+    half = onehot.shape[0]
+    copy.wait()
     weight = 6.0 * column(mass[...])
-    force_m[:half], force_m[half:] = by_pairs(to_multipliers(hot, force[:half]), force[half:])
-    weight_m[:half], weight_m[half:] = by_pairs(to_multipliers(hot, weight[:half]), weight[half:])
-    for copy in copies[1:]:
-        copy.wait()
-    tm = lax.axis_index("tm")
-    rates = column(rate[...])
-    rate_own[...] = jnp.where(tm % 2 == 0, rates[:half], rates[half:])
-    same, up, down = coarse(rates)
-    early_u[...] = -jnp.where(tm == 0, 0.0, same * u[...] + up * v[...])
-    early_v[...] = base[...] - jnp.where(tm == 0, 0.0, down * u[...] + same * v[...])
+    lane = lax.broadcasted_iota(jnp.int32, (half, 128), 1)
+    three = triple(weight[:half])
+    packed = jnp.where(
+        lane == 0, three[:, :128].astype(F32), jnp.where(lane == 1, three[:, 128:256].astype(F32), three[:, 256:].astype(F32))
+    )
+    both = jnp.concatenate([triple(force[:half]), jnp.where(lane < 3, packed, 0.0).astype(BF16)], axis=1)
+    moved = jnp.dot(onehot[...], both, preferred_element_type=F32)
+    force_m[:half], force_m[half:] = by_pairs(fold(moved[:, :384]), force[half:])
+    left = jnp.broadcast_to(jnp.sum(moved[:, 384:], axis=1, keepdims=True), (half, 128))
+    weight_m[:half], weight_m[half:] = by_pairs(left, weight[half:])
 
 
 def jump(f_a, f_b, from_a, from_b):
     sub = lax.axis_index("sub")
     alone = jnp.logical_or(sub == 0, sub == lax.axis_size("sub") - 1)
-    return f_a[...] - from_a[...], jnp.where(alone, 0.0, f_b[...] - from_b[...])
+    return jnp.where(alone, 0.0, f_a[...] - from_a[...]), f_b[...] - from_b[...]
 
 
 def first_kernel(b, y_a, y_b, from_a, from_b, order, q_a, q_b, t_a, t_b, sums):
     half = y_a.shape[0]
     r_a, r_b = jump(y_a, y_b, from_a, from_b)
-    z = jnp.concatenate([pair(r_a), pair(r_b)], axis=0)
-    wide = jnp.dot(b[...], z, preferred_element_type=F32)
+    wide = jnp.dot(b[...], jnp.concatenate([pair(r_a), pair(r_b)], axis=0), preferred_element_type=F32)
     q = wide[:, :128]
     t = q + wide[:, 128:]
     q_a[...], q_b[...] = q[:half], q[half:]
@@ -193,8 +193,7 @@
 def second_kernel(b, q_a, q_b, from_a, from_b, sums, s_a, s_b, spread):
     half = q_a.shape[0]
     w_a, w_b = jump(q_a, q_b, from_a, from_b)
-    z = jnp.concatenate([pair(w_a), pair(w_b)], axis=0)
-    wide = jnp.dot(b[...], z, preferred_element_type=F32)
+    wide = jnp.dot(b[...], jnp.concatenate([pair(w_a), pair(w_b)], axis=0), preferred_element_type=F32)
     s = wide[:, :128] + wide[:, 128:]
     s_a[...], s_b[...] = s[:half], s[half:]
     ww = 0.5 * (add_up(w_a * w_a) + add_up(w_b * w_b))
@@ -231,12 +230,24 @@
     return (1.0 - rate) * scale, 2.0 * scale, -2.0 * rate * scale
 
 
-def early_kernel(onehot, u_a, u_b, early_in, early_v, order):
+def early_kernel(onehot, u_a, u_b, base, rate_in, u_in, v_in, early_u, early_v, rate_own, order, rate, u, v, sem):
+    copies = [
+        pltpu.make_async_copy(source, target, sem.at[k]) for k, (source, target) in enumerate([(rate_in, rate), (u_in, u), (v_in, v)])
+    ]
+    for copy in copies:
+        copy.start()
     order[...] = jnp.zeros(order.shape, F32)
     half = u_a.shape[0]
     left, right = by_sides(u_a[...], u_b[...])
-    early_v[:half] = early_in[:half] - 4.0 * to_left(onehot[...], left)
-    early_v[half:] = early_in[half:] - 4.0 * right
+    later = jnp.concatenate([to_left(onehot[...], left), right], axis=0)
+    for copy in copies:
+        copy.wait()
+    tm = lax.axis_index("tm")
+    rates = column(rate[...])
+    rate_own[...] = jnp.where(tm % 2 == 0, rates[:half], rates[half:])
+    same, up, down = coarse(rates)
+    early_u[...] = -jnp.where(tm == 0, 0.0, same * u[...] + up * v[...])
+    early_v[...] = base[...] - 4.0 * later - jnp.where(tm == 0, 0.0, down * u[...] + same * v[...])
 
 
 def finish_kernel(onehot, gathered, y_a, y_b, q_a, q_b, t_a, t_b, s_a, s_b, early_u, early_v, own, give):
@@ -315,7 +326,7 @@
         pltpu.with_memory_space_constraint(value, pltpu.HBM)
         for value in (flex[0], mass, coarse_rate, face_perm, start_u[0, 0], start_v[0, 0], load[0, 0])
     ]
-    pairs = [[p for s in range(k, subs - 1, 2) for p in ((s, s + 1), (s + 1, s))] for k in range(2)]
+    pairs = [[p for s in range(k, subs - 1, 2) for p in ((s, s + 1), (s + 1, s))] for k in (1, 0)]
     face = ((half, cases), F32)
     whole = ((size, cases), F32)
     small = ((8, cases), F32)
@@ -323,8 +334,8 @@
     once = 2 * size * size * cases
 
     def exchange(face_a, face_b):
-        from_b = lax.ppermute(face_b, "sub", pairs[1])
-        return lax.ppermute(face_a, "sub", pairs[0]), from_b
+        from_a = lax.ppermute(face_a, "sub", pairs[0])
+        return from_a, lax.ppermute(face_b, "sub", pairs[1])
 
     a, onehot, y_a, y_b, base, force = call(
         start_kernel,
@@ -343,7 +354,6 @@
             pltpu.SemaphoreType.DMA((CHUNKS,)),
         ],
     )
-    matrix = None
     for step in range(2):
         from_a, from_b = exchange(y_a, y_b)
         if step == 0:
@@ -351,26 +361,33 @@
                 prepare_kernel, "prepare", [square, small], (a, onehot), 8 * half**3, scratch=[pltpu.VMEM((half, half), BF16)]
             )
         else:
-            early_v, order = call(early_kernel, "early", [whole, small], (onehot, u_a, u_b, early_v), 2 * half * half * 3 * cases)
+            early_u, early_v, rate_own, order = call(
+                early_kernel,
+                "early",
+                [whole, whole, face, small],
+                (onehot, u_a, u_b, base, coarse_rate, u, v),
+                2 * half * half * 3 * cases,
+                in_specs=[VMEM] * 4 + [HBM] * 3,
+                scratch=[
+                    pltpu.VMEM((1, size), F32),
+                    pltpu.VMEM((size, cases), F32),
+                    pltpu.VMEM((size, cases), F32),
+                    pltpu.SemaphoreType.DMA((3,)),
+                ],
+            )
         q_a, q_b, t_a, t_b, sums = call(
             first_kernel, "first", [face] * 4 + [small], (matrix, y_a, y_b, from_a, from_b, order), 2 * once
         )
         from_a, from_b = exchange(q_a, q_b)
         if step == 0:
-            force_m, weight_m, early_u, early_v, rate_own, sums = call(
+            force_m, weight_m, sums = call(
                 ready_kernel,
                 "ready",
-                [whole] * 4 + [face, small],
-                (onehot, force, mass, coarse_rate, u, v, base, sums),
-                2 * half * half * 6 * cases,
-                in_specs=[VMEM] * 2 + [HBM] * 4 + [VMEM] * 2,
-                scratch=[
-                    pltpu.VMEM((1, size), F32),
-                    pltpu.VMEM((1, size), F32),
-                    pltpu.VMEM((size, cases), F32),
-                    pltpu.VMEM((size, cases), F32),
-                    pltpu.SemaphoreType.DMA((4,)),
-                ],
+                [whole, whole, small],
+                (onehot, force, mass, sums),
+                2 * half * half * 4 * cases,
+                in_specs=[VMEM, VMEM, HBM, VMEM],
+                scratch=[pltpu.VMEM((1, size), F32), pltpu.SemaphoreType.DMA(())],
             )
         s_a, s_b, spread = call(
             second_kernel,
@@ -379,7 +396,7 @@
             (matrix, q_a, q_b, from_a, from_b, sums),
             2 * once,
         )
-        gathered = lax.all_to_all(spread, "sub", 0, 0)
+        gathered = lax.all_to_all(spread, "sub", 0, 0, axis_index_groups=[list(range(subs))[::-1]])
         fields = (gathered, y_a, y_b, q_a, q_b, t_a, t_b, s_a, s_b)
         if step == 0:
             y_a, y_b, u_a, u_b = call(next_kernel, "next", [face] * 4, (matrix,) + fields + (force_m, weight_m), once)

time: 167 us -> 163 us (0.976)
  blocking collectives: 75.9 us -> 65 us
  starting transfers between devices: 26.7 us -> 31.5 us
  waiting for transfers between devices: 23 us -> 26.4 us
    all_to_all x2, blocking collectives: 42 us -> 31.1 us  [on_device(): lax.all_to_all(spread, 'sub', 0, 0, axis_index_groups=[list(range(subs))[...]
    ppermute x8, starting transfers between devices: 16 us -> 20.9 us  [the longest x4 18.1 us: exchange(): return (from_a, lax.ppermute(face_b, 'sub', pairs[1]))]
    ppermute x8, waiting for transfers between devices: 18.5 us -> 21.8 us  [the longest x4 21.8 us: exchange(): return (from_a, lax.ppermute(face_b, 'sub', pairs[1]))]
where the time goes in v5:
time: 163 us
  blocking collectives  65 us (40%)
  Pallas kernels  38.9 us (24%)
  starting transfers between devices  31.5 us (19%)
  waiting for transfers between devices  26.4 us (16%)
    pallas_call x14, Pallas kernels, call(): pl.pallas_call(kernel, name=name, out_shape=[space(shape, dtype) for shap...  38.9 us
    all_to_all x2, blocking collectives, on_device(): lax.all_to_all(spread, 'sub', 0, 0, axis_index_groups=[list(range(subs))[...  31.1 us
    ppermute x4, waiting for transfers between devices, exchange(): return (from_a, lax.ppermute(face_b, 'sub', pairs[1]))  21.8 us
    all_to_all x1, blocking collectives, on_device(): parts = lax.all_to_all(parts, 'tm', 0, 0, axis_index_groups=groups)  18.2 us
    ppermute x4, starting transfers between devices, exchange(): return (from_a, lax.ppermute(face_b, 'sub', pairs[1]))  18.1 us
    all_to_all x1, blocking collectives, on_device(): states = lax.all_to_all(states, 'tm', 0, 0, axis_index_groups=groups)  15.7 us
    ppermute x2, starting transfers between devices, swap(): return lax.ppermute(value, 'tm', [(t, t ^ 1) for t in range(slices)])  10.6 us
    ppermute x2, waiting for transfers between devices, swap(): return lax.ppermute(value, 'tm', [(t, t ^ 1) for t in range(slices)])  4.57 us
  transfers between devices with their start and end apart: 10, of which 6 were waited for; matrix products, arithmetic and copies ran while one was open for 0% of the time, Pallas kernels for 9%

profile of v5, /device:TPU:1, one launch (start us, length us, event | category | flops | bytes accessed | tf_op | source)
XLA Modules:
  0.0 162.6 jit_solution(16552905236525836899)
XLA Ops:
  0.6 7.5 %start.1 = (bf16[2048,2048]{1,0:T(8,128)(2,1)S(1)}, bf16[1024,1024]{1,0:T(8,128)(2,1)S(1)}, f32[1024,128]{1,0:T(8,128)S(1)}, f32[1024,128]{1,0:T(8,128)S(1)}, f3...) custom-call(bf16[2048,2048]{1,0:T(8,128)(2,1)} %bitcast.6, f32[2048,128]{1,0:T(8,128)} %bitcast.7, f32[2048,128]{1,0:T(8,128)} %bitcast.9, ...), custom_call_target="tpu_custom_call" | custom-call | flops 1073741824 | bytes 11022336 | tf_op jit(solution)/shard_map/start/pallas_call | solution.py:17
  8.2 0.7 collective-permute-start
  8.9 5.6 %collective-permute-start.1 = (f32[1024,128]{1,0:T(8,128)S(1)}, f32[1024,128]{1,0:T(8,128)S(1)}, u32[]{:S(2)}, u32[]{:S(2)}) collective-permute-start(f32[1024,128]{1,0:T(8,128)S(1)} %get-tuple-element.47.y_b), channel_id=1, source_target_pairs={{0,1},{1,0},{2,3},{3,2},{4,5},{5,4},{6,7},{7,6},{8,9},{9,8},{10,11... | collective-permute-start | bytes 1572872 | tf_op jit(solution)/shard_map/ppermute | solution.py:338
  14.5 9.0 %prepare.1 = (bf16[2048,2048]{1,0:T(8,128)(2,1)S(1)}, f32[8,128]{1,0:T(8,128)S(1)}) custom-call(bf16[2048,2048]{1,0:T(8,128)(2,1)S(1)} %get-tuple-element.44.a, bf16[1024,1024]{1,0:T(8,128)(2,1)S(1)} %get-tuple-element.43.onehot), custom_call_target="tpu_custom_call" | custom-call | flops 8589934592 | bytes 10485760 | tf_op jit(solution)/shard_map/prepare/pallas_call | solution.py:17
  23.5 0.0 collective-permute-done.from_a
  23.5 2.3 %collective-permute-done.1.from_b = f32[1024,128]{1,0:T(8,128)S(1)} collective-permute-done((f32[1024,128]{1,0:T(8,128)S(1)}, f32[1024,128]{1,0:T(8,128)S(1)}, u32[]{:S(2)}, u32[]{:S(2)}) %collective-permute-start.1) | collective-permute-done | bytes 524320 | tf_op jit(solution)/shard_map/ppermute | solution.py:338
  25.8 2.5 %first.2 = (f32[1024,128]{1,0:T(8,128)S(1)}, f32[1024,128]{1,0:T(8,128)S(1)}, f32[1024,128]{1,0:T(8,128)S(1)}, f32[1024,128]{1,0:T(8,128)S(1)}, f32[8,128]{1,0:T(8,128)S(1)}) custom-call(bf16[2048,2048]{1,0:T(8,128)(2,1)S(1)} %get-tuple-element.45.b, f32[1024,128]{1,0:T(8,128)S(1)} %get-tuple-element.46.y_a, f32[1024,128]{1,0:T(8,128)S(1)} %get-tuple-element.47.y_b, ...), custom_call_target="tpu_custom_call" | custom-call | flops 2147483648 | bytes 10489856 | tf_op jit(solution)/shard_map/first/pallas_call | solution.py:17
  28.3 0.7 collective-permute-start.2
  29.0 6.0 %collective-permute-start.3 = (f32[1024,128]{1,0:T(8,128)S(1)}, f32[1024,128]{1,0:T(8,128)S(1)}, u32[]{:S(2)}, u32[]{:S(2)}) collective-permute-start(f32[1024,128]{1,0:T(8,128)S(1)} %get-tuple-element.50.q_b), channel_id=1, source_target_pairs={{0,1},{1,0},{2,3},{3,2},{4,5},{5,4},{6,7},{7,6},{8,9},{9,8},{10,11... | collective-permute-start | bytes 1572872 | tf_op jit(solution)/shard_map/ppermute | solution.py:338
  35.0 2.1 %ready.1 = (f32[2048,128]{1,0:T(8,128)S(1)}, f32[2048,128]{1,0:T(8,128)S(1)}, f32[8,128]{1,0:T(8,128)S(1)}) custom-call(bf16[1024,1024]{1,0:T(8,128)(2,1)S(1)} %get-tuple-element.43.onehot, f32[2048,128]{1,0:T(8,128)S(1)} %get-tuple-element.51.force, f32[1,2048]{1,0:T(1,128)} %mass_in.3, f32[8,128]{1,0:T(8,128)S(1)} %get-tuple-element.52.sums_in), custom_call_target="tpu_custom_call" | custom-call | flops 1073741824 | bytes 3158016 | tf_op jit(solution)/shard_map/ready/pallas_call | solution.py:17
  37.1 0.0 collective-permute-done.2.from_a
  37.2 8.3 %collective-permute-done.3.from_b = f32[1024,128]{1,0:T(8,128)S(1)} collective-permute-done((f32[1024,128]{1,0:T(8,128)S(1)}, f32[1024,128]{1,0:T(8,128)S(1)}, u32[]{:S(2)}, u32[]{:S(2)}) %collective-permute-start.3) | collective-permute-done | bytes 524320 | tf_op jit(solution)/shard_map/ppermute | solution.py:338
  45.4 2.5 %second.2 = (f32[1024,128]{1,0:T(8,128)S(1)}, f32[1024,128]{1,0:T(8,128)S(1)}, f32[32,8,128]{2,1,0:T(8,128)S(1)}) custom-call(bf16[2048,2048]{1,0:T(8,128)(2,1)S(1)} %get-tuple-element.45.b, f32[1024,128]{1,0:T(8,128)S(1)} %get-tuple-element.49.q_a, f32[1024,128]{1,0:T(8,128)S(1)} %get-tuple-element.50.q_b, f32[1024,128]{1,0:T(8,128)S(1)} %collective-permute-done.2.from_a, ...), custom_call_target="tpu_custom_call" | custom-call | flops 2147483648 | bytes 10489856 | tf_op jit(solution)/shard_map/second/pallas_call | solution.py:17
  47.9 15.4 %all_to_all.20.gathered = f32[32,8,128]{2,1,0:T(8,128)S(1)} all-to-all(f32[32,8,128]{2,1,0:T(8,128)S(1)} %get-tuple-element.54), channel_id=1, replica_groups={{31,30,29,28,27,26,25,24,23,22,21,20,19,18,17,16,15,14,13,12,11,10,9,8,..., dimensions={0} | all-to-all | bytes 262144 | tf_op jit(solution)/shard_map/all_to_all | solution.py:399
  63.3 2.5 %next.1 = (f32[1024,128]{1,0:T(8,128)S(1)}, f32[1024,128]{1,0:T(8,128)S(1)}, f32[1024,128]{1,0:T(8,128)S(1)}, f32[1024,128]{1,0:T(8,128)S(1)}) custom-call(bf16[2048,2048]{1,0:T(8,128)(2,1)S(1)} %get-tuple-element.45.b, f32[32,8,128]{2,1,0:T(8,128)S(1)} %all_to_all.20.gathered, f32[1024,128]{1,0:T(8,128)S(1)} %get-tuple-element.46.y_a, ...), custom_call_target="tpu_custom_call" | custom-call | flops 1073741824 | bytes 14811136 | tf_op jit(solution)/shard_map/next/pallas_call | solution.py:17
  65.9 0.7 collective-permute-start.4
  66.6 2.4 %collective-permute-start.5 = (f32[1024,128]{1,0:T(8,128)S(1)}, f32[1024,128]{1,0:T(8,128)S(1)}, u32[]{:S(2)}, u32[]{:S(2)}) collective-permute-start(f32[1024,128]{1,0:T(8,128)S(1)} %get-tuple-element.62.y_b), channel_id=1, source_target_pairs={{0,1},{1,0},{2,3},{3,2},{4,5},{5,4},{6,7},{7,6},{8,9},{9,8},{10,11... | collective-permute-start | bytes 1572872 | tf_op jit(solution)/shard_map/ppermute | solution.py:338
  68.9 3.4 %early.1 = (f32[2048,128]{1,0:T(8,128)S(1)}, f32[2048,128]{1,0:T(8,128)S(1)}, f32[1024,128]{1,0:T(8,128)S(1)}, f32[8,128]{1,0:T(8,128)S(1)}) custom-call(bf16[1024,1024]{1,0:T(8,128)(2,1)S(1)} %get-tuple-element.43.onehot, f32[1024,128]{1,0:T(8,128)S(1)} %get-tuple-element.63.u_a, f32[1024,128]{1,0:T(8,128)S(1)} %get-tuple-element.64.u_b, ...), custom_call_target="tpu_custom_call" | custom-call | flops 805306368 | bytes 6299648 | tf_op jit(solution)/shard_map/early/pallas_call | solution.py:17
  72.3 0.0 collective-permute-done.4.from_a
  72.3 4.7 %collective-permute-done.5.from_b = f32[1024,128]{1,0:T(8,128)S(1)} collective-permute-done((f32[1024,128]{1,0:T(8,128)S(1)}, f32[1024,128]{1,0:T(8,128)S(1)}, u32[]{:S(2)}, u32[]{:S(2)}) %collective-permute-start.5) | collective-permute-done | bytes 524320 | tf_op jit(solution)/shard_map/ppermute | solution.py:338
  77.0 2.5 %first.3 = (f32[1024,128]{1,0:T(8,128)S(1)}, f32[1024,128]{1,0:T(8,128)S(1)}, f32[1024,128]{1,0:T(8,128)S(1)}, f32[1024,128]{1,0:T(8,128)S(1)}, f32[8,128]{1,0:T(8,128)S(1)}) custom-call(bf16[2048,2048]{1,0:T(8,128)(2,1)S(1)} %get-tuple-element.45.b, f32[1024,128]{1,0:T(8,128)S(1)} %get-tuple-element.61.y_a, f32[1024,128]{1,0:T(8,128)S(1)} %get-tuple-element.62.y_b, ...), custom_call_target="tpu_custom_call" | custom-call | flops 2147483648 | bytes 10489856 | tf_op jit(solution)/shard_map/first/pallas_call | solution.py:17
  79.5 0.7 collective-permute-start.6
  80.2 4.2 %collective-permute-start.7 = (f32[1024,128]{1,0:T(8,128)S(1)}, f32[1024,128]{1,0:T(8,128)S(1)}, u32[]{:S(2)}, u32[]{:S(2)}) collective-permute-start(f32[1024,128]{1,0:T(8,128)S(1)} %get-tuple-element.68.q_b), channel_id=1, source_target_pairs={{0,1},{1,0},{2,3},{3,2},{4,5},{5,4},{6,7},{7,6},{8,9},{9,8},{10,11... | collective-permute-start | bytes 1572872 | tf_op jit(solution)/shard_map/ppermute | solution.py:338
  84.4 0.0 collective-permute-done.6.from_a
  84.4 6.6 %collective-permute-done.7.from_b = f32[1024,128]{1,0:T(8,128)S(1)} collective-permute-done((f32[1024,128]{1,0:T(8,128)S(1)}, f32[1024,128]{1,0:T(8,128)S(1)}, u32[]{:S(2)}, u32[]{:S(2)}) %collective-permute-start.7) | collective-permute-done | bytes 524320 | tf_op jit(solution)/shard_map/ppermute | solution.py:338
  91.0 2.5 %second.3 = (f32[1024,128]{1,0:T(8,128)S(1)}, f32[1024,128]{1,0:T(8,128)S(1)}, f32[32,8,128]{2,1,0:T(8,128)S(1)}) custom-call(bf16[2048,2048]{1,0:T(8,128)(2,1)S(1)} %get-tuple-element.45.b, f32[1024,128]{1,0:T(8,128)S(1)} %get-tuple-element.67.q_a, f32[1024,128]{1,0:T(8,128)S(1)} %get-tuple-element.68.q_b, f32[1024,128]{1,0:T(8,128)S(1)} %collective-permute-done.6.from_a, ...), custom_call_target="tpu_custom_call" | custom-call | flops 2147483648 | bytes 10489856 | tf_op jit(solution)/shard_map/second/pallas_call | solution.py:17
  93.5 15.7 %all_to_all.21.gathered = f32[32,8,128]{2,1,0:T(8,128)S(1)} all-to-all(f32[32,8,128]{2,1,0:T(8,128)S(1)} %get-tuple-element.70), channel_id=1, replica_groups={{31,30,29,28,27,26,25,24,23,22,21,20,19,18,17,16,15,14,13,12,11,10,9,8,..., dimensions={0} | all-to-all | bytes 262144 | tf_op jit(solution)/shard_map/all_to_all | solution.py:399
  109.1 1.4 finish.1
  110.6 7.8 %collective-permute-start.8 = (f32[2,1024,128]{2,1,0:T(8,128)S(1)}, f32[2,1024,128]{2,1,0:T(8,128)S(1)}, u32[]{:S(2)}, u32[]{:S(2)}) collective-permute-start(f32[2,1024,128]{2,1,0:T(8,128)S(1)} %get-tuple-element.78), channel_id=1, source_target_pairs={{0,32},{32,0},{64,96},{96,64},{128,160},{160,128},{192,224},{224,1... | collective-permute-start | bytes 3145736 | tf_op jit(solution)/shard_map/ppermute | solution.py:412
  118.4 2.3 %collective-permute-done.8.got = f32[2,1024,128]{2,1,0:T(8,128)S(1)} collective-permute-done((f32[2,1024,128]{2,1,0:T(8,128)S(1)}, f32[2,1024,128]{2,1,0:T(8,128)S(1)}, u32[]{:S(2)}, u32[]{:S(2)}) %collective-permute-start.8) | collective-permute-done | bytes 1048608 | tf_op jit(solution)/shard_map/ppermute | solution.py:412
  120.7 0.4 combine.1
  121.1 18.2 %all_to_all.22.blocks = f32[4,2,256,128]{3,2,1,0:T(8,128)S(1)} all-to-all(f32[4,2,256,128]{3,2,1,0:T(8,128)S(1)} %combine.1), channel_id=1, replica_groups={{0,64,128,192},{32,96,160,224},{1,65,129,193},{33,97,161,225},{2,66,130..., dimensions={0} | all-to-all | bytes 2097152 | tf_op jit(solution)/shard_map/all_to_all | solution.py:417
  139.3 0.3 prefix.1
  139.6 15.7 %all_to_all.23.states = f32[4,2,256,128]{3,2,1,0:T(8,128)S(1)} all-to-all(f32[4,2,256,128]{3,2,1,0:T(8,128)S(1)} %prefix.1), channel_id=1, replica_groups={{0,64,128,192},{32,96,160,224},{1,65,129,193},{33,97,161,225},{2,66,130..., dimensions={0} | all-to-all | bytes 2097152 | tf_op jit(solution)/shard_map/all_to_all | solution.py:419
  155.3 0.7 end.1
  156.0 2.8 %collective-permute-start.9 = (f32[2,1024,128]{2,1,0:T(8,128)S(1)}, f32[2,1024,128]{2,1,0:T(8,128)S(1)}, u32[]{:S(2)}, u32[]{:S(2)}) collective-permute-start(f32[2,1024,128]{2,1,0:T(8,128)S(1)} %get-tuple-element.81), channel_id=1, source_target_pairs={{0,32},{32,0},{64,96},{96,64},{128,160},{160,128},{192,224},{224,1... | collective-permute-start | bytes 3145736 | tf_op jit(solution)/shard_map/ppermute | solution.py:412
  158.8 2.3 %collective-permute-done.9.got = f32[2,1024,128]{2,1,0:T(8,128)S(1)} collective-permute-done((f32[2,1024,128]{2,1,0:T(8,128)S(1)}, f32[2,1024,128]{2,1,0:T(8,128)S(1)}, u32[]{:S(2)}, u32[]{:S(2)}) %collective-permute-start.9) | collective-permute-done | bytes 1048608 | tf_op jit(solution)/shard_map/ppermute | solution.py:412
  161.1 1.5 join.1
Async XLA Ops:
  8.2 15.3 %collective-permute-start = (f32[1024,128]{1,0:T(8,128)S(1)}, f32[1024,128]{1,0:T(8,128)S(1)}, u32[]{:S(2)}, u32[]{:S(2)}) collective-permute-start(f32[1024,128]{1,0:T(8,128)S(1)} %get-tuple-element.46.y_a), channel_id=1, source_target_pairs={{1,2},{2,1},{3,4},{4,3},{5,6},{6,5},{7,8},{8,7},{9,10},{10,9},{11,... | collective-permute-start | bytes 1572872 | tf_op jit(solution)/shard_map/ppermute | solution.py:337
  8.9 16.9 %collective-permute-start.1 = (f32[1024,128]{1,0:T(8,128)S(1)}, f32[1024,128]{1,0:T(8,128)S(1)}, u32[]{:S(2)}, u32[]{:S(2)}) collective-permute-start(f32[1024,128]{1,0:T(8,128)S(1)} %get-tuple-element.47.y_b), channel_id=1, source_target_pairs={{0,1},{1,0},{2,3},{3,2},{4,5},{5,4},{6,7},{7,6},{8,9},{9,8},{10,11... | collective-permute-start | bytes 1572872 | tf_op jit(solution)/shard_map/ppermute | solution.py:338
  28.3 8.8 %collective-permute-start.2 = (f32[1024,128]{1,0:T(8,128)S(1)}, f32[1024,128]{1,0:T(8,128)S(1)}, u32[]{:S(2)}, u32[]{:S(2)}) collective-permute-start(f32[1024,128]{1,0:T(8,128)S(1)} %get-tuple-element.49.q_a), channel_id=1, source_target_pairs={{1,2},{2,1},{3,4},{4,3},{5,6},{6,5},{7,8},{8,7},{9,10},{10,9},{11,... | collective-permute-start | bytes 1572872 | tf_op jit(solution)/shard_map/ppermute | solution.py:337
  29.0 16.4 %collective-permute-start.3 = (f32[1024,128]{1,0:T(8,128)S(1)}, f32[1024,128]{1,0:T(8,128)S(1)}, u32[]{:S(2)}, u32[]{:S(2)}) collective-permute-start(f32[1024,128]{1,0:T(8,128)S(1)} %get-tuple-element.50.q_b), channel_id=1, source_target_pairs={{0,1},{1,0},{2,3},{3,2},{4,5},{5,4},{6,7},{7,6},{8,9},{9,8},{10,11... | collective-permute-start | bytes 1572872 | tf_op jit(solution)/shard_map/ppermute | solution.py:338
  65.9 6.4 %collective-permute-start.4 = (f32[1024,128]{1,0:T(8,128)S(1)}, f32[1024,128]{1,0:T(8,128)S(1)}, u32[]{:S(2)}, u32[]{:S(2)}) collective-permute-start(f32[1024,128]{1,0:T(8,128)S(1)} %get-tuple-element.61.y_a), channel_id=1, source_target_pairs={{1,2},{2,1},{3,4},{4,3},{5,6},{6,5},{7,8},{8,7},{9,10},{10,9},{11,... | collective-permute-start | bytes 1572872 | tf_op jit(solution)/shard_map/ppermute | solution.py:337
  66.6 10.5 %collective-permute-start.5 = (f32[1024,128]{1,0:T(8,128)S(1)}, f32[1024,128]{1,0:T(8,128)S(1)}, u32[]{:S(2)}, u32[]{:S(2)}) collective-permute-start(f32[1024,128]{1,0:T(8,128)S(1)} %get-tuple-element.62.y_b), channel_id=1, source_target_pairs={{0,1},{1,0},{2,3},{3,2},{4,5},{5,4},{6,7},{7,6},{8,9},{9,8},{10,11... | collective-permute-start | bytes 1572872 | tf_op jit(solution)/shard_map/ppermute | solution.py:338
  79.5 4.9 %collective-permute-start.6 = (f32[1024,128]{1,0:T(8,128)S(1)}, f32[1024,128]{1,0:T(8,128)S(1)}, u32[]{:S(2)}, u32[]{:S(2)}) collective-permute-start(f32[1024,128]{1,0:T(8,128)S(1)} %get-tuple-element.67.q_a), channel_id=1, source_target_pairs={{1,2},{2,1},{3,4},{4,3},{5,6},{6,5},{7,8},{8,7},{9,10},{10,9},{11,... | collective-permute-start | bytes 1572872 | tf_op jit(solution)/shard_map/ppermute | solution.py:337
  80.2 10.7 %collective-permute-start.7 = (f32[1024,128]{1,0:T(8,128)S(1)}, f32[1024,128]{1,0:T(8,128)S(1)}, u32[]{:S(2)}, u32[]{:S(2)}) collective-permute-start(f32[1024,128]{1,0:T(8,128)S(1)} %get-tuple-element.68.q_b), channel_id=1, source_target_pairs={{0,1},{1,0},{2,3},{3,2},{4,5},{5,4},{6,7},{7,6},{8,9},{9,8},{10,11... | collective-permute-start | bytes 1572872 | tf_op jit(solution)/shard_map/ppermute | solution.py:338
  110.6 10.1 %collective-permute-start.8 = (f32[2,1024,128]{2,1,0:T(8,128)S(1)}, f32[2,1024,128]{2,1,0:T(8,128)S(1)}, u32[]{:S(2)}, u32[]{:S(2)}) collective-permute-start(f32[2,1024,128]{2,1,0:T(8,128)S(1)} %get-tuple-element.78), channel_id=1, source_target_pairs={{0,32},{32,0},{64,96},{96,64},{128,160},{160,128},{192,224},{224,1... | collective-permute-start | bytes 3145736 | tf_op jit(solution)/shard_map/ppermute | solution.py:412
  156.0 5.1 %collective-permute-start.9 = (f32[2,1024,128]{2,1,0:T(8,128)S(1)}, f32[2,1024,128]{2,1,0:T(8,128)S(1)}, u32[]{:S(2)}, u32[]{:S(2)}) collective-permute-start(f32[2,1024,128]{2,1,0:T(8,128)S(1)} %get-tuple-element.81), channel_id=1, source_target_pairs={{0,32},{32,0},{64,96},{96,64},{128,160},{160,128},{192,224},{224,1... | collective-permute-start | bytes 3145736 | tf_op jit(solution)/shard_map/ppermute | solution.py:412

commit v6 on v5

--- a/solution.py
+++ b/solution.py
@@ -177,10 +177,15 @@
     return jnp.where(alone, 0.0, f_a[...] - from_a[...]), f_b[...] - from_b[...]
 
 
-def first_kernel(b, y_a, y_b, from_a, from_b, order, q_a, q_b, t_a, t_b, sums):
+def part_kernel(b, f_b, from_b, part):
+    half = f_b.shape[0]
+    part[...] = jnp.dot(b[:, half:], pair(f_b[...] - from_b[...]), preferred_element_type=F32)
+
+
+def first_kernel(b, part, y_a, y_b, from_a, from_b, order, q_a, q_b, t_a, t_b, sums):
     half = y_a.shape[0]
     r_a, r_b = jump(y_a, y_b, from_a, from_b)
-    wide = jnp.dot(b[...], jnp.concatenate([pair(r_a), pair(r_b)], axis=0), preferred_element_type=F32)
+    wide = part[...] + jnp.dot(b[:, :half], pair(r_a), preferred_element_type=F32)
     q = wide[:, :128]
     t = q + wide[:, 128:]
     q_a[...], q_b[...] = q[:half], q[half:]
@@ -190,10 +195,10 @@
     sums[...] = jnp.concatenate([rr, pw, order[2:]], axis=0)
 
 
-def second_kernel(b, q_a, q_b, from_a, from_b, sums, s_a, s_b, spread):
+def second_kernel(b, part, q_a, q_b, from_a, from_b, sums, s_a, s_b, spread):
     half = q_a.shape[0]
     w_a, w_b = jump(q_a, q_b, from_a, from_b)
-    wide = jnp.dot(b[...], jnp.concatenate([pair(w_a), pair(w_b)], axis=0), preferred_element_type=F32)
+    wide = part[...] + jnp.dot(b[:, :half], pair(w_a), preferred_element_type=F32)
     s = wide[:, :128] + wide[:, 128:]
     s_a[...], s_b[...] = s[:half], s[half:]
     ww = 0.5 * (add_up(w_a * w_a) + add_up(w_b * w_b))
@@ -329,6 +334,7 @@
     pairs = [[p for s in range(k, subs - 1, 2) for p in ((s, s + 1), (s + 1, s))] for k in (1, 0)]
     face = ((half, cases), F32)
     whole = ((size, cases), F32)
+    wide = ((size, 2 * cases), F32)
     small = ((8, cases), F32)
     square = ((size, size), BF16)
     once = 2 * size * size * cases
@@ -375,8 +381,9 @@
                     pltpu.SemaphoreType.DMA((3,)),
                 ],
             )
+        (part,) = call(part_kernel, "part", [wide], (matrix, y_b, from_b), once)
         q_a, q_b, t_a, t_b, sums = call(
-            first_kernel, "first", [face] * 4 + [small], (matrix, y_a, y_b, from_a, from_b, order), 2 * once
+            first_kernel, "first", [face] * 4 + [small], (matrix, part, y_a, y_b, from_a, from_b, order), once
         )
         from_a, from_b = exchange(q_a, q_b)
         if step == 0:
@@ -389,12 +396,13 @@
                 in_specs=[VMEM, VMEM, HBM, VMEM],
                 scratch=[pltpu.VMEM((1, size), F32), pltpu.SemaphoreType.DMA(())],
             )
+        (part,) = call(part_kernel, "part", [wide], (matrix, q_b, from_b), once)
         s_a, s_b, spread = call(
             second_kernel,
             "second",
             [face] * 2 + [((subs, 8, cases), F32)],
-            (matrix, q_a, q_b, from_a, from_b, sums),
-            2 * once,
+            (matrix, part, q_a, q_b, from_a, from_b, sums),
+            once,
         )
         gathered = lax.all_to_all(spread, "sub", 0, 0, axis_index_groups=[list(range(subs))[::-1]])
         fields = (gathered, y_a, y_b, q_a, q_b, t_a, t_b, s_a, s_b)

time: 163 us -> 160 us (0.982)
  starting transfers between devices: 31.5 us -> 23.7 us
  blocking collectives: 65 us -> 70 us
    ppermute x4, starting transfers between devices: 18.1 us -> 10.1 us  [exchange(): return (from_a, lax.ppermute(face_b, 'sub', pairs[1]))]
    all_to_all x2, blocking collectives: 31.1 us -> 36.1 us  [on_device(): lax.all_to_all(spread, 'sub', 0, 0, axis_index_groups=[list(range(subs))[...]
    pallas_call x14 -> x18, Pallas kernels: 38.9 us -> 39.6 us  [call(): pl.pallas_call(kernel, name=name, out_shape=[space(shape, dtype) for shap...]
  transfers between devices with their start and end apart: 10 -> 10, of which waited for: 6 -> 6; matrix products, arithmetic and copies ran while one was open for 0% -> 0% of each run, Pallas kernels for 9% -> 12%
where the time goes in v6:
time: 160 us
  blocking collectives  70 us (44%)
  Pallas kernels  39.6 us (25%)
  waiting for transfers between devices  25.4 us (16%)
  starting transfers between devices  23.7 us (15%)
    pallas_call x18, Pallas kernels, call(): pl.pallas_call(kernel, name=name, out_shape=[space(shape, dtype) for shap...  39.6 us
    all_to_all x2, blocking collectives, on_device(): lax.all_to_all(spread, 'sub', 0, 0, axis_index_groups=[list(range(subs))[...  36.1 us
    ppermute x4, waiting for transfers between devices, exchange(): return (from_a, lax.ppermute(face_b, 'sub', pairs[1]))  20.8 us
    all_to_all x1, blocking collectives, on_device(): parts = lax.all_to_all(parts, 'tm', 0, 0, axis_index_groups=groups)  18.2 us
    all_to_all x1, blocking collectives, on_device(): states = lax.all_to_all(states, 'tm', 0, 0, axis_index_groups=groups)  15.7 us
    ppermute x2, starting transfers between devices, swap(): return lax.ppermute(value, 'tm', [(t, t ^ 1) for t in range(slices)])  10.7 us
    ppermute x4, starting transfers between devices, exchange(): return (from_a, lax.ppermute(face_b, 'sub', pairs[1]))  10.1 us
    ppermute x2, waiting for transfers between devices, swap(): return lax.ppermute(value, 'tm', [(t, t ^ 1) for t in range(slices)])  4.57 us
  transfers between devices with their start and end apart: 10, of which 6 were waited for; matrix products, arithmetic and copies ran while one was open for 0% of the time, Pallas kernels for 12%

profile of v6, /device:TPU:1, one launch (start us, length us, event | category | flops | bytes accessed | tf_op | source)
XLA Modules:
  0.0 159.5 jit_solution(5200125656782790010)
XLA Ops:
  0.6 7.5 %start.1 = (bf16[2048,2048]{1,0:T(8,128)(2,1)S(1)}, bf16[1024,1024]{1,0:T(8,128)(2,1)S(1)}, f32[1024,128]{1,0:T(8,128)S(1)}, f32[1024,128]{1,0:T(8,128)S(1)}, f3...) custom-call(bf16[2048,2048]{1,0:T(8,128)(2,1)} %bitcast.6, f32[2048,128]{1,0:T(8,128)} %bitcast.7, f32[2048,128]{1,0:T(8,128)} %bitcast.9, ...), custom_call_target="tpu_custom_call" | custom-call | flops 1073741824 | bytes 11022336 | tf_op jit(solution)/shard_map/start/pallas_call | solution.py:17
  8.2 0.7 collective-permute-start.1
  8.9 5.6 %collective-permute-start = (f32[1024,128]{1,0:T(8,128)S(1)}, f32[1024,128]{1,0:T(8,128)S(1)}, u32[]{:S(2)}, u32[]{:S(2)}) collective-permute-start(f32[1024,128]{1,0:T(8,128)S(1)} %get-tuple-element.46.f_b.y_b), channel_id=1, source_target_pairs={{0,1},{1,0},{2,3},{3,2},{4,5},{5,4},{6,7},{7,6},{8,9},{9,8},{10,11... | collective-permute-start | bytes 1572872 | tf_op jit(solution)/shard_map/ppermute | solution.py:344
  14.5 9.0 %prepare.1 = (bf16[2048,2048]{1,0:T(8,128)(2,1)S(1)}, f32[8,128]{1,0:T(8,128)S(1)}) custom-call(bf16[2048,2048]{1,0:T(8,128)(2,1)S(1)} %get-tuple-element.44.a, bf16[1024,1024]{1,0:T(8,128)(2,1)S(1)} %get-tuple-element.43.onehot), custom_call_target="tpu_custom_call" | custom-call | flops 8589934592 | bytes 10485760 | tf_op jit(solution)/shard_map/prepare/pallas_call | solution.py:17
  23.5 2.3 %collective-permute-done.from_b = f32[1024,128]{1,0:T(8,128)S(1)} collective-permute-done((f32[1024,128]{1,0:T(8,128)S(1)}, f32[1024,128]{1,0:T(8,128)S(1)}, u32[]{:S(2)}, u32[]{:S(2)}) %collective-permute-start) | collective-permute-done | bytes 524320 | tf_op jit(solution)/shard_map/ppermute | solution.py:344
  25.8 1.3 part.4
  27.1 0.0 collective-permute-done.1.from_a
  27.1 1.4 first.2
  28.5 1.2 collective-permute-start.2
  29.7 0.9 collective-permute-start.3
  30.6 2.1 %ready.1 = (f32[2048,128]{1,0:T(8,128)S(1)}, f32[2048,128]{1,0:T(8,128)S(1)}, f32[8,128]{1,0:T(8,128)S(1)}) custom-call(bf16[1024,1024]{1,0:T(8,128)(2,1)S(1)} %get-tuple-element.43.onehot, f32[2048,128]{1,0:T(8,128)S(1)} %get-tuple-element.51.force, f32[1,2048]{1,0:T(1,128)} %mass_in.3, f32[8,128]{1,0:T(8,128)S(1)} %get-tuple-element.52.sums_in), custom_call_target="tpu_custom_call" | custom-call | flops 1073741824 | bytes 3158016 | tf_op jit(solution)/shard_map/ready/pallas_call | solution.py:17
  32.8 7.7 %collective-permute-done.2.from_b = f32[1024,128]{1,0:T(8,128)S(1)} collective-permute-done((f32[1024,128]{1,0:T(8,128)S(1)}, f32[1024,128]{1,0:T(8,128)S(1)}, u32[]{:S(2)}, u32[]{:S(2)}) %collective-permute-start.2) | collective-permute-done | bytes 524320 | tf_op jit(solution)/shard_map/ppermute | solution.py:344
  40.4 1.3 part.5
  41.7 0.0 collective-permute-done.3.from_a
  41.7 1.4 second.2
  43.1 19.3 %all_to_all.20.gathered = f32[32,8,128]{2,1,0:T(8,128)S(1)} all-to-all(f32[32,8,128]{2,1,0:T(8,128)S(1)} %get-tuple-element.54), channel_id=1, replica_groups={{31,30,29,28,27,26,25,24,23,22,21,20,19,18,17,16,15,14,13,12,11,10,9,8,..., dimensions={0} | all-to-all | bytes 262144 | tf_op jit(solution)/shard_map/all_to_all | solution.py:407
  62.4 2.5 %next.1 = (f32[1024,128]{1,0:T(8,128)S(1)}, f32[1024,128]{1,0:T(8,128)S(1)}, f32[1024,128]{1,0:T(8,128)S(1)}, f32[1024,128]{1,0:T(8,128)S(1)}) custom-call(bf16[2048,2048]{1,0:T(8,128)(2,1)S(1)} %get-tuple-element.45.b, f32[32,8,128]{2,1,0:T(8,128)S(1)} %all_to_all.20.gathered, f32[1024,128]{1,0:T(8,128)S(1)} %get-tuple-element.47.y_a, ...), custom_call_target="tpu_custom_call" | custom-call | flops 1073741824 | bytes 14811136 | tf_op jit(solution)/shard_map/next/pallas_call | solution.py:17
  65.0 1.1 collective-permute-start.4
  66.1 0.7 collective-permute-start.5
  66.8 3.4 %early.1 = (f32[2048,128]{1,0:T(8,128)S(1)}, f32[2048,128]{1,0:T(8,128)S(1)}, f32[1024,128]{1,0:T(8,128)S(1)}, f32[8,128]{1,0:T(8,128)S(1)}) custom-call(bf16[1024,1024]{1,0:T(8,128)(2,1)S(1)} %get-tuple-element.43.onehot, f32[1024,128]{1,0:T(8,128)S(1)} %get-tuple-element.63.u_a, f32[1024,128]{1,0:T(8,128)S(1)} %get-tuple-element.64.u_b, ...), custom_call_target="tpu_custom_call" | custom-call | flops 805306368 | bytes 6299648 | tf_op jit(solution)/shard_map/early/pallas_call | solution.py:17
  70.2 4.4 %collective-permute-done.4.from_b = f32[1024,128]{1,0:T(8,128)S(1)} collective-permute-done((f32[1024,128]{1,0:T(8,128)S(1)}, f32[1024,128]{1,0:T(8,128)S(1)}, u32[]{:S(2)}, u32[]{:S(2)}) %collective-permute-start.4) | collective-permute-done | bytes 524320 | tf_op jit(solution)/shard_map/ppermute | solution.py:344
  74.6 1.3 part.6
  75.9 0.0 collective-permute-done.5.from_a
  75.9 1.4 first.3
  77.2 2.1 %collective-permute-start.6 = (f32[1024,128]{1,0:T(8,128)S(1)}, f32[1024,128]{1,0:T(8,128)S(1)}, u32[]{:S(2)}, u32[]{:S(2)}) collective-permute-start(f32[1024,128]{1,0:T(8,128)S(1)} %get-tuple-element.67.f_b.q_b), channel_id=1, source_target_pairs={{0,1},{1,0},{2,3},{3,2},{4,5},{5,4},{6,7},{7,6},{8,9},{9,8},{10,11... | collective-permute-start | bytes 1572872 | tf_op jit(solution)/shard_map/ppermute | solution.py:344
  79.4 0.7 collective-permute-start.7
  80.1 6.5 %collective-permute-done.6.from_b = f32[1024,128]{1,0:T(8,128)S(1)} collective-permute-done((f32[1024,128]{1,0:T(8,128)S(1)}, f32[1024,128]{1,0:T(8,128)S(1)}, u32[]{:S(2)}, u32[]{:S(2)}) %collective-permute-start.6) | collective-permute-done | bytes 524320 | tf_op jit(solution)/shard_map/ppermute | solution.py:344
  86.5 1.3 part.7
  87.8 0.0 collective-permute-done.7.from_a
  87.8 1.4 second.3
  89.3 16.8 %all_to_all.21.gathered = f32[32,8,128]{2,1,0:T(8,128)S(1)} all-to-all(f32[32,8,128]{2,1,0:T(8,128)S(1)} %get-tuple-element.70), channel_id=1, replica_groups={{31,30,29,28,27,26,25,24,23,22,21,20,19,18,17,16,15,14,13,12,11,10,9,8,..., dimensions={0} | all-to-all | bytes 262144 | tf_op jit(solution)/shard_map/all_to_all | solution.py:407
  106.1 1.4 finish.1
  107.5 7.8 %collective-permute-start.8 = (f32[2,1024,128]{2,1,0:T(8,128)S(1)}, f32[2,1024,128]{2,1,0:T(8,128)S(1)}, u32[]{:S(2)}, u32[]{:S(2)}) collective-permute-start(f32[2,1024,128]{2,1,0:T(8,128)S(1)} %get-tuple-element.78), channel_id=1, source_target_pairs={{0,32},{32,0},{64,96},{96,64},{128,160},{160,128},{192,224},{224,1... | collective-permute-start | bytes 3145736 | tf_op jit(solution)/shard_map/ppermute | solution.py:420
  115.3 2.3 %collective-permute-done.8.got = f32[2,1024,128]{2,1,0:T(8,128)S(1)} collective-permute-done((f32[2,1024,128]{2,1,0:T(8,128)S(1)}, f32[2,1024,128]{2,1,0:T(8,128)S(1)}, u32[]{:S(2)}, u32[]{:S(2)}) %collective-permute-start.8) | collective-permute-done | bytes 1048608 | tf_op jit(solution)/shard_map/ppermute | solution.py:420
  117.6 0.4 combine.1
  118.0 18.2 %all_to_all.22.blocks = f32[4,2,256,128]{3,2,1,0:T(8,128)S(1)} all-to-all(f32[4,2,256,128]{3,2,1,0:T(8,128)S(1)} %combine.1), channel_id=1, replica_groups={{0,64,128,192},{32,96,160,224},{1,65,129,193},{33,97,161,225},{2,66,130..., dimensions={0} | all-to-all | bytes 2097152 | tf_op jit(solution)/shard_map/all_to_all | solution.py:425
  136.2 0.3 prefix.1
  136.5 15.7 %all_to_all.23.states = f32[4,2,256,128]{3,2,1,0:T(8,128)S(1)} all-to-all(f32[4,2,256,128]{3,2,1,0:T(8,128)S(1)} %prefix.1), channel_id=1, replica_groups={{0,64,128,192},{32,96,160,224},{1,65,129,193},{33,97,161,225},{2,66,130..., dimensions={0} | all-to-all | bytes 2097152 | tf_op jit(solution)/shard_map/all_to_all | solution.py:427
  152.2 0.7 end.1
  152.9 2.8 %collective-permute-start.9 = (f32[2,1024,128]{2,1,0:T(8,128)S(1)}, f32[2,1024,128]{2,1,0:T(8,128)S(1)}, u32[]{:S(2)}, u32[]{:S(2)}) collective-permute-start(f32[2,1024,128]{2,1,0:T(8,128)S(1)} %get-tuple-element.81), channel_id=1, source_target_pairs={{0,32},{32,0},{64,96},{96,64},{128,160},{160,128},{192,224},{224,1... | collective-permute-start | bytes 3145736 | tf_op jit(solution)/shard_map/ppermute | solution.py:420
  155.7 2.3 %collective-permute-done.9.got = f32[2,1024,128]{2,1,0:T(8,128)S(1)} collective-permute-done((f32[2,1024,128]{2,1,0:T(8,128)S(1)}, f32[2,1024,128]{2,1,0:T(8,128)S(1)}, u32[]{:S(2)}, u32[]{:S(2)}) %collective-permute-start.9) | collective-permute-done | bytes 1048608 | tf_op jit(solution)/shard_map/ppermute | solution.py:420
  158.0 1.5 join.1
Async XLA Ops:
  8.2 18.9 %collective-permute-start.1 = (f32[1024,128]{1,0:T(8,128)S(1)}, f32[1024,128]{1,0:T(8,128)S(1)}, u32[]{:S(2)}, u32[]{:S(2)}) collective-permute-start(f32[1024,128]{1,0:T(8,128)S(1)} %get-tuple-element.47.y_a), channel_id=1, source_target_pairs={{1,2},{2,1},{3,4},{4,3},{5,6},{6,5},{7,8},{8,7},{9,10},{10,9},{11,... | collective-permute-start | bytes 1572872 | tf_op jit(solution)/shard_map/ppermute | solution.py:343
  8.9 16.9 %collective-permute-start = (f32[1024,128]{1,0:T(8,128)S(1)}, f32[1024,128]{1,0:T(8,128)S(1)}, u32[]{:S(2)}, u32[]{:S(2)}) collective-permute-start(f32[1024,128]{1,0:T(8,128)S(1)} %get-tuple-element.46.f_b.y_b), channel_id=1, source_target_pairs={{0,1},{1,0},{2,3},{3,2},{4,5},{5,4},{6,7},{7,6},{8,9},{9,8},{10,11... | collective-permute-start | bytes 1572872 | tf_op jit(solution)/shard_map/ppermute | solution.py:344
  28.5 12.0 %collective-permute-start.2 = (f32[1024,128]{1,0:T(8,128)S(1)}, f32[1024,128]{1,0:T(8,128)S(1)}, u32[]{:S(2)}, u32[]{:S(2)}) collective-permute-start(f32[1024,128]{1,0:T(8,128)S(1)} %get-tuple-element.49.f_b.q_b), channel_id=1, source_target_pairs={{0,1},{1,0},{2,3},{3,2},{4,5},{5,4},{6,7},{7,6},{8,9},{9,8},{10,11... | collective-permute-start | bytes 1572872 | tf_op jit(solution)/shard_map/ppermute | solution.py:344
  29.7 12.0 %collective-permute-start.3 = (f32[1024,128]{1,0:T(8,128)S(1)}, f32[1024,128]{1,0:T(8,128)S(1)}, u32[]{:S(2)}, u32[]{:S(2)}) collective-permute-start(f32[1024,128]{1,0:T(8,128)S(1)} %get-tuple-element.50.q_a), channel_id=1, source_target_pairs={{1,2},{2,1},{3,4},{4,3},{5,6},{6,5},{7,8},{8,7},{9,10},{10,9},{11,... | collective-permute-start | bytes 1572872 | tf_op jit(solution)/shard_map/ppermute | solution.py:343
  65.0 9.6 %collective-permute-start.4 = (f32[1024,128]{1,0:T(8,128)S(1)}, f32[1024,128]{1,0:T(8,128)S(1)}, u32[]{:S(2)}, u32[]{:S(2)}) collective-permute-start(f32[1024,128]{1,0:T(8,128)S(1)} %get-tuple-element.61.f_b.y_b), channel_id=1, source_target_pairs={{0,1},{1,0},{2,3},{3,2},{4,5},{5,4},{6,7},{7,6},{8,9},{9,8},{10,11... | collective-permute-start | bytes 1572872 | tf_op jit(solution)/shard_map/ppermute | solution.py:344
  66.1 9.8 %collective-permute-start.5 = (f32[1024,128]{1,0:T(8,128)S(1)}, f32[1024,128]{1,0:T(8,128)S(1)}, u32[]{:S(2)}, u32[]{:S(2)}) collective-permute-start(f32[1024,128]{1,0:T(8,128)S(1)} %get-tuple-element.62.y_a), channel_id=1, source_target_pairs={{1,2},{2,1},{3,4},{4,3},{5,6},{6,5},{7,8},{8,7},{9,10},{10,9},{11,... | collective-permute-start | bytes 1572872 | tf_op jit(solution)/shard_map/ppermute | solution.py:343
  77.2 9.3 %collective-permute-start.6 = (f32[1024,128]{1,0:T(8,128)S(1)}, f32[1024,128]{1,0:T(8,128)S(1)}, u32[]{:S(2)}, u32[]{:S(2)}) collective-permute-start(f32[1024,128]{1,0:T(8,128)S(1)} %get-tuple-element.67.f_b.q_b), channel_id=1, source_target_pairs={{0,1},{1,0},{2,3},{3,2},{4,5},{5,4},{6,7},{7,6},{8,9},{9,8},{10,11... | collective-permute-start | bytes 1572872 | tf_op jit(solution)/shard_map/ppermute | solution.py:344
  79.4 8.4 %collective-permute-start.7 = (f32[1024,128]{1,0:T(8,128)S(1)}, f32[1024,128]{1,0:T(8,128)S(1)}, u32[]{:S(2)}, u32[]{:S(2)}) collective-permute-start(f32[1024,128]{1,0:T(8,128)S(1)} %get-tuple-element.68.q_a), channel_id=1, source_target_pairs={{1,2},{2,1},{3,4},{4,3},{5,6},{6,5},{7,8},{8,7},{9,10},{10,9},{11,... | collective-permute-start | bytes 1572872 | tf_op jit(solution)/shard_map/ppermute | solution.py:343
  107.5 10.1 %collective-permute-start.8 = (f32[2,1024,128]{2,1,0:T(8,128)S(1)}, f32[2,1024,128]{2,1,0:T(8,128)S(1)}, u32[]{:S(2)}, u32[]{:S(2)}) collective-permute-start(f32[2,1024,128]{2,1,0:T(8,128)S(1)} %get-tuple-element.78), channel_id=1, source_target_pairs={{0,32},{32,0},{64,96},{96,64},{128,160},{160,128},{192,224},{224,1... | collective-permute-start | bytes 3145736 | tf_op jit(solution)/shard_map/ppermute | solution.py:420
  152.9 5.1 %collective-permute-start.9 = (f32[2,1024,128]{2,1,0:T(8,128)S(1)}, f32[2,1024,128]{2,1,0:T(8,128)S(1)}, u32[]{:S(2)}, u32[]{:S(2)}) collective-permute-start(f32[2,1024,128]{2,1,0:T(8,128)S(1)} %get-tuple-element.81), channel_id=1, source_target_pairs={{0,32},{32,0},{64,96},{96,64},{128,160},{160,128},{192,224},{224,1... | collective-permute-start | bytes 3145736 | tf_op jit(solution)/shard_map/ppermute | solution.py:420

commit v7 on v6

--- a/solution.py
+++ b/solution.py
@@ -12,15 +12,16 @@
 CHUNKS = 8
 
 
-def call(kernel, name, outs, args, flops=0, in_specs=None, scratch=(), limit=12, space=pltpu.VMEM):
-    moved = sum(a.size * a.dtype.itemsize for a in args)
+def call(kernel, name, outs, args, flops=0, moved=None, in_specs=None, scratch=(), limit=12, in_hbm=False, aliases=None):
+    moved = moved or sum(a.size * a.dtype.itemsize for a in args)
     return pl.pallas_call(
         kernel,
         name=name,
-        out_shape=[space(shape, dtype) for shape, dtype in outs],
+        out_shape=[(jax.ShapeDtypeStruct if in_hbm else pltpu.VMEM)(shape, dtype) for shape, dtype in outs],
         in_specs=in_specs or [VMEM] * len(args),
-        out_specs=[VMEM] * len(outs),
+        out_specs=[HBM if in_hbm else VMEM] * len(outs),
         scratch_shapes=scratch,
+        input_output_aliases=aliases or {},
         compiler_params=pltpu.CompilerParams(vmem_limit_bytes=limit * 2**20),
         cost_estimate=pl.CostEstimate(flops=flops, bytes_accessed=moved, transcendentals=0),
     )(*args)
@@ -102,13 +103,13 @@
         pltpu.make_async_copy(a_in.at[pl.ds(k * rows, rows)], a.at[pl.ds(k * rows, rows)], a_sem.at[k])
         for k in range(CHUNKS)
     ]
-    for copy in small:
+    for copy in small + big[:2]:
         copy.start()
     small[0].wait()
     onehot[...] = (lax.broadcasted_iota(jnp.int32, (half, half), 0) == perm[...]).astype(F32).astype(BF16)
     for copy in small[1:]:
         copy.wait()
-    for copy in big:
+    for copy in big[2:]:
         copy.start()
     weight = 2.0 * column(mass[...])
     outer = load[...].astype(F32)
@@ -203,7 +204,7 @@
     s_a[...], s_b[...] = s[:half], s[half:]
     ww = 0.5 * (add_up(w_a * w_a) + add_up(w_b * w_b))
     wfw = add_up(w_a * s[:half]) + add_up(w_b * s[half:])
-    own = jnp.concatenate([sums[:2], ww, wfw, jnp.zeros((4, 128), F32)], axis=0)
+    own = jnp.concatenate([sums[:2], ww, wfw], axis=0)
     spread[...] = jnp.broadcast_to(own[None], spread.shape)
 
 
@@ -315,12 +316,24 @@
         give[k] = jnp.where(even, second[k], first[k])
 
 
-def join_kernel(stay, got, end_u, end_v):
-    even = lax.axis_index("tm") % 2 == 0
-    half = stay.shape[1]
-    for k, out in enumerate([end_u, end_v]):
-        out[:half] = jnp.where(even, stay[k], got[k])
-        out[half:] = jnp.where(even, got[k], stay[k])
+def copy_half(source, outs, start, sem):
+    half = source.shape[1]
+    place = pl.ds(pl.multiple_of(start, half), half)
+    copies = [pltpu.make_async_copy(source.at[k], out.at[place], sem.at[k]) for k, out in enumerate(outs)]
+    for copy in copies:
+        copy.start()
+    for copy in copies:
+        copy.wait()
+
+
+def keep_kernel(stay, end_u, end_v, sem):
+    core = lax.rem(lax.axis_index("tm"), 2)
+    copy_half(stay, [end_u, end_v], core * stay.shape[1], sem)
+
+
+def join_kernel(got, in_u, in_v, end_u, end_v, sem):
+    core = lax.rem(lax.axis_index("tm"), 2)
+    copy_half(got, [end_u, end_v], (1 - core) * got.shape[1], sem)
 
 
 def on_device(flex, mass, coarse_rate, face_perm, start_u, start_v, load):
@@ -364,7 +377,7 @@
         from_a, from_b = exchange(y_a, y_b)
         if step == 0:
             matrix, order = call(
-                prepare_kernel, "prepare", [square, small], (a, onehot), 8 * half**3, scratch=[pltpu.VMEM((half, half), BF16)]
+                prepare_kernel, "prepare", [square, small], (a, onehot), once, moved=half * cases, scratch=[pltpu.VMEM((half, half), BF16)]
             )
         else:
             early_u, early_v, rate_own, order = call(
@@ -400,7 +413,7 @@
         s_a, s_b, spread = call(
             second_kernel,
             "second",
-            [face] * 2 + [((subs, 8, cases), F32)],
+            [face] * 2 + [((subs, 4, cases), F32)],
             (matrix, part, q_a, q_b, from_a, from_b, sums),
             once,
         )
@@ -426,7 +439,12 @@
     (states,) = call(prefix_kernel, "prefix", [blocks], (parts, rate_own), light)
     states = lax.all_to_all(states, "tm", 0, 0, axis_index_groups=groups)
     stay, give = call(end_kernel, "end", [two, two], (states, own, got, rate_own), light)
-    end_u, end_v = call(join_kernel, "join", [whole, whole], (stay, swap(give)), light, space=jax.ShapeDtypeStruct)
+    got = swap(give)
+    ends = dict(in_hbm=True, scratch=[pltpu.SemaphoreType.DMA((2,))])
+    end_u, end_v = call(keep_kernel, "keep", [whole] * 2, (stay,), **ends)
+    end_u, end_v = call(
+        join_kernel, "join", [whole] * 2, (got, end_u, end_v), in_specs=[VMEM, HBM, HBM], aliases={1: 0, 2: 1}, **ends
+    )
     return end_u[None, None], end_v[None, None]
 
 

time: 160 us -> 156 us (0.975)
  waiting for transfers between devices: 25.4 us -> 22 us
    ppermute x4, waiting for transfers between devices: 20.8 us -> 18.4 us  [exchange(): return (from_a, lax.ppermute(face_b, 'sub', pairs[1]))]
    pallas_call x18 -> x19, Pallas kernels: 39.6 us -> 39.6 us  [call(): pl.pallas_call(kernel, name=name, out_shape=[(jax.ShapeDtypeStruct if in_...]
  transfers between devices with their start and end apart: 10 -> 10, of which waited for: 6 -> 6; matrix products, arithmetic and copies ran while one was open for 0% -> 0% of each run, Pallas kernels for 12% -> 13%
where the time goes in v7:
time: 156 us
  blocking collectives  69.3 us (44%)
  Pallas kernels  39.6 us (25%)
  starting transfers between devices  24.1 us (15%)
  waiting for transfers between devices  22 us (14%)
    pallas_call x19, Pallas kernels, call(): pl.pallas_call(kernel, name=name, out_shape=[(jax.ShapeDtypeStruct if in_...  39.6 us
    all_to_all x2, blocking collectives, on_device(): lax.all_to_all(spread, 'sub', 0, 0, axis_index_groups=[list(range(subs))[...  35.3 us
    ppermute x4, waiting for transfers between devices, exchange(): return (from_a, lax.ppermute(face_b, 'sub', pairs[1]))  18.4 us
    all_to_all x1, blocking collectives, on_device(): parts = lax.all_to_all(parts, 'tm', 0, 0, axis_index_groups=groups)  18.3 us
    all_to_all x1, blocking collectives, on_device(): states = lax.all_to_all(states, 'tm', 0, 0, axis_index_groups=groups)  15.7 us
    ppermute x2, starting transfers between devices, swap(): return lax.ppermute(value, 'tm', [(t, t ^ 1) for t in range(slices)])  10.7 us
    ppermute x4, starting transfers between devices, exchange(): return (from_a, lax.ppermute(face_b, 'sub', pairs[1]))  10.3 us
    ppermute x2, waiting for transfers between devices, swap(): return lax.ppermute(value, 'tm', [(t, t ^ 1) for t in range(slices)])  3.58 us
  transfers between devices with their start and end apart: 10, of which 6 were waited for; matrix products, arithmetic and copies ran while one was open for 0% of the time, Pallas kernels for 13%

profile of v7, /device:TPU:1, one launch (start us, length us, event | category | flops | bytes accessed | tf_op | source)
XLA Modules:
  0.0 155.9 jit_solution(11592734490695510841)
XLA Ops:
  0.6 7.1 %start.1 = (bf16[2048,2048]{1,0:T(8,128)(2,1)S(1)}, bf16[1024,1024]{1,0:T(8,128)(2,1)S(1)}, f32[1024,128]{1,0:T(8,128)S(1)}, f32[1024,128]{1,0:T(8,128)S(1)}, f3...) custom-call(bf16[2048,2048]{1,0:T(8,128)(2,1)} %bitcast.6, f32[2048,128]{1,0:T(8,128)} %bitcast.7, f32[2048,128]{1,0:T(8,128)} %bitcast.9, ...), custom_call_target="tpu_custom_call" | custom-call | flops 1073741824 | bytes 11022336 | tf_op jit(solution)/shard_map/start/pallas_call | solution.py:17
  7.7 2.6 %collective-permute-start = (f32[1024,128]{1,0:T(8,128)S(1)}, f32[1024,128]{1,0:T(8,128)S(1)}, u32[]{:S(2)}, u32[]{:S(2)}) collective-permute-start(f32[1024,128]{1,0:T(8,128)S(1)} %get-tuple-element.48.f_b.y_b), channel_id=1, source_target_pairs={{0,1},{1,0},{2,3},{3,2},{4,5},{5,4},{6,7},{7,6},{8,9},{9,8},{10,11... | collective-permute-start | bytes 1572872 | tf_op jit(solution)/shard_map/ppermute | solution.py:357
  10.3 0.9 collective-permute-start.1
  11.2 9.0 %prepare.1 = (bf16[2048,2048]{1,0:T(8,128)(2,1)S(1)}, f32[8,128]{1,0:T(8,128)S(1)}) custom-call(bf16[2048,2048]{1,0:T(8,128)(2,1)S(1)} %get-tuple-element.46.a, bf16[1024,1024]{1,0:T(8,128)(2,1)S(1)} %get-tuple-element.45.onehot), custom_call_target="tpu_custom_call" | custom-call | flops 1073741824 | bytes 131072 | tf_op jit(solution)/shard_map/prepare/pallas_call | solution.py:17
  20.2 0.7 collective-permute-done.from_b
  20.9 1.3 part.4
  22.2 0.0 collective-permute-done.1.from_a
  22.2 1.4 first.2
  23.6 4.7 %collective-permute-start.2 = (f32[1024,128]{1,0:T(8,128)S(1)}, f32[1024,128]{1,0:T(8,128)S(1)}, u32[]{:S(2)}, u32[]{:S(2)}) collective-permute-start(f32[1024,128]{1,0:T(8,128)S(1)} %get-tuple-element.51.f_b.q_b), channel_id=1, source_target_pairs={{0,1},{1,0},{2,3},{3,2},{4,5},{5,4},{6,7},{7,6},{8,9},{9,8},{10,11... | collective-permute-start | bytes 1572872 | tf_op jit(solution)/shard_map/ppermute | solution.py:357
  28.2 0.9 collective-permute-start.3
  29.1 2.1 %ready.1 = (f32[2048,128]{1,0:T(8,128)S(1)}, f32[2048,128]{1,0:T(8,128)S(1)}, f32[8,128]{1,0:T(8,128)S(1)}) custom-call(bf16[1024,1024]{1,0:T(8,128)(2,1)S(1)} %get-tuple-element.45.onehot, f32[2048,128]{1,0:T(8,128)S(1)} %get-tuple-element.53.force, f32[1,2048]{1,0:T(1,128)} %mass_in.3, f32[8,128]{1,0:T(8,128)S(1)} %get-tuple-element.54.sums_in), custom_call_target="tpu_custom_call" | custom-call | flops 1073741824 | bytes 3158016 | tf_op jit(solution)/shard_map/ready/pallas_call | solution.py:17
  31.3 7.6 %collective-permute-done.2.from_b = f32[1024,128]{1,0:T(8,128)S(1)} collective-permute-done((f32[1024,128]{1,0:T(8,128)S(1)}, f32[1024,128]{1,0:T(8,128)S(1)}, u32[]{:S(2)}, u32[]{:S(2)}) %collective-permute-start.2) | collective-permute-done | bytes 524320 | tf_op jit(solution)/shard_map/ppermute | solution.py:357
  38.9 1.3 part.5
  40.2 0.0 collective-permute-done.3.from_a
  40.2 1.4 second.2
  41.6 17.9 %all_to_all.20.gathered = f32[32,4,128]{2,1,0:T(4,128)S(1)} all-to-all(f32[32,4,128]{2,1,0:T(4,128)S(1)} %get-tuple-element.56), channel_id=1, replica_groups={{31,30,29,28,27,26,25,24,23,22,21,20,19,18,17,16,15,14,13,12,11,10,9,8,..., dimensions={0} | all-to-all | bytes 131072 | tf_op jit(solution)/shard_map/all_to_all | solution.py:420
  59.5 2.5 %next.1 = (f32[1024,128]{1,0:T(8,128)S(1)}, f32[1024,128]{1,0:T(8,128)S(1)}, f32[1024,128]{1,0:T(8,128)S(1)}, f32[1024,128]{1,0:T(8,128)S(1)}) custom-call(bf16[2048,2048]{1,0:T(8,128)(2,1)S(1)} %get-tuple-element.47.b, f32[32,4,128]{2,1,0:T(4,128)S(1)} %all_to_all.20.gathered, f32[1024,128]{1,0:T(8,128)S(1)} %get-tuple-element.49.y_a, ...), custom_call_target="tpu_custom_call" | custom-call | flops 1073741824 | bytes 14745600 | tf_op jit(solution)/shard_map/next/pallas_call | solution.py:17
  62.0 1.0 collective-permute-start.4
  63.0 0.7 collective-permute-start.5
  63.7 3.4 %early.1 = (f32[2048,128]{1,0:T(8,128)S(1)}, f32[2048,128]{1,0:T(8,128)S(1)}, f32[1024,128]{1,0:T(8,128)S(1)}, f32[8,128]{1,0:T(8,128)S(1)}) custom-call(bf16[1024,1024]{1,0:T(8,128)(2,1)S(1)} %get-tuple-element.45.onehot, f32[1024,128]{1,0:T(8,128)S(1)} %get-tuple-element.65.u_a, f32[1024,128]{1,0:T(8,128)S(1)} %get-tuple-element.66.u_b, ...), custom_call_target="tpu_custom_call" | custom-call | flops 805306368 | bytes 6299648 | tf_op jit(solution)/shard_map/early/pallas_call | solution.py:17
  67.1 4.2 %collective-permute-done.4.from_b = f32[1024,128]{1,0:T(8,128)S(1)} collective-permute-done((f32[1024,128]{1,0:T(8,128)S(1)}, f32[1024,128]{1,0:T(8,128)S(1)}, u32[]{:S(2)}, u32[]{:S(2)}) %collective-permute-start.4) | collective-permute-done | bytes 524320 | tf_op jit(solution)/shard_map/ppermute | solution.py:357
  71.3 1.3 part.6
  72.6 0.0 collective-permute-done.5.from_a
  72.6 1.4 first.3
  74.0 2.1 %collective-permute-start.6 = (f32[1024,128]{1,0:T(8,128)S(1)}, f32[1024,128]{1,0:T(8,128)S(1)}, u32[]{:S(2)}, u32[]{:S(2)}) collective-permute-start(f32[1024,128]{1,0:T(8,128)S(1)} %get-tuple-element.69.f_b.q_b), channel_id=1, source_target_pairs={{0,1},{1,0},{2,3},{3,2},{4,5},{5,4},{6,7},{7,6},{8,9},{9,8},{10,11... | collective-permute-start | bytes 1572872 | tf_op jit(solution)/shard_map/ppermute | solution.py:357
  76.1 0.7 collective-permute-start.7
  76.8 5.9 %collective-permute-done.6.from_b = f32[1024,128]{1,0:T(8,128)S(1)} collective-permute-done((f32[1024,128]{1,0:T(8,128)S(1)}, f32[1024,128]{1,0:T(8,128)S(1)}, u32[]{:S(2)}, u32[]{:S(2)}) %collective-permute-start.6) | collective-permute-done | bytes 524320 | tf_op jit(solution)/shard_map/ppermute | solution.py:357
  82.7 1.3 part.7
  84.0 0.0 collective-permute-done.7.from_a
  84.0 1.4 second.3
  85.4 17.3 %all_to_all.21.gathered = f32[32,4,128]{2,1,0:T(4,128)S(1)} all-to-all(f32[32,4,128]{2,1,0:T(4,128)S(1)} %get-tuple-element.72), channel_id=1, replica_groups={{31,30,29,28,27,26,25,24,23,22,21,20,19,18,17,16,15,14,13,12,11,10,9,8,..., dimensions={0} | all-to-all | bytes 131072 | tf_op jit(solution)/shard_map/all_to_all | solution.py:420
  102.7 1.4 finish.1
  104.1 7.8 %collective-permute-start.8 = (f32[2,1024,128]{2,1,0:T(8,128)S(1)}, f32[2,1024,128]{2,1,0:T(8,128)S(1)}, u32[]{:S(2)}, u32[]{:S(2)}) collective-permute-start(f32[2,1024,128]{2,1,0:T(8,128)S(1)} %get-tuple-element.80), channel_id=1, source_target_pairs={{0,32},{32,0},{64,96},{96,64},{128,160},{160,128},{192,224},{224,1... | collective-permute-start | bytes 3145736 | tf_op jit(solution)/shard_map/ppermute | solution.py:433
  112.0 2.3 %collective-permute-done.8.got = f32[2,1024,128]{2,1,0:T(8,128)S(1)} collective-permute-done((f32[2,1024,128]{2,1,0:T(8,128)S(1)}, f32[2,1024,128]{2,1,0:T(8,128)S(1)}, u32[]{:S(2)}, u32[]{:S(2)}) %collective-permute-start.8) | collective-permute-done | bytes 1048608 | tf_op jit(solution)/shard_map/ppermute | solution.py:433
  114.3 0.4 combine.1
  114.7 18.3 %all_to_all.22.blocks = f32[4,2,256,128]{3,2,1,0:T(8,128)S(1)} all-to-all(f32[4,2,256,128]{3,2,1,0:T(8,128)S(1)} %combine.1), channel_id=1, replica_groups={{0,64,128,192},{32,96,160,224},{1,65,129,193},{33,97,161,225},{2,66,130..., dimensions={0} | all-to-all | bytes 2097152 | tf_op jit(solution)/shard_map/all_to_all | solution.py:438
  133.0 0.3 prefix.1
  133.2 15.7 %all_to_all.23.states = f32[4,2,256,128]{3,2,1,0:T(8,128)S(1)} all-to-all(f32[4,2,256,128]{3,2,1,0:T(8,128)S(1)} %prefix.1), channel_id=1, replica_groups={{0,64,128,192},{32,96,160,224},{1,65,129,193},{33,97,161,225},{2,66,130..., dimensions={0} | all-to-all | bytes 2097152 | tf_op jit(solution)/shard_map/all_to_all | solution.py:440
  149.0 0.7 end.1
  149.6 2.8 %collective-permute-start.9 = (f32[2,1024,128]{2,1,0:T(8,128)S(1)}, f32[2,1024,128]{2,1,0:T(8,128)S(1)}, u32[]{:S(2)}, u32[]{:S(2)}) collective-permute-start(f32[2,1024,128]{2,1,0:T(8,128)S(1)} %get-tuple-element.82), channel_id=1, source_target_pairs={{0,32},{32,0},{64,96},{96,64},{128,160},{160,128},{192,224},{224,1... | collective-permute-start | bytes 3145736 | tf_op jit(solution)/shard_map/ppermute | solution.py:433
  152.5 1.0 keep.1
  153.5 1.3 collective-permute-done.9.got
  154.8 1.0 join.1
Async XLA Ops:
  7.7 13.1 %collective-permute-start = (f32[1024,128]{1,0:T(8,128)S(1)}, f32[1024,128]{1,0:T(8,128)S(1)}, u32[]{:S(2)}, u32[]{:S(2)}) collective-permute-start(f32[1024,128]{1,0:T(8,128)S(1)} %get-tuple-element.48.f_b.y_b), channel_id=1, source_target_pairs={{0,1},{1,0},{2,3},{3,2},{4,5},{5,4},{6,7},{7,6},{8,9},{9,8},{10,11... | collective-permute-start | bytes 1572872 | tf_op jit(solution)/shard_map/ppermute | solution.py:357
  10.3 11.9 %collective-permute-start.1 = (f32[1024,128]{1,0:T(8,128)S(1)}, f32[1024,128]{1,0:T(8,128)S(1)}, u32[]{:S(2)}, u32[]{:S(2)}) collective-permute-start(f32[1024,128]{1,0:T(8,128)S(1)} %get-tuple-element.49.y_a), channel_id=1, source_target_pairs={{1,2},{2,1},{3,4},{4,3},{5,6},{6,5},{7,8},{8,7},{9,10},{10,9},{11,... | collective-permute-start | bytes 1572872 | tf_op jit(solution)/shard_map/ppermute | solution.py:356
  23.6 15.3 %collective-permute-start.2 = (f32[1024,128]{1,0:T(8,128)S(1)}, f32[1024,128]{1,0:T(8,128)S(1)}, u32[]{:S(2)}, u32[]{:S(2)}) collective-permute-start(f32[1024,128]{1,0:T(8,128)S(1)} %get-tuple-element.51.f_b.q_b), channel_id=1, source_target_pairs={{0,1},{1,0},{2,3},{3,2},{4,5},{5,4},{6,7},{7,6},{8,9},{9,8},{10,11... | collective-permute-start | bytes 1572872 | tf_op jit(solution)/shard_map/ppermute | solution.py:357
  28.2 11.9 %collective-permute-start.3 = (f32[1024,128]{1,0:T(8,128)S(1)}, f32[1024,128]{1,0:T(8,128)S(1)}, u32[]{:S(2)}, u32[]{:S(2)}) collective-permute-start(f32[1024,128]{1,0:T(8,128)S(1)} %get-tuple-element.52.q_a), channel_id=1, source_target_pairs={{1,2},{2,1},{3,4},{4,3},{5,6},{6,5},{7,8},{8,7},{9,10},{10,9},{11,... | collective-permute-start | bytes 1572872 | tf_op jit(solution)/shard_map/ppermute | solution.py:356
  62.0 9.3 %collective-permute-start.4 = (f32[1024,128]{1,0:T(8,128)S(1)}, f32[1024,128]{1,0:T(8,128)S(1)}, u32[]{:S(2)}, u32[]{:S(2)}) collective-permute-start(f32[1024,128]{1,0:T(8,128)S(1)} %get-tuple-element.63.f_b.y_b), channel_id=1, source_target_pairs={{0,1},{1,0},{2,3},{3,2},{4,5},{5,4},{6,7},{7,6},{8,9},{9,8},{10,11... | collective-permute-start | bytes 1572872 | tf_op jit(solution)/shard_map/ppermute | solution.py:357
  63.0 9.6 %collective-permute-start.5 = (f32[1024,128]{1,0:T(8,128)S(1)}, f32[1024,128]{1,0:T(8,128)S(1)}, u32[]{:S(2)}, u32[]{:S(2)}) collective-permute-start(f32[1024,128]{1,0:T(8,128)S(1)} %get-tuple-element.64.y_a), channel_id=1, source_target_pairs={{1,2},{2,1},{3,4},{4,3},{5,6},{6,5},{7,8},{8,7},{9,10},{10,9},{11,... | collective-permute-start | bytes 1572872 | tf_op jit(solution)/shard_map/ppermute | solution.py:356
  74.0 8.7 %collective-permute-start.6 = (f32[1024,128]{1,0:T(8,128)S(1)}, f32[1024,128]{1,0:T(8,128)S(1)}, u32[]{:S(2)}, u32[]{:S(2)}) collective-permute-start(f32[1024,128]{1,0:T(8,128)S(1)} %get-tuple-element.69.f_b.q_b), channel_id=1, source_target_pairs={{0,1},{1,0},{2,3},{3,2},{4,5},{5,4},{6,7},{7,6},{8,9},{9,8},{10,11... | collective-permute-start | bytes 1572872 | tf_op jit(solution)/shard_map/ppermute | solution.py:357
  76.1 7.9 %collective-permute-start.7 = (f32[1024,128]{1,0:T(8,128)S(1)}, f32[1024,128]{1,0:T(8,128)S(1)}, u32[]{:S(2)}, u32[]{:S(2)}) collective-permute-start(f32[1024,128]{1,0:T(8,128)S(1)} %get-tuple-element.70.q_a), channel_id=1, source_target_pairs={{1,2},{2,1},{3,4},{4,3},{5,6},{6,5},{7,8},{8,7},{9,10},{10,9},{11,... | collective-permute-start | bytes 1572872 | tf_op jit(solution)/shard_map/ppermute | solution.py:356
  104.1 10.1 %collective-permute-start.8 = (f32[2,1024,128]{2,1,0:T(8,128)S(1)}, f32[2,1024,128]{2,1,0:T(8,128)S(1)}, u32[]{:S(2)}, u32[]{:S(2)}) collective-permute-start(f32[2,1024,128]{2,1,0:T(8,128)S(1)} %get-tuple-element.80), channel_id=1, source_target_pairs={{0,32},{32,0},{64,96},{96,64},{128,160},{160,128},{192,224},{224,1... | collective-permute-start | bytes 3145736 | tf_op jit(solution)/shard_map/ppermute | solution.py:433
  149.6 5.1 %collective-permute-start.9 = (f32[2,1024,128]{2,1,0:T(8,128)S(1)}, f32[2,1024,128]{2,1,0:T(8,128)S(1)}, u32[]{:S(2)}, u32[]{:S(2)}) collective-permute-start(f32[2,1024,128]{2,1,0:T(8,128)S(1)} %get-tuple-element.82), channel_id=1, source_target_pairs={{0,32},{32,0},{64,96},{96,64},{128,160},{160,128},{192,224},{224,1... | collective-permute-start | bytes 3145736 | tf_op jit(solution)/shard_map/ppermute | solution.py:433
